TPU v7x, 32 devices: a whole 2x2x4 slice. The times are simulated.
32 devices in a mesh: rep: 8 (over z, core), shard: 4 (over y, x).
Axes of the slice: x: 2, y: 2, z: 4, core: 2. Of those that a mesh axis runs over, the one named last changes fastest.
Arguments:
- tokens: bfloat16 [8192, 2048], P(('rep', 'shard')), may hold values from -6 to 6
- lengths: int32 [32, 4], P(('rep', 'shard')), may hold values from 1 to 128, 256 in all within a row
- ln_gain: bfloat16 [2048], P(('rep', 'shard')), may hold values from 0.5 to 1.5
- ln_bias: bfloat16 [2048], P(('rep', 'shard')), may hold values from -1.1953125 to 1.1953125
- qkv_weight: bfloat16 [2048, 6144], P(('rep', 'shard')), may hold values from -0.125 to 0.125
- qkv_bias: bfloat16 [6144], P(('rep', 'shard')), may hold values from -1.1953125 to 1.1953125
- dense_weight: bfloat16 [2048, 2048], P(('rep', 'shard')), may hold values from -0.375 to 0.375
- dense_bias: bfloat16 [2048], P(('rep', 'shard')), may hold values from -1.1953125 to 1.1953125
- up_weight: bfloat16 [2048, 8192], P(('rep', 'shard')), may hold values from -0.125 to 0.125
- up_bias: bfloat16 [8192], P(('rep', 'shard')), may hold values from -1.1953125 to 1.1953125
- down_weight: bfloat16 [8192, 2048], P(('rep', 'shard')), may hold values from -0.0625 to 0.0625
- down_bias: bfloat16 [2048], P(('rep', 'shard')), may hold values from -1.1953125 to 1.1953125
- cotangent: bfloat16 [8192, 2048], P(('rep', 'shard')), may hold values from -6 to 6
Outputs:
- output: bfloat16 [8192, 2048], P(('rep', 'shard'))
- grad_tokens: bfloat16 [8192, 2048], P(('rep', 'shard'))
- grad_ln_gain: float32 [2048], P(('rep', 'shard'))
- grad_ln_bias: float32 [2048], P(('rep', 'shard'))
- grad_qkv_weight: float32 [2048, 6144], P(('rep', 'shard'))
- grad_qkv_bias: float32 [6144], P(('rep', 'shard'))
- grad_dense_weight: float32 [2048, 2048], P(('rep', 'shard'))
- grad_dense_bias: float32 [2048], P(('rep', 'shard'))
- grad_up_weight: float32 [2048, 8192], P(('rep', 'shard'))
- grad_up_bias: float32 [8192], P(('rep', 'shard'))
- grad_down_weight: float32 [8192, 2048], P(('rep', 'shard'))
- grad_down_bias: float32 [2048], P(('rep', 'shard'))
Inputs may be any that keep to these rules, and one draw needn't show every extreme that they name: `lengths`: each row lists the documents of one device; they sum to 256, and the longest is exactly 128 tokens.
All inputs are finite; a program needn't handle non-finite values.
Results may differ from a plain program's by a relative error of at most 0.0091.
Values may be sent and summed in bfloat16 or wider, within the bound.
No kernel may reach another device: no remote copies, remote signals or barrier semaphores. Data moves between devices by JAX's collectives and lax.ppermute only.
A program may use at most 448 MiB of HBM per device.

v0:
```python
import math

import jax
import jax.numpy as jnp
from jax import lax
from jax.sharding import PartitionSpec as P

HEADS = 32
HEAD_DIM = 64
ROT = 32


EPSILON = 1e-05


def positions(doc_sizes, row_count):
    ends_at = jnp.cumsum(doc_sizes)
    starts_at = ends_at - doc_sizes
    indices = jnp.arange(row_count, dtype=jnp.int32)
    doc_ids = jnp.sum((indices[:, None] >= ends_at[None, :]).astype(jnp.int32), axis=1)
    member = doc_ids[:, None] == jnp.arange(doc_sizes.shape[0], dtype=jnp.int32)[None, :]
    offsets = jnp.sum(jnp.where(member, starts_at[None, :], 0), axis=1)
    places = (indices - offsets).astype(jnp.float32)
    allowed = (doc_ids[:, None] == doc_ids[None, :]) & (indices[None, :] <= indices[:, None])
    return (places, allowed)


def rotary(places):
    indices = jnp.arange(ROT // 2, dtype=jnp.float32)
    inverse = jnp.power(jnp.float32(10000.0), -2.0 * indices / ROT)
    angles = places[:, None] * inverse[None, :]
    return (jnp.cos(angles)[:, None, :], jnp.sin(angles)[:, None, :])


def rotate(values, cosine, sine):
    lower_half = values[..., : ROT // 2]
    upper_half = values[..., ROT // 2 : ROT]
    return jnp.concatenate(
        [
            lower_half * cosine - upper_half * sine,
            upper_half * cosine + lower_half * sine,
            values[..., ROT:],
        ],
        axis=-1,
    )


def unrotate(incoming, cosine, sine):
    lower_half = incoming[..., : ROT // 2]
    upper_half = incoming[..., ROT // 2 : ROT]
    return jnp.concatenate(
        [
            lower_half * cosine + upper_half * sine,
            upper_half * cosine - lower_half * sine,
            incoming[..., ROT:],
        ],
        axis=-1,
    )


def project(weight, left_side):
    whole = lax.all_gather(weight, ("rep", "shard"), axis=0, tiled=True)
    return jnp.dot(left_side, whole, preferred_element_type=jnp.float32)


def back_project(weight, incoming):
    whole = lax.all_gather(weight, ("rep", "shard"), axis=0, tiled=True)
    return lax.dot_general(
        incoming, whole, (((1,), (1,)), ((), ())), preferred_element_type=jnp.float32
    )


def weight_grad(left_side, incoming):
    return lax.psum_scatter(
        lax.dot_general(
            left_side, incoming, (((0,), (0,)), ((), ())), preferred_element_type=jnp.float32
        ),
        ("rep", "shard"),
        scatter_dimension=0,
        tiled=True,
    )


def on_device(
    tokens,
    lengths,
    ln_gain,
    ln_bias,
    qkv_weight,
    qkv_bias,
    dense_weight,
    dense_bias,
    up_weight,
    up_bias,
    down_weight,
    down_bias,
    cotangent,
):
    row_count = tokens.shape[0]
    width = tokens.shape[1]
    small = (
        lax.all_gather(ln_gain, ("rep", "shard"), axis=0, tiled=True),
        lax.all_gather(ln_bias, ("rep", "shard"), axis=0, tiled=True),
        lax.all_gather(qkv_bias, ("rep", "shard"), axis=0, tiled=True),
        lax.all_gather(dense_bias, ("rep", "shard"), axis=0, tiled=True),
        lax.all_gather(up_bias, ("rep", "shard"), axis=0, tiled=True),
        lax.all_gather(down_bias, ("rep", "shard"), axis=0, tiled=True),
    )
    gain, shift, packed_bias, dense_shift, upward_bias, downward_bias = [
        tensor.astype(jnp.float32) for tensor in small
    ]
    places, allowed = positions(lengths[0], row_count)
    cosine, sine = rotary(places)
    scaling = 1.0 / math.sqrt(HEAD_DIM)
    inputs_f = tokens.astype(jnp.float32)
    average = jnp.mean(inputs_f, axis=1, keepdims=True)
    centered = inputs_f - average
    spread = jnp.mean(centered * centered, axis=1, keepdims=True)
    inv_std = lax.rsqrt(spread + EPSILON)
    normed = centered * inv_std
    hidden_low = (normed * gain + shift).astype(jnp.bfloat16)
    packed = (project(qkv_weight, hidden_low) + packed_bias).reshape(row_count, 3, HEADS, HEAD_DIM)
    queries = rotate(packed[:, 0], cosine, sine).astype(jnp.bfloat16)
    keys_rot = rotate(packed[:, 1], cosine, sine).astype(jnp.bfloat16)
    values_low = packed[:, 2].astype(jnp.bfloat16)
    scores = scaling * jnp.einsum(
        "qhd,khd->hqk", queries, keys_rot, preferred_element_type=jnp.float32
    )
    scores = jnp.where(allowed[None], scores, -1e30)
    maximum = jnp.max(scores, axis=-1, keepdims=True)
    raised = jnp.exp(scores - maximum)
    totals = jnp.sum(raised, axis=-1, keepdims=True)
    probs = raised / totals
    log_total = maximum + jnp.log(totals)
    context = jnp.einsum(
        "hqk,khd->qhd", probs.astype(jnp.bfloat16), values_low, preferred_element_type=jnp.float32
    )
    context_low = context.reshape(row_count, width).astype(jnp.bfloat16)
    attended = project(dense_weight, context_low) + dense_shift
    upward = project(up_weight, hidden_low) + upward_bias
    active_low = jax.nn.gelu(upward, approximate=True).astype(jnp.bfloat16)
    downward = project(down_weight, active_low) + downward_bias
    output = (inputs_f + attended + downward).astype(jnp.bfloat16)
    grad_out = cotangent.astype(jnp.float32)
    d_active = back_project(down_weight, cotangent)
    gelu_value, gelu_pull = jax.vjp(lambda inner: jax.nn.gelu(inner, approximate=True), upward)
    d_upward_low = gelu_pull(d_active)[0].astype(jnp.bfloat16)
    d_context_low = (
        back_project(dense_weight, cotangent)
        .astype(jnp.bfloat16)
        .reshape(row_count, HEADS, HEAD_DIM)
    )
    again = scaling * jnp.einsum(
        "qhd,khd->hqk", queries, keys_rot, preferred_element_type=jnp.float32
    )
    again = jnp.where(allowed[None], again, -1e30)
    probs_again = jnp.exp(again - log_total)
    d_values = jnp.einsum(
        "hqk,qhd->khd",
        probs_again.astype(jnp.bfloat16),
        d_context_low,
        preferred_element_type=jnp.float32,
    )
    d_probs = jnp.einsum(
        "qhd,khd->hqk", d_context_low, values_low, preferred_element_type=jnp.float32
    )
    d_scores = probs_again * (d_probs - jnp.sum(d_probs * probs_again, axis=-1, keepdims=True))
    d_scores_low = d_scores.astype(jnp.bfloat16)
    d_queries = scaling * jnp.einsum(
        "hqk,khd->qhd", d_scores_low, keys_rot, preferred_element_type=jnp.float32
    )
    d_keys = scaling * jnp.einsum(
        "hqk,qhd->khd", d_scores_low, queries, preferred_element_type=jnp.float32
    )
    d_packed = jnp.stack(
        [unrotate(d_queries, cosine, sine), unrotate(d_keys, cosine, sine), d_values], axis=1
    )
    d_packed_low = d_packed.reshape(row_count, 3 * width).astype(jnp.bfloat16)
    d_hidden = back_project(qkv_weight, d_packed_low) + back_project(up_weight, d_upward_low)
    d_norm = d_hidden * gain
    d_inputs = inv_std * (
        d_norm
        - jnp.mean(d_norm, axis=1, keepdims=True)
        - normed * jnp.mean(d_norm * normed, axis=1, keepdims=True)
    )
    grad_tokens = (grad_out + d_inputs).astype(jnp.bfloat16)
    grad_qkv_w = weight_grad(hidden_low, d_packed_low)
    grad_dense_w = weight_grad(context_low, cotangent)
    grad_up_w = weight_grad(hidden_low, d_upward_low)
    grad_down_w = weight_grad(active_low, cotangent)
    small_terms = (
        jnp.sum(d_hidden * normed, axis=0),
        jnp.sum(d_hidden, axis=0),
        jnp.sum(d_packed_low.astype(jnp.float32), axis=0),
        jnp.sum(grad_out, axis=0),
        jnp.sum(d_upward_low.astype(jnp.float32), axis=0),
    )
    reduced = (
        lax.psum_scatter(small_terms[0], ("rep", "shard"), scatter_dimension=0, tiled=True),
        lax.psum_scatter(small_terms[1], ("rep", "shard"), scatter_dimension=0, tiled=True),
        lax.psum_scatter(small_terms[2], ("rep", "shard"), scatter_dimension=0, tiled=True),
        lax.psum_scatter(small_terms[3], ("rep", "shard"), scatter_dimension=0, tiled=True),
        lax.psum_scatter(small_terms[4], ("rep", "shard"), scatter_dimension=0, tiled=True),
    )
    grad_gain, grad_shift, grad_packed_b, grad_out_b, grad_up_b = reduced
    return (
        output,
        grad_tokens,
        grad_gain,
        grad_shift,
        grad_qkv_w,
        grad_packed_b,
        grad_dense_w,
        grad_out_b,
        grad_up_w,
        grad_up_b,
        grad_down_w,
        grad_out_b,
    )


def solution(mesh):
    return jax.shard_map(
        on_device,
        mesh=mesh,
        in_specs=(
            P(("rep", "shard"), None),
            P(("rep", "shard"), None),
            P(("rep", "shard")),
            P(("rep", "shard")),
            P(("rep", "shard"), None),
            P(("rep", "shard")),
            P(("rep", "shard"), None),
            P(("rep", "shard")),
            P(("rep", "shard"), None),
            P(("rep", "shard")),
            P(("rep", "shard"), None),
            P(("rep", "shard")),
            P(("rep", "shard"), None),
        ),
        out_specs=(
            P(("rep", "shard"), None),
            P(("rep", "shard"), None),
            P(("rep", "shard")),
            P(("rep", "shard")),
            P(("rep", "shard"), None),
            P(("rep", "shard")),
            P(("rep", "shard"), None),
            P(("rep", "shard")),
            P(("rep", "shard"), None),
            P(("rep", "shard")),
            P(("rep", "shard"), None),
            P(("rep", "shard")),
        ),
        check_vma=False,
    )
```

profile of v0, /device:TPU:0, one launch (start us, length us, event | category | flops | bytes accessed | tf_op | source)
XLA Modules:
  0.0 4430.9 jit_solution(2729186458216941077)
XLA Ops:
  14.3 43.1 all-reduce.11
  58.1 66.8 %all-gather = bf16[32,1,256]{2,1,0:T(2,128)(2,1)S(1)} all-gather(bf16[1,1,256]{2,1,0:T(2,128)(2,1)S(1)} %reshape.196), channel_id=1, replica_groups=mesh['rep'=8,'shard'=4] {'rep','shard'}, dimensions={0}, use_global_device_ids=true | all-gather | bytes 16896 | tf_op jit(solution)/shard_map/all_gather | solution.py:106
  128.8 6.7 convolution_convert_fusion
  137.5 110.3 %all-gather.6.cloned.1.call-done = bf16[2048,6144]{1,0:T(8,128)(2,1)} async-done(((bf16[64,6144]{1,0:T(8,128)(2,1)}), bf16[2048,6144]{1,0:T(8,128)(2,1)}) %all-gather.6.cloned.1.call-update) | async-done | bytes 25165840 | tf_op jit(solution)/shard_map/all_gather | solution.py:62
  247.8 13.5 convolution_add_fusion.1
  261.2 6.7 copy.46
  289.7 6.4 fusion.33
  296.1 13.6 fusion.56
  309.7 134.0 %all-gather.12.cloned.1.call-done = bf16[8192,2048]{1,0:T(8,128)(2,1)} async-done(((bf16[256,2048]{1,0:T(8,128)(2,1)}), bf16[8192,2048]{1,0:T(8,128)(2,1)}) %all-gather.12.cloned.1.call-update) | async-done | bytes 33554448 | tf_op jit(solution)/shard_map/all_gather | solution.py:62
  443.7 18.6 fusion.57
  462.3 177.1 %all-gather.10.cloned.1.call-done = bf16[2048,8192]{1,0:T(8,128)(2,1)} async-done(((bf16[64,8192]{1,0:T(8,128)(2,1)}), bf16[2048,8192]{1,0:T(8,128)(2,1)}) %all-gather.10.cloned.1.call-update) | async-done | bytes 33554448 | tf_op jit(solution)/shard_map/all_gather | solution.py:62
  639.4 25.1 convert_reduce_fusion
  664.5 18.6 fusion.27
  687.9 8.1 fusion.58
  696.1 21.7 fusion.51
  717.9 25.6 fusion.49
  743.7 27.4 fusion.48
  771.8 7.0 convert_add_fusion
  778.8 19.9 fusion.15
  798.7 9.4 all-reduce.14.cloned.1.call-done
  814.0 355.8 %reduce-scatter.7.cloned.1.call-done = f32[64,2048]{1,0:T(8,128)} async-done(((f32[2048,2048]{1,0:T(8,128)}), f32[64,2048]{1,0:T(8,128)}) %reduce-scatter.7.cloned.1.call-update) | async-done | bytes 524304 | tf_op jit(solution)/shard_map/reduce_scatter | solution.py:74
  1169.8 440.0 %reduce-scatter.5.cloned.1.call-done = f32[64,6144]{1,0:T(8,128)} async-done(((f32[2048,6144]{1,0:T(8,128)}), f32[64,6144]{1,0:T(8,128)}) %reduce-scatter.5.cloned.1.call-update) | async-done | bytes 1572880 | tf_op jit(solution)/shard_map/reduce_scatter | solution.py:74
  1609.8 1406.3 %reduce-scatter.9.cloned.1.call-done = f32[64,8192]{1,0:T(8,128)} async-done(((f32[2048,8192]{1,0:T(8,128)}), f32[64,8192]{1,0:T(8,128)}) %reduce-scatter.9.cloned.1.call-update) | async-done | bytes 2097168 | tf_op jit(solution)/shard_map/reduce_scatter | solution.py:74
  3016.2 1407.5 %reduce-scatter.11.cloned.1.call-done = f32[256,2048]{1,0:T(8,128)} async-done(((f32[8192,2048]{1,0:T(8,128)}), f32[256,2048]{1,0:T(8,128)}) %reduce-scatter.11.cloned.1.call-update) | async-done | bytes 2097168 | tf_op jit(solution)/shard_map/reduce_scatter | solution.py:74
  (88 shorter events, 47.4 us)
Async XLA Ops:
  7.2 120.8 %copy-start.1 = (bf16[256,2048]{1,0:T(8,128)(2,1)S(1)}, bf16[256,2048]{1,0:T(8,128)(2,1)}, u32[]{:S(2)}) copy-start(bf16[256,2048]{1,0:T(8,128)(2,1)} %param.13) | copy-start | bytes 3145732
  7.2 121.6 %copy-start.2 = (bf16[256,2048]{1,0:T(8,128)(2,1)S(1)}, bf16[256,2048]{1,0:T(8,128)(2,1)}, u32[]{:S(2)}) copy-start(bf16[256,2048]{1,0:T(8,128)(2,1)} %param.25) | copy-start | bytes 3145732
  7.2 121.6 %all-gather.8.cloned.1.call-start = ((), (), s32[]{:S(2)}) async-start(), calls=%async_computation.5 | async-start | bytes 8650752 | tf_op jit(solution)/shard_map/all_gather | solution.py:62
  7.9 239.9 %all-gather.6.cloned.1.call-start = ((), (), s32[]{:S(2)}) async-start(), calls=%async_computation.4 | async-start | bytes 25952256 | tf_op jit(solution)/shard_map/all_gather | solution.py:62
  8.7 435.0 %all-gather.12.cloned.1.call-start = ((), (), s32[]{:S(2)}) async-start(), calls=%async_computation.7 | async-start | bytes 34603008 | tf_op jit(solution)/shard_map/all_gather | solution.py:62
  9.4 630.0 %all-gather.10.cloned.1.call-start = ((), (), s32[]{:S(2)}) async-start(), calls=%async_computation.6 | async-start | bytes 34603008 | tf_op jit(solution)/shard_map/all_gather | solution.py:62
  10.0 798.1 %all-reduce.14.cloned.1.call-start = ((), (), s32[]{:S(2)}) async-start(), calls=%async_computation.12 | async-start | bytes 163840
  272.5 12.4 copy-start
  687.4 482.4 %reduce-scatter.7.cloned.1.call-start = ((), (), s32[]{:S(2)}) async-start(), calls=%async_computation.9 | async-start | bytes 17301504 | tf_op jit(solution)/shard_map/reduce_scatter | solution.py:74
  696.0 913.8 %reduce-scatter.5.cloned.1.call-start = ((), (), s32[]{:S(2)}) async-start(), calls=%async_computation.8 | async-start | bytes 51904512 | tf_op jit(solution)/shard_map/reduce_scatter | solution.py:74
  717.8 2298.3 %reduce-scatter.9.cloned.1.call-start = ((), (), s32[]{:S(2)}) async-start(), calls=%async_computation.10 | async-start | bytes 69206016 | tf_op jit(solution)/shard_map/reduce_scatter | solution.py:74
  743.5 3680.2 %reduce-scatter.11.cloned.1.call-start = ((), (), s32[]{:S(2)}) async-start(), calls=%async_computation.11 | async-start | bytes 69206016 | tf_op jit(solution)/shard_map/reduce_scatter | solution.py:74
  771.1 0.7 copy-start.4
  771.1 0.7 copy-start.3
  808.9 3615.3 %copy-start.5 = (f32[64]{0:T(128)}, f32[64]{0:T(128)S(1)}, u32[]{:S(2)}) copy-start(f32[64]{0:T(128)S(1)} %dynamic-slice.3) | copy-start | bytes 772
Sparse Core Ops, SparseCore 0:
  10.9 80.4 all-gather.7
  94.3 153.4 all-gather.5
  250.7 192.9 all-gather.11
  446.4 192.9 all-gather.9
  687.5 120.5 all-reduce.13
  810.8 358.9 reduce-scatter.6
  1176.8 432.9 reduce-scatter.4
  1612.8 1403.3 reduce-scatter.8
  3019.1 1404.5 reduce-scatter.10
where the time goes:
time: 4440 us; the launch traced here: 4430 us
  waiting for transfers between devices  4040 us (91%)
  matrix products  223 us (5%)
  blocking collectives  110 us (2%)
    reduce_scatter x4, waiting for transfers between devices, weight_grad(): lax.psum_scatter(lax.dot_general(left_side, incoming, (((0,), (0,)), ((),...  3610 us
    all_gather x4, waiting for transfers between devices, project(): whole = lax.all_gather(weight, ('rep', 'shard'), axis=0, tiled=True)  421 us
  transfers between devices with their start and end apart: 9, of which 8 were waited for; matrix products, arithmetic and copies ran while one was open for 5% of the time, Pallas kernels for 0%

commit v1 on v0

--- a/solution.py
+++ b/solution.py
@@ -8,6 +8,10 @@
 HEADS = 32
 HEAD_DIM = 64
 ROT = 32
+CORES = 2
+AXES = ("rep", "shard")
+BF16 = jnp.bfloat16
+F32 = jnp.float32
 
 
 EPSILON = 1e-05
@@ -81,7 +85,7 @@
     )
 
 
-def on_device(
+def gathered_whole(
     tokens,
     lengths,
     ln_gain,
@@ -219,38 +223,358 @@
     )
 
 
+def tokens_dot(left_side, incoming):
+    return lax.dot_general(
+        left_side, incoming, (((0,), (0,)), ((), ())), preferred_element_type=F32
+    )
+
+
+def dot_transposed(left_side, weight):
+    return lax.dot_general(
+        left_side, weight, (((1,), (1,)), ((), ())), preferred_element_type=F32
+    )
+
+
+def by_planes(
+    planes,
+    mates,
+    tokens,
+    lengths,
+    ln_gain,
+    ln_bias,
+    qkv_weight,
+    qkv_bias,
+    dense_weight,
+    dense_bias,
+    up_weight,
+    up_bias,
+    down_weight,
+    down_bias,
+    cotangent,
+):
+    row_count, width = tokens.shape
+    owners = planes * mates
+    rank = lax.axis_index("rep") * (mates // CORES) + lax.axis_index("shard")
+    z, m = rank // mates, rank % mates
+
+    def flip(value, r):
+        return lax.ppermute(
+            value,
+            AXES,
+            [(p * mates + i, p * mates + (i ^ r)) for p in range(planes) for i in range(mates)],
+        )
+
+    def shift(value, step, first, last):
+        return lax.ppermute(
+            value,
+            AXES,
+            [
+                (p * mates + i, (p + step) * mates + i)
+                for p in range(first, last)
+                for i in range(mates)
+            ],
+        )
+
+    def along_planes(piece):
+        ups, downs = [piece], [piece]
+        for k in range(1, planes):
+            ups.append(shift(ups[-1], 1, k - 1, planes - 1))
+            downs.append(shift(downs[-1], -1, 1, planes - k + 1))
+        return ups, downs
+
+    def newest_first(ups, downs):
+        return jnp.concatenate(
+            [ups[0]]
+            + [jnp.where(z >= k, ups[k], downs[planes - k]) for k in range(1, planes)],
+            axis=0,
+        )
+
+    def in_order(ups, downs):
+        def block(p):
+            return lax.select_n(
+                z, *[ups[q - p] if q >= p else downs[p - q] for q in range(planes)]
+            )
+
+        return jnp.concatenate([block(p) for p in range(planes)], axis=0)
+
+    def back_to_planes(blocks):
+        up = down = None
+        for s in range(1, planes):
+            out_up, out_down = blocks[s], blocks[planes - s]
+            if up is not None:
+                out_up, out_down = out_up + up.astype(F32), out_down + down.astype(F32)
+            up = shift(out_up.astype(BF16), 1, 0, s)
+            down = shift(out_down.astype(BF16), -1, planes - s, planes)
+        return blocks[0] + up.astype(F32) + down.astype(F32)
+
+    def exchange(pieces):
+        result = jnp.zeros(pieces.shape, pieces.dtype)
+        for r in range(mates):
+            own = lax.dynamic_index_in_dim(pieces, m ^ r, 0, keepdims=False)
+            result = lax.dynamic_update_index_in_dim(
+                result, own if r == 0 else flip(own, r), m ^ r, 0
+            )
+        return result
+
+    def gather_rows(block):
+        half = block.shape[0] // 2
+        by_x, by_y = flip(block, 1), flip(block, 2)
+        near = jnp.concatenate(
+            [block, by_x, by_y, flip(by_y[:half], 1), flip(by_x[half:], 2)], axis=0
+        )
+        return jnp.concatenate([near, flip(near, 4)], axis=0)
+
+    def scatter_rows(near, far):
+        total = near + flip(far.astype(BF16), 4).astype(F32)
+        own, for_x, for_y, diagonal = [
+            total[i * row_count : (i + 1) * row_count] for i in range(4)
+        ]
+        half = row_count // 2
+        extra_y = flip(diagonal[:half].astype(BF16), 1).astype(F32)
+        extra_x = flip(diagonal[half:].astype(BF16), 2).astype(F32)
+        for_x = jnp.concatenate([for_x[:half], for_x[half:] + extra_x], axis=0)
+        for_y = jnp.concatenate([for_y[:half] + extra_y, for_y[half:]], axis=0)
+        return own + flip(for_x.astype(BF16), 1).astype(F32) + flip(for_y.astype(BF16), 2).astype(F32)
+
+    def everywhere(table):
+        for r in (1, 2, 4):
+            table = table + flip(table, r)
+        for r in (1, 2):
+            table = table + lax.ppermute(
+                table,
+                AXES,
+                [(p * mates + i, (p ^ r) * mates + i) for p in range(planes) for i in range(mates)],
+            )
+        return table
+
+    parts = [ln_gain, ln_bias, qkv_bias, dense_bias, up_bias, down_bias, lengths[0].astype(BF16)]
+    sizes = [part.shape[0] for part in parts]
+    starts = [sum(sizes[:i]) for i in range(len(sizes))]
+    own_row = jnp.concatenate(parts)
+    own_row = jnp.pad(own_row, (0, -len(own_row) % 128))
+    table = jnp.where(jnp.arange(owners)[:, None] == rank, own_row[None, :], 0)
+    table = everywhere(table).astype(F32)
+
+    def column(i):
+        return table[:, starts[i] : starts[i] + sizes[i]].reshape(-1)
+
+    gain, shift_by = column(0), column(1)
+    heads_here = HEADS // mates
+    ff_block = up_bias.shape[0]
+    packed_bias = lax.dynamic_index_in_dim(
+        column(2).reshape(3, planes, mates, HEAD_DIM), m, 2, keepdims=False
+    ).reshape(-1)
+    upward_bias = lax.dynamic_index_in_dim(
+        column(4).reshape(planes, mates, ff_block), m, 1, keepdims=False
+    ).reshape(-1)
+    out_bias = column(3) + column(5)
+    all_lengths = table[:, starts[6] : starts[6] + sizes[6]].astype(jnp.int32)
+    doc_sizes = jnp.stack(
+        [
+            lax.dynamic_index_in_dim(all_lengths, z * mates + (m ^ r), 0, keepdims=False)
+            for r in range(mates)
+        ]
+    )
+
+    rows_own = qkv_weight.shape[0]
+    up_pieces = (
+        up_weight.reshape(rows_own, planes, mates, ff_block)
+        .transpose(2, 0, 1, 3)
+        .reshape(mates, rows_own, planes * ff_block)
+    )
+    qkv_pieces = (
+        qkv_weight.reshape(rows_own, 3, planes, mates, HEAD_DIM)
+        .transpose(3, 0, 1, 2, 4)
+        .reshape(mates, rows_own, 3 * planes * HEAD_DIM)
+    )
+    up_w = newest_first(*along_planes(exchange(up_pieces).reshape(mates * rows_own, -1)))
+    dense_w = in_order(*along_planes(dense_weight))
+    qkv_w = newest_first(*along_planes(exchange(qkv_pieces).reshape(mates * rows_own, -1)))
+    down_w = in_order(*along_planes(down_weight))
+
+    def turned(value):
+        blocks = value.reshape(value.shape[0], planes, -1)
+        return jnp.concatenate(
+            [
+                lax.dynamic_index_in_dim(blocks, (z - k) % planes, 1, keepdims=False)
+                for k in range(planes)
+            ],
+            axis=1,
+        )
+
+    inputs_f = tokens.astype(F32)
+    average = jnp.mean(inputs_f, axis=1, keepdims=True)
+    centered = inputs_f - average
+    spread = jnp.mean(centered * centered, axis=1, keepdims=True)
+    inv_std = lax.rsqrt(spread + EPSILON)
+    normed = centered * inv_std
+    hidden_own = (normed * gain + shift_by).astype(BF16)
+
+    cot = gather_rows(cotangent)
+    hidden = gather_rows(turned(hidden_own))
+
+    upward = jnp.dot(hidden, up_w, preferred_element_type=F32) + upward_bias
+    active, gelu_pull = jax.vjp(lambda inner: jax.nn.gelu(inner, approximate=True), upward)
+    active = active.astype(BF16)
+
+    def rows_by_plane(left_side, incoming, block):
+        sliced = left_side.reshape(left_side.shape[0], planes, block)
+        return back_to_planes(
+            [
+                tokens_dot(
+                    lax.dynamic_index_in_dim(sliced, (z - k) % planes, 1, keepdims=False), incoming
+                )
+                for k in range(planes)
+            ]
+        )
+
+    def rows_by_turn(left_side, incoming):
+        block = left_side.shape[1] // planes
+        return back_to_planes(
+            [
+                tokens_dot(left_side[:, k * block : (k + 1) * block], incoming)
+                for k in range(planes)
+            ]
+        )
+
+    grad_down_w = rows_by_plane(active, cot, ff_block)
+
+    places, allowed = jax.vmap(lambda sizes_now: positions(sizes_now, row_count))(doc_sizes)
+    cosine, sine = jax.vmap(rotary)(places)
+    scaling = 1.0 / math.sqrt(HEAD_DIM)
+    packed = (jnp.dot(hidden, qkv_w, preferred_element_type=F32) + packed_bias).reshape(
+        mates, row_count, 3, heads_here, HEAD_DIM
+    )
+    queries = rotate(packed[:, :, 0], cosine, sine).astype(BF16)
+    keys_rot = rotate(packed[:, :, 1], cosine, sine).astype(BF16)
+    values_low = packed[:, :, 2].astype(BF16)
+    scores = scaling * jnp.einsum("rqhd,rkhd->rhqk", queries, keys_rot, preferred_element_type=F32)
+    scores = jnp.where(allowed[:, None], scores, -1e30)
+    maximum = jnp.max(scores, axis=-1, keepdims=True)
+    raised = jnp.exp(scores - maximum)
+    probs = raised / jnp.sum(raised, axis=-1, keepdims=True)
+    probs_low = probs.astype(BF16)
+    context = jnp.einsum("rhqk,rkhd->rqhd", probs_low, values_low, preferred_element_type=F32)
+    context = context.astype(BF16).reshape(mates * row_count, heads_here * HEAD_DIM)
+    d_context = dot_transposed(cot, dense_w).astype(BF16)
+    grad_dense_w = rows_by_plane(context, cot, HEAD_DIM)
+    d_context = d_context.reshape(mates, row_count, heads_here, HEAD_DIM)
+    d_values = jnp.einsum("rhqk,rqhd->rkhd", probs_low, d_context, preferred_element_type=F32)
+    d_probs = jnp.einsum("rqhd,rkhd->rhqk", d_context, values_low, preferred_element_type=F32)
+    d_scores = probs * (d_probs - jnp.sum(d_probs * probs, axis=-1, keepdims=True))
+    d_scores = d_scores.astype(BF16)
+    d_queries = scaling * jnp.einsum(
+        "rhqk,rkhd->rqhd", d_scores, keys_rot, preferred_element_type=F32
+    )
+    d_keys = scaling * jnp.einsum("rhqk,rqhd->rkhd", d_scores, queries, preferred_element_type=F32)
+    d_packed = jnp.stack(
+        [unrotate(d_queries, cosine, sine), unrotate(d_keys, cosine, sine), d_values], axis=2
+    )
+    d_packed = d_packed.astype(BF16).reshape(mates * row_count, -1)
+
+    d_active = dot_transposed(cot, down_w)
+    d_upward = gelu_pull(d_active)[0].astype(BF16)
+    grad_up_rows = rows_by_turn(hidden, d_upward)
+    grad_qkv_rows = rows_by_turn(hidden, d_packed)
+
+    near = row_count * mates // 2
+
+    def out_of(part):
+        return jnp.dot(context[part], dense_w, preferred_element_type=F32) + jnp.dot(
+            active[part], down_w, preferred_element_type=F32
+        )
+
+    def d_hidden_of(part):
+        return dot_transposed(d_packed[part], qkv_w) + dot_transposed(d_upward[part], up_w)
+
+    summed = scatter_rows(out_of(slice(0, near)), out_of(slice(near, None)))
+    output = (inputs_f + summed + out_bias).astype(BF16)
+
+    d_hidden = turned(scatter_rows(d_hidden_of(slice(0, near)), d_hidden_of(slice(near, None))))
+    grad_out = cotangent.astype(F32)
+    d_norm = d_hidden * gain
+    d_inputs = inv_std * (
+        d_norm
+        - jnp.mean(d_norm, axis=1, keepdims=True)
+        - normed * jnp.mean(d_norm * normed, axis=1, keepdims=True)
+    )
+    grad_tokens = (grad_out + d_inputs).astype(BF16)
+
+    def pieces_of(rows):
+        return exchange(rows.astype(BF16).reshape(mates, rows_own, -1)).astype(F32)
+
+    grad_up_w = (
+        pieces_of(grad_up_rows)
+        .reshape(mates, rows_own, planes, ff_block)
+        .transpose(1, 2, 0, 3)
+        .reshape(rows_own, -1)
+    )
+    grad_qkv_w = (
+        pieces_of(grad_qkv_rows)
+        .reshape(mates, rows_own, 3, planes, HEAD_DIM)
+        .transpose(1, 2, 3, 0, 4)
+        .reshape(rows_own, -1)
+    )
+
+    mine = jnp.arange(mates) == m
+    packed_sum = jnp.sum(d_packed.astype(F32), axis=0).reshape(3, planes, 1, HEAD_DIM)
+    packed_sum = jnp.where(mine[None, None, :, None], packed_sum, 0.0)
+    upward_sum = jnp.sum(d_upward.astype(F32), axis=0).reshape(planes, 1, ff_block)
+    upward_sum = jnp.where(mine[None, :, None], upward_sum, 0.0)
+    sums = jnp.concatenate(
+        [
+            jnp.sum(d_hidden * normed, axis=0).reshape(owners, -1),
+            jnp.sum(d_hidden, axis=0).reshape(owners, -1),
+            jnp.sum(grad_out, axis=0).reshape(owners, -1),
+            packed_sum.reshape(owners, -1),
+            upward_sum.reshape(owners, -1),
+        ],
+        axis=1,
+    )
+    total = lax.dynamic_index_in_dim(everywhere(sums), rank, 0, keepdims=False)
+    grad_gain, grad_shift, grad_out_b, grad_packed_b, grad_up_b = jnp.split(
+        total,
+        [
+            sizes[0],
+            sizes[0] + sizes[1],
+            sizes[0] + sizes[1] + sizes[3],
+            sizes[0] + sizes[1] + sizes[3] + sizes[2],
+        ],
+    )
+    return (
+        output,
+        grad_tokens,
+        grad_gain,
+        grad_shift,
+        grad_qkv_w,
+        grad_packed_b,
+        grad_dense_w,
+        grad_out_b,
+        grad_up_w,
+        grad_up_b,
+        grad_down_w,
+        grad_out_b,
+    )
+
+
 def solution(mesh):
+    planes, mates = mesh.shape["rep"] // CORES, CORES * mesh.shape["shard"]
+    rows, vector = P(AXES, None), P(AXES)
+
+    def layer(*arrays):
+        width = arrays[0].shape[1]
+        if mesh.shape["shard"] == 4 and planes * mates * HEAD_DIM == width:
+            return by_planes(planes, mates, *arrays)
+        return gathered_whole(*arrays)
+
     return jax.shard_map(
-        on_device,
+        layer,
         mesh=mesh,
         in_specs=(
-            P(("rep", "shard"), None),
-            P(("rep", "shard"), None),
-            P(("rep", "shard")),
-            P(("rep", "shard")),
-            P(("rep", "shard"), None),
-            P(("rep", "shard")),
-            P(("rep", "shard"), None),
-            P(("rep", "shard")),
-            P(("rep", "shard"), None),
-            P(("rep", "shard")),
-            P(("rep", "shard"), None),
-            P(("rep", "shard")),
-            P(("rep", "shard"), None),
+            rows, rows, vector, vector, rows, vector, rows, vector, rows, vector, rows, vector, rows,
         ),
         out_specs=(
-            P(("rep", "shard"), None),
-            P(("rep", "shard"), None),
-            P(("rep", "shard")),
-            P(("rep", "shard")),
-            P(("rep", "shard"), None),
-            P(("rep", "shard")),
-            P(("rep", "shard"), None),
-            P(("rep", "shard")),
-            P(("rep", "shard"), None),
-            P(("rep", "shard")),
-            P(("rep", "shard"), None),
-            P(("rep", "shard")),
+            rows, rows, vector, vector, rows, vector, rows, vector, rows, vector, rows, vector,
         ),
         check_vma=False,
     )

time: 4440 us -> 961 us (0.22)
  waiting for transfers between devices: 4040 us -> 330 us
  starting transfers between devices: 0.93 us -> 212 us
  blocking collectives: 110 us -> 0 us
  local copies, waits for them, and re-layouts: 24.2 us -> 130 us
  other arithmetic: 15.8 us -> 69.8 us
    reduce_scatter x4 -> x0, waiting for transfers between devices: 3610 us -> none  [weight_grad(): lax.psum_scatter(lax.dot_general(left_side, incoming, (((0,), (0,)), ((),...]
    all_gather x4 -> x0, waiting for transfers between devices: 421 us -> none  [project(): whole = lax.all_gather(weight, ('rep', 'shard'), axis=0, tiled=True)]
    ppermute x0 -> x106, waiting for transfers between devices: none -> 330 us  [the longest x48 204 us: shift(): lax.ppermute(value, AXES, [(p * mates + i, (p + step) * mates + i) for p...]
    ppermute x0 -> x106, starting transfers between devices: none -> 212 us  [the longest x54 111 us: flip(): lax.ppermute(value, AXES, [(p * mates + i, p * mates + (i ^ r)) for p in...]
    all_gather x1 -> x0, blocking collectives: 66.8 us -> none  [on_device(): lax.all_gather(up_bias, ('rep', 'shard'), axis=0, tiled=True)]
    dot_general x18 -> x33, matrix products: 223 us -> 198 us  [the longest x16 76.2 us: tokens_dot(): lax.dot_general(left_side, incoming, (((0,), (0,)), ((), ())), preferred_...]
  transfers between devices with their start and end apart: 9 -> 106, of which waited for: 8 -> 51; matrix products, arithmetic and copies ran while one was open for 5% -> 20% of each run, Pallas kernels for 0% -> 0%
where the time goes in v1:
time: 961 us; the launch traced here: 950 us
  waiting for transfers between devices  330 us (34%)
  starting transfers between devices  212 us (22%)
  matrix products  204 us (21%)
  local copies, waits for them, and re-layouts  130 us (14%)
  other arithmetic  69.8 us (7%)
    ppermute x48, waiting for transfers between devices, shift(): lax.ppermute(value, AXES, [(p * mates + i, (p + step) * mates + i) for p...  204 us
    ppermute x54, starting transfers between devices, flip(): lax.ppermute(value, AXES, [(p * mates + i, p * mates + (i ^ r)) for p in...  111 us
    ppermute x54, waiting for transfers between devices, flip(): lax.ppermute(value, AXES, [(p * mates + i, p * mates + (i ^ r)) for p in...  106 us
    ppermute x48, starting transfers between devices, shift(): lax.ppermute(value, AXES, [(p * mates + i, (p + step) * mates + i) for p...  92.7 us
    dot_general x16, matrix products, tokens_dot(): lax.dot_general(left_side, incoming, (((0,), (0,)), ((), ())), preferred_...  76.2 us
    dot_general x6, matrix products, dot_transposed(): lax.dot_general(left_side, weight, (((1,), (1,)), ((), ())), preferred_el...  61.4 us
    unnamed x246, local copies, waits for them, and re-layouts  38.3 us
    ppermute x4, waiting for transfers between devices, everywhere(): lax.ppermute(table, AXES, [(p * mates + i, (p ^ r) * mates + i) for p in...  20.1 us
  transfers between devices with their start and end apart: 106, of which 51 were waited for; matrix products, arithmetic and copies ran while one was open for 20% of the time, Pallas kernels for 0%

profile of v1, /device:TPU:0, one launch (start us, length us, event | category | flops | bytes accessed | tf_op | source)
XLA Modules:
  0.0 949.8 jit_solution(587523869081173052)
XLA Ops:
  97.1 14.8 %collective-permute-done.4 = bf16[32,768]{1,0:T(8,128)(2,1)S(1)} collective-permute-done((bf16[32,768]{1,0:T(8,128)(2,1)S(1)}, bf16[32,768]{1,0:T(8,128)(2,1)S(1)}, u32[]{:S(2)}, u32[]{:S(2)}) %collective-permute-start.4) | collective-permute-done | bytes 49184 | tf_op jit(solution)/shard_map/ppermute | solution.py:343
  120.6 17.2 %collective-permute-done.27 = bf16[64,2048]{1,0:T(8,128)(2,1)S(1)} collective-permute-done((bf16[64,2048]{1,0:T(8,128)(2,1)}, bf16[64,2048]{1,0:T(8,128)(2,1)S(1)}, u32[]{:S(2)}, u32[]{:S(2)}) %collective-permute-start.27) | collective-permute-done | bytes 262176 | tf_op jit(solution)/shard_map/ppermute | solution.py:268
  225.1 13.5 %collective-permute-done.46 = bf16[256,2048]{1,0:T(8,128)(2,1)} collective-permute-done((bf16[256,2048]{1,0:T(8,128)(2,1)}, bf16[256,2048]{1,0:T(8,128)(2,1)}, u32[]{:S(2)}, u32[]{:S(2)}) %collective-permute-start.46) | collective-permute-done | bytes 1048608 | tf_op jit(solution)/shard_map/ppermute | solution.py:268
  241.5 15.3 %collective-permute-done.38 = bf16[512,1024]{1,0:T(8,128)(2,1)S(1)} collective-permute-done((bf16[512,1024]{1,0:T(8,128)(2,1)}, bf16[512,1024]{1,0:T(8,128)(2,1)S(1)}, u32[]{:S(2)}, u32[]{:S(2)}) %collective-permute-start.38) | collective-permute-done | bytes 1048608 | tf_op jit(solution)/shard_map/ppermute | solution.py:268
  265.6 13.8 %collective-permute-done.20 = bf16[512,768]{1,0:T(8,128)(2,1)S(1)} collective-permute-done((bf16[512,768]{1,0:T(8,128)(2,1)}, bf16[512,768]{1,0:T(8,128)(2,1)S(1)}, u32[]{:S(2)}, u32[]{:S(2)}) %collective-permute-start.20) | collective-permute-done | bytes 786464 | tf_op jit(solution)/shard_map/ppermute | solution.py:268
  282.6 19.3 %collective-permute-done.47 = bf16[256,2048]{1,0:T(8,128)(2,1)S(1)} collective-permute-done((bf16[256,2048]{1,0:T(8,128)(2,1)}, bf16[256,2048]{1,0:T(8,128)(2,1)S(1)}, u32[]{:S(2)}, u32[]{:S(2)}) %collective-permute-start.47) | collective-permute-done | bytes 1048608 | tf_op jit(solution)/shard_map/ppermute | solution.py:268
  305.7 13.7 %collective-permute-done.39 = bf16[512,1024]{1,0:T(8,128)(2,1)S(1)} collective-permute-done((bf16[512,1024]{1,0:T(8,128)(2,1)S(1)}, bf16[512,1024]{1,0:T(8,128)(2,1)S(1)}, u32[]{:S(2)}, u32[]{:S(2)}) %collective-permute-start.39) | collective-permute-done | bytes 1048608 | tf_op jit(solution)/shard_map/ppermute | solution.py:268
  339.0 17.8 %multiply_convert_fusion.1 = (bf16[2048,1024]{0,1:T(8,128)(2,1)}, f32[2048,1024]{0,1:T(8,128)}) fusion(f32[1024]{0:T(1024)S(1)} %bitcast.346, bf16[2048,2048]{1,0:T(8,128)(2,1)} %constant_dynamic-update-slice_fusion.5, bf16[512,1024]{1,0:T(8,128)(2,1)S(1)} %copy-done.41, bf16[512,1024]{1,0:T(8,128)(2,1)S(1)} %copy-done.37, ...), kind=kOutput, calls=%fused_computation.17 | convolution fusion | flops 8627683328 | bytes 25169920 | tf_op jit(solution)/shard_map/dot_general | solution.py:416
  372.2 17.9 %convert_reduce_fusion = (f32[1024]{0:T(1024)}, bf16[2048,1024]{0,1:T(8,128)(2,1)}) fusion(f32[2048,1024]{0,1:T(8,128)} %get-tuple-element.151, f32[1024]{0:T(1024)S(1)} %bitcast.347, bf16[2048,2048]{1,0:T(8,128)(2,1)S(1)} %bitcast.282, bf16[256,2048]{1,0:T(8,128)(2,1)} %get-tuple-element.38, bf16[256,2048]{1,0:T(8,128)(2,1)} %get-tuple-element.37, ...), kind=kOutput, calls=%fused_computation.10 | convolution fusion | flops 8654945280 | bytes 25174016 | tf_op jit(solution)/shard_map/dot_general | solution.py:233
  406.5 8.6 broadcast_add_fusion
  415.2 12.1 %reshape.301 = f32[8,256,3,4,64]{4,3,2,1,0:T(4,128)} reshape(f32[2048,768]{1,0:T(8,128)} %broadcast_add_fusion) | data formatting | bytes 12582912 | tf_op jit(solution)/shard_map/reshape | solution.py:445
  503.4 8.7 fusion.38
  512.1 11.6 %fusion.33 = f32[1024,2048]{1,0:T(8,128)} fusion(bf16[2048,1024]{0,1:T(8,128)(2,1)} %get-tuple-element.155, bf16[512,1024]{1,0:T(8,128)(2,1)S(1)} %copy-done.42, bf16[512,1024]{1,0:T(8,128)(2,1)S(1)} %copy-done.38, bf16[512,1024]{1,0:T(8,128)(2,1)S(1)} %copy-done.40, bf16[512,1024]{1,0:T(8,128)(2,1)S(1)} %bitcast.333), kind=kOutput, calls=%fused_computation.61 | convolution fusion | flops 4311744512 | bytes 14680064 | tf_op jit(solution)/shard_map/dot_general | solution.py:233
  525.0 11.7 %fusion.31 = f32[1024,2048]{1,0:T(8,128)} fusion(bf16[2048,1024]{0,1:T(8,128)(2,1)} %get-tuple-element.155, bf16[512,1024]{1,0:T(8,128)(2,1)S(1)} %copy-done.42, bf16[512,1024]{1,0:T(8,128)(2,1)S(1)} %copy-done.38, bf16[512,1024]{1,0:T(8,128)(2,1)S(1)} %copy-done.40, bf16[512,1024]{1,0:T(8,128)(2,1)S(1)} %bitcast.334), kind=kOutput, calls=%fused_computation.59 | convolution fusion | flops 4311744512 | bytes 14680064 | tf_op jit(solution)/shard_map/dot_general | solution.py:233
  549.2 8.5 fusion.113
  559.3 9.2 add_convert_fusion
  571.8 19.3 %collective-permute-done.81 = bf16[64,2048]{1,0:T(8,128)(2,1)} collective-permute-done((bf16[64,2048]{1,0:T(8,128)(2,1)S(1)}, bf16[64,2048]{1,0:T(8,128)(2,1)}, u32[]{:S(2)}, u32[]{:S(2)}) %collective-permute-start.81) | collective-permute-done | bytes 262176 | tf_op jit(solution)/shard_map/ppermute | solution.py:268
  624.7 12.6 %collective-permute-done.69 = bf16[512,768]{1,0:T(8,128)(2,1)S(1)} collective-permute-done((bf16[512,768]{1,0:T(8,128)(2,1)S(1)}, bf16[512,768]{1,0:T(8,128)(2,1)S(1)}, u32[]{:S(2)}, u32[]{:S(2)}) %collective-permute-start.69) | collective-permute-done | bytes 786464 | tf_op jit(solution)/shard_map/ppermute | solution.py:268
  649.7 15.6 %collective-permute-done.101 = bf16[256,2048]{1,0:T(8,128)(2,1)S(1)} collective-permute-done((bf16[256,2048]{1,0:T(8,128)(2,1)S(1)}, bf16[256,2048]{1,0:T(8,128)(2,1)S(1)}, u32[]{:S(2)}, u32[]{:S(2)}) %collective-permute-start.101) | collective-permute-done | bytes 1048608 | tf_op jit(solution)/shard_map/ppermute | solution.py:268
  670.7 10.5 %collective-permute-done.88 = bf16[512,1024]{1,0:T(8,128)(2,1)S(1)} collective-permute-done((bf16[512,1024]{1,0:T(8,128)(2,1)S(1)}, bf16[512,1024]{1,0:T(8,128)(2,1)S(1)}, u32[]{:S(2)}, u32[]{:S(2)}) %collective-permute-start.88) | collective-permute-done | bytes 1048608 | tf_op jit(solution)/shard_map/ppermute | solution.py:268
  724.1 47.3 %collective-permute-start.77 = (bf16[64,768]{1,0:T(8,128)(2,1)S(1)}, bf16[64,768]{1,0:T(8,128)(2,1)S(1)}, u32[]{:S(2)}, u32[]{:S(2)}) collective-permute-start(bf16[64,768]{1,0:T(8,128)(2,1)S(1)} %get-tuple-element.99), channel_id=1, source_target_pairs={{0,4},{1,5},{2,6},{3,7},{4,0},{5,1},{6,2},{7,3},{8,12},{9,13},{10,... | collective-permute-start | bytes 294920 | tf_op jit(solution)/shard_map/ppermute | solution.py:261
  819.8 8.3 fusion.116
  850.8 19.2 %collective-permute-done.92 = bf16[512,1024]{1,0:T(8,128)(2,1)S(1)} collective-permute-done((bf16[512,1024]{1,0:T(8,128)(2,1)S(1)}, bf16[512,1024]{1,0:T(8,128)(2,1)S(1)}, u32[]{:S(2)}, u32[]{:S(2)}) %collective-permute-start.92) | collective-permute-done | bytes 1048608 | tf_op jit(solution)/shard_map/ppermute | solution.py:268
  882.3 14.0 %collective-permute-done.93 = bf16[64,1024]{1,0:T(8,128)(2,1)S(1)} collective-permute-done((bf16[64,1024]{1,0:T(8,128)(2,1)S(1)}, bf16[64,1024]{1,0:T(8,128)(2,1)S(1)}, u32[]{:S(2)}, u32[]{:S(2)}) %collective-permute-start.93) | collective-permute-done | bytes 131104 | tf_op jit(solution)/shard_map/ppermute | solution.py:261
  (654 shorter events, 585.7 us)
Async XLA Ops:
  0.6 116.9 %collective-permute-start.23 = (bf16[64,2048]{1,0:T(8,128)(2,1)}, bf16[64,2048]{1,0:T(8,128)(2,1)}, u32[]{:S(2)}, u32[]{:S(2)}) collective-permute-start(bf16[64,2048]{1,0:T(8,128)(2,1)} %param.19), channel_id=1, source_target_pairs={{0,8},{1,9},{2,10},{3,11},{4,12},{5,13},{6,14},{7,15},{8,16},{9,17... | collective-permute-start | bytes 786440 | tf_op jit(solution)/shard_map/ppermute | solution.py:268
  6.3 112.1 %collective-permute-start.26 = (bf16[64,2048]{1,0:T(8,128)(2,1)}, bf16[64,2048]{1,0:T(8,128)(2,1)}, u32[]{:S(2)}, u32[]{:S(2)}) collective-permute-start(bf16[64,2048]{1,0:T(8,128)(2,1)} %param.19), channel_id=1, source_target_pairs={{8,0},{9,1},{10,2},{11,3},{12,4},{13,5},{14,6},{15,7},{16,8},{17,9... | collective-permute-start | bytes 786440 | tf_op jit(solution)/shard_map/ppermute | solution.py:268
  12.5 58.5 %collective-permute-start.29 = (bf16[64,1024]{1,0:T(8,128)(2,1)}, bf16[64,1024]{1,0:T(8,128)(2,1)}, u32[]{:S(2)}, u32[]{:S(2)}) collective-permute-start(bf16[64,1024]{1,0:T(8,128)(2,1)} %get-tuple-element.83), channel_id=1, source_target_pairs={{0,1},{1,0},{2,3},{3,2},{4,5},{5,4},{6,7},{7,6},{8,9},{9,8},{10,11... | collective-permute-start | bytes 393224 | tf_op jit(solution)/shard_map/ppermute | solution.py:261
  15.4 137.2 %collective-permute-start.54 = (bf16[256,2048]{1,0:T(8,128)(2,1)}, bf16[256,2048]{1,0:T(8,128)(2,1)}, u32[]{:S(2)}, u32[]{:S(2)}) collective-permute-start(bf16[256,2048]{1,0:T(8,128)(2,1)} %param.25), channel_id=1, source_target_pairs={{0,2},{1,3},{2,0},{3,1},{4,6},{5,7},{6,4},{7,5},{8,10},{9,11},{10,... | collective-permute-start | bytes 3145736 | tf_op jit(solution)/shard_map/ppermute | solution.py:261
  90.5 58.9 %collective-permute-start.17 = (bf16[512,768]{1,0:T(8,128)(2,1)}, bf16[512,768]{1,0:T(8,128)(2,1)}, u32[]{:S(2)}, u32[]{:S(2)}) collective-permute-start(bf16[512,768]{1,0:T(8,128)(2,1)} %bitcast.335), channel_id=1, source_target_pairs={{0,8},{1,9},{2,10},{3,11},{4,12},{5,13},{6,14},{7,15},{8,16},{9,17... | collective-permute-start | bytes 2359304 | tf_op jit(solution)/shard_map/ppermute | solution.py:268
  216.0 106.9 %collective-permute-start.57 = (bf16[1024,2048]{1,0:T(8,128)(2,1)}, bf16[1024,2048]{1,0:T(8,128)(2,1)}, u32[]{:S(2)}, u32[]{:S(2)}) collective-permute-start(bf16[1024,2048]{1,0:T(8,128)(2,1)} %get-tuple-element.118), channel_id=1, source_target_pairs={{0,4},{1,5},{2,6},{3,7},{4,0},{5,1},{6,2},{7,3},{8,12},{9,13},{10,... | collective-permute-start | bytes 12582920 | tf_op jit(solution)/shard_map/ppermute | solution.py:261
  238.6 95.6 %collective-permute-start.9 = (bf16[1024,2048]{1,0:T(8,128)(2,1)}, bf16[1024,2048]{1,0:T(8,128)(2,1)}, u32[]{:S(2)}, u32[]{:S(2)}) collective-permute-start(bf16[1024,2048]{1,0:T(8,128)(2,1)} %get-tuple-element.122), channel_id=1, source_target_pairs={{0,4},{1,5},{2,6},{3,7},{4,0},{5,1},{6,2},{7,3},{8,12},{9,13},{10,... | collective-permute-start | bytes 12582920 | tf_op jit(solution)/shard_map/ppermute | solution.py:261
  258.9 43.0 %collective-permute-start.47 = (bf16[256,2048]{1,0:T(8,128)(2,1)}, bf16[256,2048]{1,0:T(8,128)(2,1)S(1)}, u32[]{:S(2)}, u32[]{:S(2)}) collective-permute-start(bf16[256,2048]{1,0:T(8,128)(2,1)} %collective-permute-done.46), channel_id=1, source_target_pairs={{8,0},{9,1},{10,2},{11,3},{12,4},{13,5},{14,6},{15,7}} | collective-permute-start | bytes 3145736 | tf_op jit(solution)/shard_map/ppermute | solution.py:268
  536.6 85.7 %collective-permute-start.100 = (bf16[256,2048]{1,0:T(8,128)(2,1)}, bf16[256,2048]{1,0:T(8,128)(2,1)}, u32[]{:S(2)}, u32[]{:S(2)}) collective-permute-start(bf16[256,2048]{1,0:T(8,128)(2,1)} %get-tuple-element.162), channel_id=1, source_target_pairs={{0,8},{1,9},{2,10},{3,11},{4,12},{5,13},{6,14},{7,15}} | collective-permute-start | bytes 3145736 | tf_op jit(solution)/shard_map/ppermute | solution.py:268
  540.3 103.4 %collective-permute-start.87 = (bf16[512,1024]{1,0:T(8,128)(2,1)}, bf16[512,1024]{1,0:T(8,128)(2,1)}, u32[]{:S(2)}, u32[]{:S(2)}) collective-permute-start(bf16[512,1024]{1,0:T(8,128)(2,1)} %get-tuple-element.160), channel_id=1, source_target_pairs={{0,8},{1,9},{2,10},{3,11},{4,12},{5,13},{6,14},{7,15}} | collective-permute-start | bytes 3145736 | tf_op jit(solution)/shard_map/ppermute | solution.py:268
  542.7 48.4 %collective-permute-start.81 = (bf16[64,2048]{1,0:T(8,128)(2,1)S(1)}, bf16[64,2048]{1,0:T(8,128)(2,1)}, u32[]{:S(2)}, u32[]{:S(2)}) collective-permute-start(bf16[64,2048]{1,0:T(8,128)(2,1)S(1)} %get-tuple-element.158), channel_id=1, source_target_pairs={{0,8},{1,9},{2,10},{3,11},{4,12},{5,13},{6,14},{7,15}} | collective-permute-start | bytes 786440 | tf_op jit(solution)/shard_map/ppermute | solution.py:268
  544.7 68.9 %collective-permute-start.68 = (bf16[512,768]{1,0:T(8,128)(2,1)}, bf16[512,768]{1,0:T(8,128)(2,1)}, u32[]{:S(2)}, u32[]{:S(2)}) collective-permute-start(bf16[512,768]{1,0:T(8,128)(2,1)} %get-tuple-element.156), channel_id=1, source_target_pairs={{0,8},{1,9},{2,10},{3,11},{4,12},{5,13},{6,14},{7,15}} | collective-permute-start | bytes 2359304 | tf_op jit(solution)/shard_map/ppermute | solution.py:268
  571.8 238.7 %collective-permute-start.48 = (bf16[1024,2048]{1,0:T(8,128)(2,1)}, bf16[1024,2048]{1,0:T(8,128)(2,1)}, u32[]{:S(2)}, u32[]{:S(2)}) collective-permute-start(bf16[1024,2048]{1,0:T(8,128)(2,1)} %add_convert_fusion.1), channel_id=1, source_target_pairs={{0,4},{1,5},{2,6},{3,7},{4,0},{5,1},{6,2},{7,3},{8,12},{9,13},{10,... | collective-permute-start | bytes 12582920 | tf_op jit(solution)/shard_map/ppermute | solution.py:261
  613.7 78.5 %collective-permute-start.83 = (bf16[64,2048]{1,0:T(8,128)(2,1)S(1)}, bf16[64,2048]{1,0:T(8,128)(2,1)S(1)}, u32[]{:S(2)}, u32[]{:S(2)}) collective-permute-start(bf16[64,2048]{1,0:T(8,128)(2,1)S(1)} %get-tuple-element.116), channel_id=1, source_target_pairs={{0,8},{1,9},{2,10},{3,11},{4,12},{5,13},{6,14},{7,15},{8,16},{9,17... | collective-permute-start | bytes 786440 | tf_op jit(solution)/shard_map/ppermute | solution.py:268
  648.2 44.7 %collective-permute-start.86 = (bf16[64,2048]{1,0:T(8,128)(2,1)S(1)}, bf16[64,2048]{1,0:T(8,128)(2,1)S(1)}, u32[]{:S(2)}, u32[]{:S(2)}) collective-permute-start(bf16[64,2048]{1,0:T(8,128)(2,1)S(1)} %add_convert_fusion.16), channel_id=1, source_target_pairs={{8,0},{9,1},{10,2},{11,3},{12,4},{13,5},{14,6},{15,7},{16,8},{17,9... | collective-permute-start | bytes 786440 | tf_op jit(solution)/shard_map/ppermute | solution.py:268
  696.7 121.7 %collective-permute-start.58 = (bf16[1024,2048]{1,0:T(8,128)(2,1)}, bf16[1024,2048]{1,0:T(8,128)(2,1)}, u32[]{:S(2)}, u32[]{:S(2)}) collective-permute-start(bf16[1024,2048]{1,0:T(8,128)(2,1)} %add_convert_fusion), channel_id=1, source_target_pairs={{0,4},{1,5},{2,6},{3,7},{4,0},{5,1},{6,2},{7,3},{8,12},{9,13},{10,... | collective-permute-start | bytes 12582920 | tf_op jit(solution)/shard_map/ppermute | solution.py:261
  702.5 98.0 %collective-permute-start.104 = (bf16[256,2048]{1,0:T(8,128)(2,1)}, bf16[256,2048]{1,0:T(8,128)(2,1)}, u32[]{:S(2)}, u32[]{:S(2)}) collective-permute-start(bf16[256,2048]{1,0:T(8,128)(2,1)} %add_convert_fusion.3), channel_id=1, source_target_pairs={{16,8},{17,9},{18,10},{19,11},{20,12},{21,13},{22,14},{23,15},{24,... | collective-permute-start | bytes 3145736 | tf_op jit(solution)/shard_map/ppermute | solution.py:268
  710.9 95.8 %collective-permute-start.91 = (bf16[512,1024]{1,0:T(8,128)(2,1)}, bf16[512,1024]{1,0:T(8,128)(2,1)}, u32[]{:S(2)}, u32[]{:S(2)}) collective-permute-start(bf16[512,1024]{1,0:T(8,128)(2,1)} %add_convert_fusion.8), channel_id=1, source_target_pairs={{16,8},{17,9},{18,10},{19,11},{20,12},{21,13},{22,14},{23,15},{24,... | collective-permute-start | bytes 3145736 | tf_op jit(solution)/shard_map/ppermute | solution.py:268
  724.1 48.5 %collective-permute-start.77 = (bf16[64,768]{1,0:T(8,128)(2,1)S(1)}, bf16[64,768]{1,0:T(8,128)(2,1)S(1)}, u32[]{:S(2)}, u32[]{:S(2)}) collective-permute-start(bf16[64,768]{1,0:T(8,128)(2,1)S(1)} %get-tuple-element.99), channel_id=1, source_target_pairs={{0,4},{1,5},{2,6},{3,7},{4,0},{5,1},{6,2},{7,3},{8,12},{9,13},{10,... | collective-permute-start | bytes 294920 | tf_op jit(solution)/shard_map/ppermute | solution.py:261
  787.8 87.1 %collective-permute-start.102 = (bf16[256,2048]{1,0:T(8,128)(2,1)}, bf16[256,2048]{1,0:T(8,128)(2,1)}, u32[]{:S(2)}, u32[]{:S(2)}) collective-permute-start(bf16[256,2048]{1,0:T(8,128)(2,1)} %get-tuple-element.47), channel_id=1, source_target_pairs={{0,8},{1,9},{2,10},{3,11},{4,12},{5,13},{6,14},{7,15},{8,16},{9,17... | collective-permute-start | bytes 3145736 | tf_op jit(solution)/shard_map/ppermute | solution.py:268
  800.5 48.8 %collective-permute-start.89 = (bf16[512,1024]{1,0:T(8,128)(2,1)}, bf16[512,1024]{1,0:T(8,128)(2,1)}, u32[]{:S(2)}, u32[]{:S(2)}) collective-permute-start(bf16[512,1024]{1,0:T(8,128)(2,1)} %get-tuple-element.49), channel_id=1, source_target_pairs={{0,8},{1,9},{2,10},{3,11},{4,12},{5,13},{6,14},{7,15},{8,16},{9,17... | collective-permute-start | bytes 3145736 | tf_op jit(solution)/shard_map/ppermute | solution.py:268
  806.7 69.8 %collective-permute-start.105 = (bf16[256,2048]{1,0:T(8,128)(2,1)}, bf16[256,2048]{1,0:T(8,128)(2,1)}, u32[]{:S(2)}, u32[]{:S(2)}) collective-permute-start(bf16[256,2048]{1,0:T(8,128)(2,1)} %add_convert_fusion.2), channel_id=1, source_target_pairs={{8,0},{9,1},{10,2},{11,3},{12,4},{13,5},{14,6},{15,7},{16,8},{17,9... | collective-permute-start | bytes 3145736 | tf_op jit(solution)/shard_map/ppermute | solution.py:268
  846.0 67.7 %collective-permute-start.50 = (bf16[256,2048]{1,0:T(8,128)(2,1)}, bf16[256,2048]{1,0:T(8,128)(2,1)}, u32[]{:S(2)}, u32[]{:S(2)}) collective-permute-start(bf16[256,2048]{1,0:T(8,128)(2,1)} %pad_maximum_fusion.8), channel_id=1, source_target_pairs={{0,1},{1,0},{2,3},{3,2},{4,5},{5,4},{6,7},{7,6},{8,9},{9,8},{10,11... | collective-permute-start | bytes 3145736 | tf_op jit(solution)/shard_map/ppermute | solution.py:261
  849.3 64.7 %collective-permute-start.52 = (bf16[256,2048]{1,0:T(8,128)(2,1)}, bf16[256,2048]{1,0:T(8,128)(2,1)}, u32[]{:S(2)}, u32[]{:S(2)}) collective-permute-start(bf16[256,2048]{1,0:T(8,128)(2,1)} %pad_maximum_fusion.9), channel_id=1, source_target_pairs={{0,2},{1,3},{2,0},{3,1},{4,6},{5,7},{6,4},{7,5},{8,10},{9,11},{10,... | collective-permute-start | bytes 3145736 | tf_op jit(solution)/shard_map/ppermute | solution.py:261
  (194 other events, 3103.2 us)

commit v2 on v0

--- a/solution.py
+++ b/solution.py
@@ -1,13 +1,20 @@
+import functools
 import math
 
 import jax
 import jax.numpy as jnp
 from jax import lax
+from jax.experimental import pallas as pl
+from jax.experimental.pallas import tpu as pltpu
 from jax.sharding import PartitionSpec as P
 
 HEADS = 32
 HEAD_DIM = 64
 ROT = 32
+CORES = 2
+AXES = ("rep", "shard")
+BF16 = jnp.bfloat16
+F32 = jnp.float32
 
 
 EPSILON = 1e-05
@@ -81,7 +88,7 @@
     )
 
 
-def on_device(
+def gathered_whole(
     tokens,
     lengths,
     ln_gain,
@@ -219,38 +226,1122 @@
     )
 
 
+MIB = 1024 * 1024
+
+
+def params(vmem=48):
+    return pltpu.CompilerParams(
+        dimension_semantics=("arbitrary",), vmem_limit_bytes=vmem * MIB
+    )
+
+
+def cost(flops, moved):
+    return pl.CostEstimate(flops=flops, bytes_accessed=moved, transcendentals=0)
+
+
+def fixed(shape, start=0):
+    index = (start,) + (0,) * (len(shape) - 1)
+    return pl.BlockSpec(shape, lambda *_: index, pipeline_mode=pl.Buffered(buffer_count=1))
+
+
+def whole(array):
+    return fixed(array.shape)
+
+
+def rows_of(array, rows, start=0):
+    return pl.BlockSpec((rows, array.shape[1]), lambda i, *_: (i + start // rows, 0))
+
+
+ANYWHERE = pl.BlockSpec(memory_space=pl.ANY)
+
+
+def kernel(body, scalars, operands, in_specs, out_specs, out_shape, grid=(1,), scratch=(), work=(0, 0)):
+    return pl.pallas_call(
+        body,
+        grid_spec=pltpu.PrefetchScalarGridSpec(
+            num_scalar_prefetch=1,
+            grid=grid,
+            in_specs=in_specs,
+            out_specs=out_specs,
+            scratch_shapes=list(scratch),
+        ),
+        out_shape=out_shape,
+        compiler_params=params(),
+        cost_estimate=cost(*work),
+    )(scalars, *operands)
+
+
+def shaped(shape, dtype=BF16):
+    return jax.ShapeDtypeStruct(shape, dtype)
+
+
+def nn(left_side, right_side):
+    return lax.dot_general(
+        left_side, right_side, (((1,), (0,)), ((), ())), preferred_element_type=F32
+    )
+
+
+def nt(left_side, right_side):
+    return lax.dot_general(
+        left_side, right_side, (((1,), (1,)), ((), ())), preferred_element_type=F32
+    )
+
+
+def tn(left_side, right_side):
+    return lax.dot_general(
+        left_side, right_side, (((0,), (0,)), ((), ())), preferred_element_type=F32
+    )
+
+
+HALF, MIDDLE, ODD, CORE, CHIP = range(5)
+
+
+def copy_all(copies, sems):
+    for at, (source, target) in enumerate(copies):
+        pltpu.make_async_copy(source, target, sems.at[at]).start()
+    for at, (source, target) in enumerate(copies):
+        pltpu.make_async_copy(source, target, sems.at[at]).wait()
+
+
+def copy_either(where, common, if_middle, if_end, sems):
+    @pl.when(where[MIDDLE] == 1)
+    def _():
+        copy_all(common + if_middle, sems)
+
+    @pl.when(where[MIDDLE] == 0)
+    def _():
+        copy_all(common + if_end, sems)
+
+
+def multiple(value, size):
+    return pl.multiple_of(value * size, size)
+
+
+def attention_body(parts, merge, where, *refs):
+    if merge:
+        hidden, cot, pair, middle_left, middle_right, end_left, end_right = refs[:7]
+        bias, cosine, sine_a, sine_b, first = refs[7:12]
+        prior = ()
+        context, d_packed, *grads = refs[12:18]
+        qkv_w, dense_w, sum_qkv, sum_dense, sems = refs[18:]
+    else:
+        hidden, cot, qkv_w, dense_w, bias, cosine, sine_a, sine_b, first = refs[:9]
+        prior = refs[9:13]
+        context, d_packed, *grads = refs[13:19]
+        sum_qkv, sum_dense = refs[19:]
+    step = pl.program_id(0)
+    run, wide = hidden.shape[0], dense_w.shape[0]
+    scaling = 1.0 / math.sqrt(HEAD_DIM)
+    block, own = sum_qkv.shape[0] // 4, wide // 4
+    across = dense_w.shape[1] // parts
+    left_columns = grads[0].shape[1]
+
+    if merge:
+
+        @pl.when(step == 0)
+        def _():
+            half = where[HALF]
+
+            def dense_copies(source, side, first_column):
+                return [
+                    (
+                        source.at[
+                            i * block + j * own : i * block + (j + 1) * own,
+                            first_column : first_column + across,
+                        ],
+                        dense_w.at[
+                            pl.ds(multiple(2 * side + i, own), own), j * across : (j + 1) * across
+                        ],
+                    )
+                    for i in range(2)
+                    for j in range(parts)
+                ]
+
+            rows, rest = 2 * block, 3 * wide - left_columns
+
+            def others(left, right):
+                return [
+                    (left, qkv_w.at[rows:, :left_columns]),
+                    (right.at[:, :rest], qkv_w.at[rows:, left_columns:]),
+                ] + dense_copies(right, 1 - half, rest)
+
+            common = [(pair.at[:, : 3 * wide], qkv_w.at[:rows])]
+            common += dense_copies(pair, half, 3 * wide)
+            copy_either(
+                where, common, others(middle_left, middle_right), others(end_left, end_right), sems
+            )
+
+    c = jnp.tile(cosine[...], (1, wide // 128))
+    sa = jnp.tile(sine_a[...], (1, wide // 128))
+    sb = jnp.tile(sine_b[...], (1, wide // 128))
+
+    def turn(value, sign):
+        ahead = pltpu.roll(value, wide - ROT // 2, 1)
+        behind = pltpu.roll(value, ROT // 2, 1)
+        return value * c + sign * (ahead * sa + behind * sb)
+
+    packed = nn(hidden[...], qkv_w[...]) + bias[...]
+    queries = (turn(packed[:, :wide], 1.0).astype(BF16).astype(F32) * scaling).astype(BF16)
+    keys = turn(packed[:, wide : 2 * wide], 1.0).astype(BF16)
+    values = packed[:, 2 * wide :].astype(BF16)
+    d_context = nt(cot[...], dense_w[...]).astype(BF16)
+    at = lax.broadcasted_iota(jnp.int32, (run, run), 1)
+    row = lax.broadcasted_iota(jnp.int32, (run, run), 0)
+    seen = (at >= first[:, :1]) & (at <= row)
+    out, d_q, d_k, d_v = [], [], [], []
+    for h in range(wide // HEAD_DIM):
+        part = slice(h * HEAD_DIM, (h + 1) * HEAD_DIM)
+        q, k, v, g = queries[:, part], keys[:, part], values[:, part], d_context[:, part]
+        scores = jnp.where(seen, nt(q, k), -1e30)
+        raised = jnp.exp(scores - jnp.max(scores, axis=1, keepdims=True))
+        probs = raised * (1.0 / jnp.sum(raised, axis=1, keepdims=True))
+        low = probs.astype(BF16)
+        o = nn(low, v)
+        out.append(o)
+        d_v.append(tn(low, g))
+        delta = jnp.sum(o * g.astype(F32), axis=1, keepdims=True)
+        d_scores = (probs * (nt(g, v) - delta)).astype(BF16)
+        d_q.append(nn(d_scores, k) * scaling)
+        d_k.append(tn(d_scores, q))
+    context[...] = jnp.concatenate(out, axis=1).astype(BF16)
+    d_packed[:, :wide] = turn(jnp.concatenate(d_q, axis=1), -1.0).astype(BF16)
+    d_packed[:, wide : 2 * wide] = turn(jnp.concatenate(d_k, axis=1), -1.0).astype(BF16)
+    d_packed[:, 2 * wide :] = jnp.concatenate(d_v, axis=1).astype(BF16)
+
+    @pl.when(step == 0)
+    def _():
+        sum_qkv[...] = jnp.zeros_like(sum_qkv)
+        sum_dense[...] = jnp.zeros_like(sum_dense)
+
+    sum_qkv[...] += tn(hidden[...], d_packed[...])
+    sum_dense[...] += tn(context[...], cot[...])
+
+    @pl.when(step == pl.num_programs(0) - 1)
+    def _():
+        for pair_at in range(2):
+            for i in range(2):
+                half = where[HALF] if pair_at == 0 else 1 - where[HALF]
+                rows = slice(i * block, (i + 1) * block)
+                start = (2 * pair_at + i) * block
+                summed = sum_qkv[start : start + block]
+                beside = sum_dense[pl.ds(multiple(2 * half + i, own), own), :]
+                beside = jnp.concatenate(
+                    [beside[:, j * across : (j + 1) * across] for j in range(parts)], axis=0
+                )
+                first_half = summed[:, :left_columns]
+                second_half = jnp.concatenate([summed[:, left_columns:], beside], axis=1)
+                if prior:
+                    first_half += prior[2 * pair_at][rows].astype(F32)
+                    second_half += prior[2 * pair_at + 1][rows].astype(F32)
+                grads[2 * pair_at][rows] = first_half.astype(BF16)
+                grads[2 * pair_at + 1][rows] = second_half.astype(BF16)
+
+
+def attention(where, run, start, count, parts, hidden, cot, weights, streams, prior):
+    width = hidden.shape[1]
+    merge = len(weights) == 5
+    bias = streams[0]
+    wide = bias.shape[1] // 3
+    grad = shaped((width // 2, (3 * wide + width // parts) // 2))
+    sums = [pltpu.VMEM((width, 3 * wide), F32), pltpu.VMEM((wide, width), F32)]
+    joined = [shaped((width, 3 * wide)), shaped((wide, width))] if merge else []
+    outs = kernel(
+        functools.partial(attention_body, parts, merge),
+        where,
+        [hidden, cot, *weights, *streams, *prior],
+        [rows_of(hidden, run, start), rows_of(cot, run, start)]
+        + ([ANYWHERE] * 5 if merge else [whole(array) for array in weights])
+        + [whole(bias)]
+        + [rows_of(array, run, start) for array in streams[1:]]
+        + [whole(array) for array in prior],
+        [
+            pl.BlockSpec((run, wide), lambda i, _: (i, 0)),
+            pl.BlockSpec((run, 3 * wide), lambda i, _: (i, 0)),
+        ]
+        + [fixed(grad.shape)] * 4
+        + [fixed(array.shape) for array in joined],
+        [shaped((count, wide)), shaped((count, 3 * wide))] + [grad] * 4 + joined,
+        grid=(count // run,),
+        scratch=sums + ([pltpu.SemaphoreType.DMA((3 + 4 * parts,))] if merge else []),
+        work=(18 * 10**9, 20 * MIB),
+    )
+    return outs[0], outs[1], outs[2:6], outs[6:]
+
+
+GELU_A = math.sqrt(2.0 / math.pi)
+GELU_B = 0.044715
+
+
+def write_halves(where, total, grads, order):
+    rows, columns = grads[0].shape
+    for pair_at in range(2):
+        if order:
+            half = where[HALF] if pair_at == 0 else 1 - where[HALF]
+            part = pl.ds(multiple(half, rows), rows)
+        else:
+            part = slice(pair_at * rows, (pair_at + 1) * rows)
+        for side in range(2):
+            grads[2 * pair_at + side][...] = total[
+                part, side * columns : (side + 1) * columns
+            ].astype(BF16)
+
+
+def forward_body(
+    columns,
+    where,
+    hidden,
+    cot,
+    pair,
+    middle_left,
+    middle_right,
+    end_left,
+    end_right,
+    bias,
+    active,
+    slope,
+    up_w,
+    *rest,
+):
+    grads, total, sems = rest[:-2], rest[-2], rest[-1]
+    step = pl.program_id(0)
+
+    @pl.when(step == 0)
+    def _():
+        rows, middle = pair.shape[0], middle_left.shape[1]
+
+        def others(left, right):
+            return [(left, up_w.at[rows:, :middle]), (right, up_w.at[rows:, middle:])]
+
+        copy_either(
+            where,
+            [(pair, up_w.at[:rows])],
+            others(middle_left, middle_right),
+            others(end_left, end_right),
+            sems,
+        )
+        total[...] = jnp.zeros_like(total)
+
+    for j in range(up_w.shape[1] // columns):
+        part = slice(j * columns, (j + 1) * columns)
+        v = nn(hidden[...], up_w[:, part]) + bias[:, part]
+        square = v * v
+        t = jnp.tanh(GELU_A * v * (1.0 + GELU_B * square))
+        gate = 0.5 * (1.0 + t)
+        low = (v * gate).astype(BF16)
+        active[:, part] = low
+        slope[:, part] = (
+            gate + 0.5 * v * (1.0 - t * t) * (GELU_A + (3.0 * GELU_A * GELU_B) * square)
+        ).astype(BF16)
+        total[part] += tn(low, cot[...])
+
+    @pl.when(step == pl.num_programs(0) - 1)
+    def _():
+        write_halves(where, total, grads, True)
+
+
+def forward(where, hidden, cot, pieces, bias, rows=512, columns=512):
+    count, wide = hidden.shape[0], bias.shape[1]
+    width = cot.shape[1]
+    grad = shaped((wide // 2, width // 2))
+    outs = kernel(
+        functools.partial(forward_body, columns),
+        where,
+        [hidden, cot, *pieces, bias],
+        [rows_of(hidden, rows), rows_of(cot, rows)] + [ANYWHERE] * 5 + [whole(bias)],
+        [pl.BlockSpec((rows, wide), lambda i, _: (i, 0))] * 2
+        + [fixed((width, wide))]
+        + [fixed(grad.shape)] * 4,
+        [shaped((count, wide))] * 2 + [shaped((width, wide))] + [grad] * 4,
+        grid=(count // rows,),
+        scratch=[pltpu.VMEM((wide, width), F32), pltpu.SemaphoreType.DMA((3,))],
+        work=(4 * hidden.size * wide, 32 * MIB),
+    )
+    return outs[0], outs[1], outs[2], outs[3:]
+
+
+def backward_body(
+    where,
+    cot,
+    hidden,
+    pair,
+    middle_left,
+    middle_right,
+    end_left,
+    end_right,
+    slope,
+    d_upward,
+    sums,
+    down_w,
+    *rest,
+):
+    grads, total, sems = rest[:-2], rest[-2], rest[-1]
+    step = pl.program_id(0)
+
+    @pl.when(step == 0)
+    def _():
+        rows, middle = middle_left.shape
+
+        def others(left, right):
+            part = pl.ds(multiple(1 - where[HALF], rows), rows)
+            return [(left, down_w.at[part, :middle]), (right, down_w.at[part, middle:])]
+
+        copy_either(
+            where,
+            [(pair, down_w.at[pl.ds(multiple(where[HALF], rows), rows)])],
+            others(middle_left, middle_right),
+            others(end_left, end_right),
+            sems,
+        )
+        sums[...] = jnp.zeros_like(sums)
+        total[...] = jnp.zeros_like(total)
+
+    low = (nt(cot[...], down_w[...]) * slope[...].astype(F32)).astype(BF16)
+    d_upward[...] = low
+    sums[...] += jnp.sum(low.astype(F32), axis=0, keepdims=True)
+    total[...] += tn(hidden[...], low)
+
+    @pl.when(step == pl.num_programs(0) - 1)
+    def _():
+        write_halves(where, total, grads, False)
+
+
+def backward(where, cot, hidden, pieces, slope, rows=256):
+    count, wide = slope.shape
+    width = hidden.shape[1]
+    grad = shaped((width // 2, wide // 2))
+    outs = kernel(
+        backward_body,
+        where,
+        [cot, hidden, *pieces, slope],
+        [rows_of(cot, rows), rows_of(hidden, rows)] + [ANYWHERE] * 5 + [rows_of(slope, rows)],
+        [
+            pl.BlockSpec((rows, wide), lambda i, _: (i, 0)),
+            pl.BlockSpec((1, wide), lambda i, _: (0, 0)),
+            fixed((wide, width)),
+        ]
+        + [fixed(grad.shape)] * 4,
+        [shaped((count, wide)), shaped((1, wide), F32), shaped((wide, width))] + [grad] * 4,
+        grid=(count // rows,),
+        scratch=[pltpu.VMEM((width, wide), F32), pltpu.SemaphoreType.DMA((3,))],
+        work=(4 * cot.size * wide, 32 * MIB),
+    )
+    return outs[0], outs[1], outs[2], outs[3:]
+
+
+def two_dots_body(dot, a, aw, b, bw, far, near):
+    result = (dot(a[...], aw[...]) + dot(b[...], bw[...])).astype(BF16)
+    step, half = pl.program_id(0), pl.num_programs(0) // 2
+
+    @pl.when(step < half)
+    def _():
+        far[...] = result
+
+    @pl.when(step >= half)
+    def _():
+        near[...] = result
+
+
+def two_dots(dot, a, aw, b, bw, width, rows=256):
+    count = a.shape[0]
+    steps = count // rows
+    half = steps // 2
+
+    def of(array):
+        return pl.BlockSpec((rows, array.shape[1]), lambda i: (lax.rem(i + half, steps), 0))
+
+    shape = jax.ShapeDtypeStruct((count // 2, width), BF16)
+    return pl.pallas_call(
+        functools.partial(two_dots_body, dot),
+        grid=(steps,),
+        in_specs=[of(a), whole(aw), of(b), whole(bw)],
+        out_specs=[
+            pl.BlockSpec((rows, width), lambda i: (jnp.minimum(i, half - 1), 0)),
+            pl.BlockSpec((rows, width), lambda i: (jnp.maximum(i - half, 0), 0)),
+        ],
+        out_shape=[shape, shape],
+        compiler_params=params(),
+        cost_estimate=cost(
+            2 * count * (aw.size + bw.size),
+            count * 2 * (width + a.shape[1] + b.shape[1]) + 2 * (aw.size + bw.size),
+        ),
+    )(a, aw, b, bw)
+
+
+def deal_first_body(planes, chips, where, up, qkv, keep, send):
+    mates, n = CORES * chips, up.shape[0]
+    block = up.shape[1] // (planes * mates)
+    for core in range(CORES):
+        for chip in range(chips):
+            i = core * chips + chip
+            pieces = [
+                up[:, (p * mates + i) * block : (p * mates + i + 1) * block] for p in range(planes)
+            ] + [
+                qkv[:, (t * mates + i) * HEAD_DIM : (t * mates + i + 1) * HEAD_DIM]
+                for t in range(3 * planes)
+            ]
+            value = jnp.concatenate(pieces, axis=1)
+
+            @pl.when(where[CORE] == core)
+            def _():
+                keep[chip] = value
+
+            @pl.when(where[CORE] != core)
+            def _():
+                send[chip] = value
+
+
+def deal_first(where, planes, chips, up, qkv):
+    out = shaped((chips, up.shape[0], (up.shape[1] + qkv.shape[1]) // (CORES * chips)))
+    return kernel(
+        functools.partial(deal_first_body, planes, chips),
+        where,
+        [up, qkv],
+        [whole(up), whole(qkv)],
+        [fixed(out.shape)] * 2,
+        [out] * 2,
+        work=(0, 4 * MIB),
+    )
+
+
+def deal_second_body(where, keep, came, *outs):
+    core = where[CORE]
+    for r, out in enumerate(outs):
+        at = where[CHIP] ^ r
+        out[pl.ds(core, 1)] = keep[pl.ds(at, 1)]
+        out[pl.ds(1 - core, 1)] = came[pl.ds(at, 1)]
+
+
+def deal_second(where, keep, came):
+    chips, n, columns = keep.shape
+    out = shaped((CORES, n, columns))
+    return kernel(
+        deal_second_body,
+        where,
+        [keep, came],
+        [whole(keep), whole(came)],
+        [fixed(out.shape)] * chips,
+        [out] * chips,
+        work=(0, 4 * MIB),
+    )
+
+
+def deal_last_body(chips, where, *refs):
+    blocks, dense, (u, a) = refs[:chips], refs[chips], refs[chips + 1 :]
+    n, columns = blocks[0].shape[1:]
+    middle = u.shape[1]
+    wide = columns - middle
+    for r, block in enumerate(blocks):
+        for core in range(CORES):
+            rows = pl.ds(multiple(core * chips + (where[CHIP] ^ r), n), n)
+            u[rows, :] = block[core, :, :middle]
+            a[rows, :wide] = block[core, :, middle:]
+    across = a.shape[1] - wide
+    for j in range(dense.shape[1] // across):
+        a[j * n : (j + 1) * n, wide:] = dense[:, j * across : (j + 1) * across]
+
+
+def deal_last(where, blocks, dense, middle):
+    chips = len(blocks)
+    n, columns = blocks[0].shape[1:]
+    mates = CORES * chips
+    shapes = [
+        shaped((mates * n, middle)),
+        shaped((mates * n, columns - middle + dense.shape[1] // mates)),
+    ]
+    return kernel(
+        functools.partial(deal_last_body, chips),
+        where,
+        [*blocks, dense],
+        [whole(array) for array in (*blocks, dense)],
+        [fixed(shape.shape) for shape in shapes],
+        shapes,
+        work=(0, 4 * MIB),
+    )
+
+
+def finish_body(chips, wide, where, own_left, own_right, came_left, came_right, left, right, *outs):
+    keep, send = outs[:2]
+    n, columns = left.shape[0], left.shape[1]
+    step = n // (CORES * chips)
+    total = jnp.concatenate(
+        [
+            own[...].astype(F32) + came[...].astype(F32) + last[...].astype(F32)
+            for own, came, last in (
+                (own_left, came_left, left),
+                (own_right, came_right, right),
+            )
+        ],
+        axis=1,
+    )
+    low = total[:, :wide].astype(BF16)
+    for core in range(CORES):
+
+        @pl.when(where[CORE] == core)
+        def _():
+            for chip in range(chips):
+                at = (core * chips + chip) * step
+                keep[chip] = low[at : at + step]
+                at = ((1 - core) * chips + chip) * step
+                send[chip] = low[at : at + step]
+
+    if len(outs) == 3:
+        beside = outs[2]
+        across = total.shape[1] - wide
+        for j in range(n // step):
+            beside[:, j * across : (j + 1) * across] = total[j * step : (j + 1) * step, wide:]
+
+
+def finish(where, chips, wide, own_left, own_right, came_left, came_right, left, right):
+    n, columns = left.shape
+    mine = pl.BlockSpec((n, columns), lambda i, where: (where[ODD], 0))
+    step = n // (CORES * chips)
+    shapes = [shaped((chips, step, wide))] * 2
+    if wide < 2 * columns:
+        shapes.append(shaped((step, (2 * columns - wide) * CORES * chips), F32))
+    return kernel(
+        functools.partial(finish_body, chips, wide),
+        where,
+        [own_left, own_right, came_left, came_right, left, right],
+        [mine] * 4 + [whole(left), whole(right)],
+        [fixed(shape.shape) for shape in shapes],
+        shapes,
+        work=(0, 4 * MIB),
+    )
+
+
+def back_body(groups, where, *refs):
+    blocks, out, held = refs[:-2], refs[-2], refs[-1]
+    chips = len(blocks)
+    n, columns = blocks[0].shape[1:]
+    size = columns // groups
+    for r, block in enumerate(blocks):
+        held[pl.ds(where[CHIP] ^ r, 1)] = block[...][None]
+    for group in range(groups):
+        for core in range(CORES):
+            start = (group * CORES + core) * chips * size
+            out[:, start : start + chips * size] = jnp.concatenate(
+                [held[chip, core, :, group * size : (group + 1) * size] for chip in range(chips)],
+                axis=1,
+            ).astype(F32)
+
+
+def back(where, blocks, groups):
+    chips = len(blocks)
+    n, columns = blocks[0].shape[1:]
+    out = shaped((n, columns * CORES * chips), F32)
+    return kernel(
+        functools.partial(back_body, groups),
+        where,
+        blocks,
+        [whole(block) for block in blocks],
+        fixed(out.shape),
+        out,
+        scratch=[pltpu.VMEM((chips,) + blocks[0].shape, BF16)],
+        work=(0, 4 * MIB),
+    )
+
+
+def corners_body(where, near_a, near_b, came_a, came_b, first, second):
+    first[...] = (near_a[...].astype(F32) + came_a[...].astype(F32)).astype(BF16)
+    second[...] = (near_b[...].astype(F32) + came_b[...].astype(F32)).astype(BF16)
+
+
+def corners(where, near, came):
+    rows, width = near.shape[0] // 8, near.shape[1]
+    blocks = [fixed((rows, width), 6), fixed((rows, width), 7)]
+    return kernel(
+        corners_body,
+        where,
+        [near, near, came, came],
+        blocks * 2,
+        [fixed((rows, width))] * 2,
+        [shaped((rows, width))] * 2,
+        work=(0, 4 * MIB),
+    )
+
+
+def sides_body(where, near_x, near_y, came_x, came_y, extra_x, extra_y, for_x, for_y):
+    half = extra_x.shape[0]
+    x = near_x[...].astype(F32) + came_x[...].astype(F32)
+    y = near_y[...].astype(F32) + came_y[...].astype(F32)
+    for_x[:half] = x[:half].astype(BF16)
+    for_x[half:] = (x[half:] + extra_x[...].astype(F32)).astype(BF16)
+    for_y[:half] = (y[:half] + extra_y[...].astype(F32)).astype(BF16)
+    for_y[half:] = y[half:].astype(BF16)
+
+
+def sides(where, near, came, extra_y, extra_x):
+    rows, width = near.shape[0] // 4, near.shape[1]
+    blocks = [fixed((rows, width), 1), fixed((rows, width), 2)]
+    return kernel(
+        sides_body,
+        where,
+        [near, near, came, came, extra_x, extra_y],
+        blocks * 2 + [whole(extra_x), whole(extra_y)],
+        [fixed((rows, width))] * 2,
+        [shaped((rows, width))] * 2,
+        work=(0, 8 * MIB),
+    )
+
+
+def norm_back_body(
+    where, near, came, by_x, by_y, tokens, cot, gain, grad_tokens, gain_sum, shift_sum
+):
+    parts = [ref[...].astype(F32) for ref in (near, came, by_x, by_y)]
+    turned = parts[0] + parts[1] + parts[2] + parts[3]
+    middle = turned.shape[1] // 2
+    swap = where[HALF] == 1
+    lower, upper = turned[:, :middle], turned[:, middle:]
+    d_hidden = jnp.concatenate(
+        [jnp.where(swap, upper, lower), jnp.where(swap, lower, upper)], axis=1
+    )
+    inputs = tokens[...].astype(F32)
+    centered = inputs - jnp.mean(inputs, axis=1, keepdims=True)
+    inv_std = lax.rsqrt(jnp.mean(centered * centered, axis=1, keepdims=True) + EPSILON)
+    normed = centered * inv_std
+    d_norm = d_hidden * gain[...]
+    d_inputs = inv_std * (
+        d_norm
+        - jnp.mean(d_norm, axis=1, keepdims=True)
+        - normed * jnp.mean(d_norm * normed, axis=1, keepdims=True)
+    )
+    grad_tokens[...] = (cot[...].astype(F32) + d_inputs).astype(BF16)
+
+    @pl.when(pl.program_id(0) == 0)
+    def _():
+        gain_sum[...] = jnp.zeros_like(gain_sum)
+        shift_sum[...] = jnp.zeros_like(shift_sum)
+
+    gain_sum[...] += jnp.sum(d_hidden * normed, axis=0, keepdims=True)
+    shift_sum[...] += jnp.sum(d_hidden, axis=0, keepdims=True)
+
+
+def norm_back(where, near, came, by_x, by_y, tokens, cot, gain, rows=128):
+    count, width = tokens.shape
+    block = pl.BlockSpec((rows, width), lambda i, _: (i, 0))
+    return kernel(
+        norm_back_body,
+        where,
+        [near, came, by_x, by_y, tokens, cot, gain],
+        [block] * 6 + [whole(gain)],
+        [block, fixed((1, width)), fixed((1, width))],
+        [shaped((count, width)), shaped((1, width), F32), shaped((1, width), F32)],
+        grid=(count // rows,),
+        work=(0, 8 * MIB),
+    )
+
+
+def tied(*groups):
+    return lax.optimization_barrier(groups)
+
+
+def by_planes(
+    planes,
+    mates,
+    tokens,
+    lengths,
+    ln_gain,
+    ln_bias,
+    qkv_weight,
+    qkv_bias,
+    dense_weight,
+    dense_bias,
+    up_weight,
+    up_bias,
+    down_weight,
+    down_bias,
+    cotangent,
+):
+    row_count, width = tokens.shape
+    owners = planes * mates
+    chips = mates // CORES
+    rank = lax.axis_index("rep") * chips + lax.axis_index("shard")
+    z, m = rank // mates, rank % mates
+    c, s = m // chips, m % chips
+    middle_plane = jnp.where((z == 1) | (z == 2), 1, 0)
+    where = jnp.stack([z // 2, middle_plane, z % 2, c, s]).astype(jnp.int32)
+    rows_own = qkv_weight.shape[0]
+    ff_block = up_bias.shape[0]
+    heads_width = planes * HEAD_DIM
+    count = mates * row_count
+
+    def flip(value, r):
+        return lax.ppermute(
+            value,
+            AXES,
+            [(p * mates + i, p * mates + (i ^ r)) for p in range(planes) for i in range(mates)],
+        )
+
+    def between(value, pairs):
+        return lax.ppermute(
+            value, AXES, [(p * mates + i, q * mates + i) for p, q in pairs for i in range(mates)]
+        )
+
+    def to_neighbour(value):
+        return between(value, [(p, p ^ 1) for p in range(planes)])
+
+    def over_middle(value):
+        return between(value, [(1, 2), (2, 1)])
+
+    def outwards(value):
+        return between(value, [(1, 0), (2, 3)])
+
+    def inwards(value):
+        return between(value, [(0, 1), (3, 2)])
+
+    def paired(own, came):
+        return jnp.where(
+            z % 2 == 0,
+            jnp.concatenate([own, came], axis=0),
+            jnp.concatenate([came, own], axis=0),
+        )
+
+    def added(*terms):
+        return sum(term.astype(F32) for term in terms)
+
+    def middle_share(other, came):
+        return added(other, came).astype(BF16)
+
+    def neighbour_share(own, came):
+        size = own.shape[0] // 2
+        lower, upper = [added(own[part], came[part]) for part in (slice(0, size), slice(size, None))]
+        return jnp.where(z % 2 == 1, lower, upper).astype(BF16)
+
+    def deal_over_chips(keep, send):
+        blocks = deal_second(where, keep, flip(send, chips))
+        return [blocks[0]] + [flip(blocks[r], r) for r in range(1, chips)]
+
+    def over_planes(table):
+        for r in (1, 2):
+            table = table + between(table, [(p, p ^ r) for p in range(planes)])
+        return table
+
+    def over_mates(table):
+        for r in (1, 2, 4):
+            table = table + flip(table, r)
+        return table
+
+    def left(value):
+        return value[:, : value.shape[1] // 2]
+
+    def right(value):
+        return value[:, value.shape[1] // 2 :]
+
+    def turned(value):
+        middle = value.shape[1] // 2
+        lower, upper, first_half = value[:, :middle], value[:, middle:], z < 2
+        return jnp.concatenate(
+            [jnp.where(first_half, lower, upper), jnp.where(first_half, upper, lower)], axis=1
+        )
+
+    half = row_count // 2
+
+    def near_first(block):
+        return flip(block, 1), flip(block, 2)
+
+    def near_second(by_x, by_y):
+        return flip(by_y[:half], 1), flip(by_x[half:], 2)
+
+    def most_of(block, by_x, by_y):
+        return jnp.concatenate([block, by_x, by_y], axis=0)
+
+    parts = [ln_gain, ln_bias, qkv_bias, dense_bias, up_bias, down_bias, lengths[0].astype(BF16)]
+    sizes = [part.shape[0] for part in parts]
+    starts = [sum(sizes[:i]) for i in range(len(sizes))]
+    own_row = jnp.concatenate(parts)
+    own_row = jnp.pad(own_row, (0, -len(own_row) % 128))
+    table = jnp.where(jnp.arange(owners)[:, None] == rank, own_row[None, :], 0)
+    table, down_own = tied(over_planes(table), down_weight)
+
+    wide = 3 * heads_width
+    w1 = to_neighbour(down_own)
+    dealt = deal_over_chips(*deal_first(where, planes, chips, up_weight, qkv_weight))
+    u_own, a_own = deal_last(where, dealt, dense_weight, planes * ff_block)
+    table = over_mates(table).astype(F32)
+
+    def column(i):
+        return table[:, starts[i] : starts[i] + sizes[i]].reshape(-1)
+
+    gain, shift_by = column(0), column(1)
+    packed_bias = lax.dynamic_index_in_dim(
+        column(2).reshape(3, planes, mates, HEAD_DIM), m, 2, keepdims=False
+    ).reshape(1, -1)
+    upward_bias = lax.dynamic_index_in_dim(
+        column(4).reshape(planes, mates, ff_block), m, 1, keepdims=False
+    ).reshape(1, -1)
+    out_bias = column(3) + column(5)
+    all_lengths = table[:, starts[6] : starts[6] + sizes[6]].astype(jnp.int32)
+    doc_sizes = jnp.stack(
+        [
+            lax.dynamic_index_in_dim(all_lengths, z * mates + (m ^ r), 0, keepdims=False)
+            for r in range(mates)
+        ]
+    )
+
+    inputs_f = tokens.astype(F32)
+    average = jnp.mean(inputs_f, axis=1, keepdims=True)
+    centered = inputs_f - average
+    spread = jnp.mean(centered * centered, axis=1, keepdims=True)
+    inv_std = lax.rsqrt(spread + EPSILON)
+    normed = centered * inv_std
+    hidden_own = turned((normed * gain + shift_by).astype(BF16))
+
+    ends_at = jnp.cumsum(doc_sizes, axis=1)
+    at = jnp.arange(row_count, dtype=jnp.int32)
+    offsets = jnp.max(jnp.where(at[None, :, None] >= ends_at[:, None, :], ends_at[:, None, :], 0), axis=2)
+    places = (at[None, :] - offsets).astype(F32).reshape(count, 1)
+    lane = jnp.arange(2 * HEAD_DIM, dtype=jnp.int32) % HEAD_DIM
+    inverse = jnp.power(jnp.float32(10000.0), -2.0 * (lane % (ROT // 2)).astype(F32) / ROT)
+    angles = places * inverse[None, :]
+    sine = jnp.sin(angles)
+    cosine = jnp.where(lane < ROT, jnp.cos(angles), 1.0)
+    sine_a = jnp.where(lane < ROT // 2, -sine, 0.0)
+    sine_b = jnp.where((lane >= ROT // 2) & (lane < ROT), sine, 0.0)
+    first = jnp.broadcast_to(offsets.reshape(count, 1), (count, 2 * HEAD_DIM))
+
+    w1, u_own, a_own, cot_own = tied(w1, u_own, a_own, cotangent)
+
+    w_pair = paired(down_own, w1)
+    u1 = to_neighbour(u_own)
+    w2_left = over_middle(left(w_pair))
+    cot_near = near_first(cot_own)
+
+    u1, w2_left, cot_near, a_own, hidden_own = tied(u1, w2_left, cot_near, a_own, hidden_own)
+    u_pair = paired(u_own, u1)
+    u2_left = over_middle(left(u_pair))
+    a1 = to_neighbour(a_own)
+    hidden_near = near_first(hidden_own)
+    cot_most = most_of(cot_own, *cot_near)
+    cot_across = flip(cot_most, chips)
+
+    u2_left, a1, hidden_near, cot_across, u_pair, cot_near = tied(
+        u2_left, a1, hidden_near, cot_across, u_pair, cot_near
+    )
+    a_pair = paired(a_own, a1)
+    u3_left = outwards(u2_left)
+    u2_right = over_middle(right(u_pair))
+    corner_y = flip(jnp.concatenate([cot_near[1][:half], hidden_near[1][:half]], axis=0), 1)
+    corner_x = flip(jnp.concatenate([cot_near[0][half:], hidden_near[0][half:]], axis=0), 2)
+    hidden_most = most_of(hidden_own, *hidden_near)
+    hidden_across = flip(hidden_most, chips)
+
+    u3_left, u2_right, corner_x, corner_y, a_pair, hidden_across = tied(
+        u3_left, u2_right, corner_x, corner_y, a_pair, hidden_across
+    )
+    u3_right = outwards(u2_right)
+    a2_left = over_middle(left(a_pair))
+    corner = jnp.concatenate([corner_y, corner_x], axis=0)
+    corner_across = flip(corner, chips)
+
+    def all_rows(most, across, at):
+        pieces = [most]
+        for corners_of in (corner, corner_across):
+            pieces += [corners_of[at : at + half], corners_of[at + 2 * half : at + 3 * half]]
+        return jnp.concatenate(pieces[:3] + [across] + pieces[3:], axis=0)
+
+    cot, hidden = all_rows(cot_most, cot_across, 0), all_rows(hidden_most, hidden_across, half)
+    u3_right, a2_left, a_pair, hidden, cot = tied(u3_right, a2_left, a_pair, hidden, cot)
+    a3_left = outwards(a2_left)
+    a2_right = over_middle(right(a_pair))
+    active, slope, up_w, g_w = forward(
+        where, hidden, cot, [u_pair, u2_left, u2_right, u3_left, u3_right], upward_bias
+    )
+
+    a3_left, a2_right, g_w, w_pair, cosine, sine_a, sine_b, first = tied(
+        a3_left, a2_right, g_w, w_pair, cosine, sine_a, sine_b, first
+    )
+    a3_right = outwards(a2_right)
+    w2_right = over_middle(right(w_pair))
+    q1_w_left = inwards(g_w[2])
+
+    a3_right, w2_right, q1_w_left, w2_left, g_w, hidden = tied(
+        a3_right, w2_right, q1_w_left, w2_left, g_w, hidden
+    )
+    w3_left = outwards(w2_left)
+    q1_w_right = inwards(g_w[3])
+    q2_w_left = over_middle(middle_share(g_w[2], q1_w_left))
+    streams = [packed_bias, cosine, sine_a, sine_b, first]
+    context_a, d_packed_a, g_a, (qkv_w, dense_w) = attention(
+        where,
+        row_count,
+        0,
+        count // 2,
+        mates,
+        hidden,
+        cot,
+        [a_pair, a2_left, a2_right, a3_left, a3_right],
+        streams,
+        [],
+    )
+
+    w3_left, q1_w_right, q2_w_left, w2_right, g_a, hidden, g_w = tied(
+        w3_left, q1_w_right, q2_w_left, w2_right, g_a, hidden, g_w
+    )
+    w3_right = outwards(w2_right)
+    q2_w_right = over_middle(middle_share(g_w[3], q1_w_right))
+    q3_w_left = to_neighbour(neighbour_share(g_w[0], q2_w_left))
+    context_b, d_packed_b, g_a, _ = attention(
+        where,
+        row_count,
+        count // 2,
+        count // 2,
+        mates,
+        hidden,
+        cot,
+        [qkv_w, dense_w],
+        streams,
+        g_a,
+    )
+
+    w3_right, q2_w_right, q3_w_left, g_a, cot, slope, g_w = tied(
+        w3_right, q2_w_right, q3_w_left, g_a, cot, slope, g_w
+    )
+    q1_a_left = inwards(g_a[2])
+    q3_w_right = to_neighbour(neighbour_share(g_w[1], q2_w_right))
+    d_upward, upward_sum, down_w, g_u = backward(
+        where, cot, hidden, [w_pair, w2_left, w2_right, w3_left, w3_right], slope
+    )
+
+    q1_a_left, q3_w_right, q3_w_left, g_u, d_upward, g_a = tied(
+        q1_a_left, q3_w_right, q3_w_left, g_u, d_upward, g_a
+    )
+    q1_a_right = inwards(g_a[3])
+    q2_a_left = over_middle(middle_share(g_a[2], q1_a_left))
+    context = jnp.concatenate([context_a, context_b], axis=0)
+    d_packed = jnp.concatenate([d_packed_a, d_packed_b], axis=0)
+    d_hidden_far, d_hidden_near = two_dots(nt, d_packed, qkv_w, d_upward, up_w, width)
+
+    q1_a_right, q2_a_left, d_hidden_far, d_hidden_near, g_u, g_a, context = tied(
+        q1_a_right, q2_a_left, d_hidden_far, d_hidden_near, g_u, g_a, context
+    )
+    d_hidden_came = flip(d_hidden_far, chips)
+    q1_u_left = inwards(g_u[2])
+    q2_a_right = over_middle(middle_share(g_a[3], q1_a_right))
+    q3_a_left = to_neighbour(neighbour_share(g_a[0], q2_a_left))
+    out_far, out_near = two_dots(nn, context, dense_w, active, down_w, width)
+    own_down = jnp.concatenate([added(*both) for both in zip(g_w[:2], (q2_w_left, q2_w_right))], axis=1)
+    grad_down_w = lax.dynamic_slice_in_dim(
+        own_down, (z % 2) * ff_block, ff_block, 0
+    ) + jnp.concatenate([q3_w_left, q3_w_right], axis=1).astype(F32)
+
+    q1_u_left, q2_a_right, q3_a_left, d_hidden_came, out_far, out_near, g_u, g_a = tied(
+        q1_u_left, q2_a_right, q3_a_left, d_hidden_came, out_far, out_near, g_u, g_a
+    )
+    out_came = flip(out_far, chips)
+    corner_a, corner_b = corners(where, d_hidden_near, d_hidden_came)
+    extra_y, extra_x = flip(corner_a, 1), flip(corner_b, 2)
+    for_x, for_y = sides(where, d_hidden_near, d_hidden_came, extra_y, extra_x)
+    d_hidden_last = flip(for_x, 1), flip(for_y, 2)
+    q1_u_right = inwards(g_u[3])
+    q2_u_left = over_middle(middle_share(g_u[2], q1_u_left))
+    q3_a_right = to_neighbour(neighbour_share(g_a[1], q2_a_right))
+
+    q1_u_right, q2_u_left, q3_a_right, d_hidden_last, out_came, g_u, q3_a_left = tied(
+        q1_u_right, q2_u_left, q3_a_right, d_hidden_last, out_came, g_u, q3_a_left
+    )
+    corner_a, corner_b = corners(where, out_near, out_came)
+    extra_y, extra_x = flip(corner_a, 1), flip(corner_b, 2)
+    for_x, for_y = sides(where, out_near, out_came, extra_y, extra_x)
+    out_last = flip(for_x, 1), flip(for_y, 2)
+    q2_u_right = over_middle(middle_share(g_u[3], q1_u_right))
+    q3_u_left = to_neighbour(neighbour_share(g_u[0], q2_u_left))
+    grad_tokens, gain_sum, shift_sum = norm_back(
+        where,
+        d_hidden_near,
+        d_hidden_came,
+        *d_hidden_last,
+        tokens,
+        cotangent,
+        gain.reshape(1, -1),
+    )
+    keep, send, grad_dense_w = finish(
+        where, chips, wide, g_a[0], g_a[1], q2_a_left, q2_a_right, q3_a_left, q3_a_right
+    )
+    blocks = deal_second(where, keep, flip(send, chips))
+
+    q2_u_right, q3_u_left, out_last, blocks, grad_tokens, gain_sum, g_u = tied(
+        q2_u_right, q3_u_left, out_last, blocks, grad_tokens, gain_sum, g_u
+    )
+    q3_u_right = to_neighbour(neighbour_share(g_u[1], q2_u_right))
+    blocks = [blocks[0]] + [flip(blocks[r], r) for r in range(1, chips)]
+    output = added(out_near[:row_count], out_came[:row_count], *out_last)
+    output = (inputs_f + output + out_bias).astype(BF16)
+
+    q3_u_right, blocks = tied(q3_u_right, blocks)
+    keep, send = finish(
+        where,
+        chips,
+        planes * ff_block,
+        g_u[0],
+        g_u[1],
+        q2_u_left,
+        q2_u_right,
+        q3_u_left,
+        q3_u_right,
+    )
+    grad_up_w = back(where, deal_over_chips(keep, send), planes)
+    grad_qkv_w = back(where, blocks, 3 * planes)
+
+    mine = jnp.arange(mates) == m
+    packed_sum = jnp.sum(d_packed.astype(F32), axis=0).reshape(3, planes, 1, HEAD_DIM)
+    packed_sum = jnp.where(mine[None, None, :, None], packed_sum, 0.0)
+    upward_sum = upward_sum.reshape(planes, 1, ff_block)
+    upward_sum = jnp.where(mine[None, :, None], upward_sum, 0.0)
+    sums = jnp.concatenate(
+        [
+            gain_sum.reshape(owners, -1),
+            shift_sum.reshape(owners, -1),
+            jnp.sum(cotangent.astype(F32), axis=0).reshape(owners, -1),
+            packed_sum.reshape(owners, -1),
+            upward_sum.reshape(owners, -1),
+        ],
+        axis=1,
+    )
+    total = lax.dynamic_index_in_dim(over_mates(over_planes(sums)), rank, 0, keepdims=False)
+    grad_gain, grad_shift, grad_out_b, grad_packed_b, grad_up_b = jnp.split(
+        total,
+        [
+            sizes[0],
+            sizes[0] + sizes[1],
+            sizes[0] + sizes[1] + sizes[3],
+            sizes[0] + sizes[1] + sizes[3] + sizes[2],
+        ],
+    )
+
+    return (
+        output,
+        grad_tokens,
+        grad_gain,
+        grad_shift,
+        grad_qkv_w,
+        grad_packed_b,
+        grad_dense_w,
+        grad_out_b,
+        grad_up_w,
+        grad_up_b,
+        grad_down_w,
+        grad_out_b,
+    )
+
+
 def solution(mesh):
+    planes, mates = mesh.shape["rep"] // CORES, CORES * mesh.shape["shard"]
+    rows, vector = P(AXES, None), P(AXES)
+
+    def layer(*arrays):
+        width = arrays[0].shape[1]
+        if mesh.shape["shard"] == 4 and planes * mates * HEAD_DIM == width:
+            return by_planes(planes, mates, *arrays)
+        return gathered_whole(*arrays)
+
     return jax.shard_map(
-        on_device,
+        layer,
         mesh=mesh,
         in_specs=(
-            P(("rep", "shard"), None),
-            P(("rep", "shard"), None),
-            P(("rep", "shard")),
-            P(("rep", "shard")),
-            P(("rep", "shard"), None),
-            P(("rep", "shard")),
-            P(("rep", "shard"), None),
-            P(("rep", "shard")),
-            P(("rep", "shard"), None),
-            P(("rep", "shard")),
-            P(("rep", "shard"), None),
-            P(("rep", "shard")),
-            P(("rep", "shard"), None),
+            rows, rows, vector, vector, rows, vector, rows, vector, rows, vector, rows, vector, rows,
         ),
         out_specs=(
-            P(("rep", "shard"), None),
-            P(("rep", "shard"), None),
-            P(("rep", "shard")),
-            P(("rep", "shard")),
-            P(("rep", "shard"), None),
-            P(("rep", "shard")),
-            P(("rep", "shard"), None),
-            P(("rep", "shard")),
-            P(("rep", "shard"), None),
-            P(("rep", "shard")),
-            P(("rep", "shard"), None),
-            P(("rep", "shard")),
+            rows, rows, vector, vector, rows, vector, rows, vector, rows, vector, rows, vector,
         ),
         check_vma=False,
     )

time: 4440 us -> 641 us (0.14)
  waiting for transfers between devices: 4040 us -> 197 us
  matrix products: 223 us -> 0 us
  Pallas kernels: 0 us -> 199 us
  blocking collectives: 110 us -> 0 us
  starting transfers between devices: 0.93 us -> 106 us
  other arithmetic: 15.8 us -> 63.6 us
    reduce_scatter x4 -> x0, waiting for transfers between devices: 3610 us -> none  [weight_grad(): lax.psum_scatter(lax.dot_general(left_side, incoming, (((0,), (0,)), ((),...]
    all_gather x4 -> x0, waiting for transfers between devices: 421 us -> none  [project(): whole = lax.all_gather(weight, ('rep', 'shard'), axis=0, tiled=True)]
    dot_general x18 -> x0, matrix products: 223 us -> none  [the longest x4 82.8 us: weight_grad(): lax.dot_general(left_side, incoming, (((0,), (0,)), ((), ())), preferred_...]
    pallas_call x0 -> x20, Pallas kernels: none -> 199 us  [the longest x18 159 us: kernel(): pl.pallas_call(body, grid_spec=pltpu.PrefetchScalarGridSpec(num_scalar_pr...]
    ppermute x0 -> x74, waiting for transfers between devices: none -> 197 us  [the longest x37 128 us: between(): lax.ppermute(value, AXES, [(p * mates + i, q * mates + i) for p, q in pai...]
    ppermute x0 -> x74, starting transfers between devices: none -> 106 us  [the longest x37 77.1 us: between(): lax.ppermute(value, AXES, [(p * mates + i, q * mates + i) for p, q in pai...]
    all_gather x1 -> x0, blocking collectives: 66.8 us -> none  [on_device(): lax.all_gather(up_bias, ('rep', 'shard'), axis=0, tiled=True)]
  transfers between devices with their start and end apart: 9 -> 74, of which waited for: 8 -> 29; matrix products, arithmetic and copies ran while one was open for 5% -> 11% of each run, Pallas kernels for 0% -> 31%
where the time goes in v2:
time: 641 us; the launch traced here: 630 us
  Pallas kernels  199 us (31%)
  waiting for transfers between devices  197 us (31%)
  starting transfers between devices  106 us (17%)
  other arithmetic  63.6 us (10%)
  local copies, waits for them, and re-layouts  61.7 us (10%)
    pallas_call x18, Pallas kernels, kernel(): pl.pallas_call(body, grid_spec=pltpu.PrefetchScalarGridSpec(num_scalar_pr...  159 us
    ppermute x37, waiting for transfers between devices, between(): lax.ppermute(value, AXES, [(p * mates + i, q * mates + i) for p, q in pai...  128 us
    ppermute x37, starting transfers between devices, between(): lax.ppermute(value, AXES, [(p * mates + i, q * mates + i) for p, q in pai...  77.1 us
    ppermute x37, waiting for transfers between devices, flip(): lax.ppermute(value, AXES, [(p * mates + i, p * mates + (i ^ r)) for p in...  69.4 us
    unnamed x202, local copies, waits for them, and re-layouts  40.4 us
    pallas_call x2, Pallas kernels, two_dots(): pl.pallas_call(functools.partial(two_dots_body, dot), grid=(steps,), in_s...  39.7 us
    ppermute x37, starting transfers between devices, flip(): lax.ppermute(value, AXES, [(p * mates + i, p * mates + (i ^ r)) for p in...  29 us
    convert_element_type x6, other arithmetic, middle_share(): return added(other, came).astype(BF16)  13 us
  transfers between devices with their start and end apart: 74, of which 29 were waited for; matrix products, arithmetic and copies ran while one was open for 11% of the time, Pallas kernels for 31%

profile of v2, /device:TPU:0, one launch (start us, length us, event | category | flops | bytes accessed | tf_op | source)
XLA Modules:
  0.0 630.3 jit_solution(12422770598075691361)
XLA Ops:
  35.4 6.9 %collective-permute-done.4.refs_1_ = bf16[2,64,1792]{2,1,0:T(8,128)(2,1)S(1)} collective-permute-done((bf16[2,64,1792]{2,1,0:T(8,128)(2,1)}, bf16[2,64,1792]{2,1,0:T(8,128)(2,1)S(1)}, u32[]{:S(2)}, u32[]{:S(2)}) %collective-permute-start.4) | collective-permute-done | bytes 458784 | tf_op jit(solution)/shard_map/ppermute | solution.py:969
  43.0 8.3 %collective-permute-done.5.refs_2_ = bf16[2,64,1792]{2,1,0:T(8,128)(2,1)S(1)} collective-permute-done((bf16[2,64,1792]{2,1,0:T(8,128)(2,1)}, bf16[2,64,1792]{2,1,0:T(8,128)(2,1)S(1)}, u32[]{:S(2)}, u32[]{:S(2)}) %collective-permute-start.5) | collective-permute-done | bytes 458784 | tf_op jit(solution)/shard_map/ppermute | solution.py:969
  71.5 19.1 %collective-permute-done.7 = bf16[512,1024]{1,0:T(8,128)(2,1)} collective-permute-done((bf16[512,1024]{1,0:T(8,128)(2,1)}, bf16[512,1024]{1,0:T(8,128)(2,1)}, u32[]{:S(2)}, u32[]{:S(2)}) %collective-permute-start.7) | collective-permute-done | bytes 1048608 | tf_op jit(solution)/shard_map/ppermute | solution.py:976
  102.4 22.5 %collective-permute-done.15 = bf16[512,1024]{1,0:T(8,128)(2,1)S(1)} collective-permute-done((bf16[512,1024]{1,0:T(8,128)(2,1)S(1)}, bf16[512,1024]{1,0:T(8,128)(2,1)S(1)}, u32[]{:S(2)}, u32[]{:S(2)}) %collective-permute-start.15) | collective-permute-done | bytes 1048608 | tf_op jit(solution)/shard_map/ppermute | solution.py:976
  130.3 5.9 fusion.10
  145.8 18.4 %collective-permute-done.22 = bf16[256,2048]{1,0:T(8,128)(2,1)S(1)} collective-permute-done((bf16[256,2048]{1,0:T(8,128)(2,1)S(1)}, bf16[256,2048]{1,0:T(8,128)(2,1)S(1)}, u32[]{:S(2)}, u32[]{:S(2)}) %collective-permute-start.22) | collective-permute-done | bytes 1048608 | tf_op jit(solution)/shard_map/ppermute | solution.py:969
  175.5 22.6 %collective-permute-done.24.end_right = bf16[1024,512]{1,0:T(8,128)(2,1)S(1)} collective-permute-done((bf16[1024,512]{1,0:T(8,128)(2,1)S(1)}, bf16[1024,512]{1,0:T(8,128)(2,1)S(1)}, u32[]{:S(2)}, u32[]{:S(2)}) %collective-permute-start.24) | collective-permute-done | bytes 1048608 | tf_op jit(solution)/shard_map/ppermute | solution.py:976
  201.2 32.2 %shard_map.223 = (bf16[2048,1024]{1,0:T(8,128)(2,1)}, bf16[2048,1024]{1,0:T(8,128)(2,1)}, bf16[2048,1024]{1,0:T(8,128)(2,1)}, bf16[512,1024]{1,0:T(8,128)(2,1)S(...) custom-call(s32[5]{0:T(128)S(1)} %stack.34.where, ...), custom_call_target="tpu_custom_call" | custom-call | flops 17179869184 | bytes 33554432 | tf_op jit(solution)/shard_map/pallas_call | solution.py:259
  240.9 7.5 %collective-permute-start.31 = (bf16[512,1024]{1,0:T(8,128)(2,1)}, bf16[512,1024]{1,0:T(8,128)(2,1)}, u32[]{:S(2)}, u32[]{:S(2)}) collective-permute-start(bf16[512,1024]{1,0:T(8,128)(2,1)} %get-tuple-element.264), channel_id=1, source_target_pairs={{0,8},{1,9},{2,10},{3,11},{4,12},{5,13},{6,14},{7,15},{24,16},{25,... | collective-permute-start | bytes 3145736 | tf_op jit(solution)/shard_map/ppermute | solution.py:976
  248.5 18.5 %collective-permute-done.29.refs_6_ = bf16[1024,512]{1,0:T(8,128)(2,1)} collective-permute-done((bf16[1024,512]{1,0:T(8,128)(2,1)}, bf16[1024,512]{1,0:T(8,128)(2,1)}, u32[]{:S(2)}, u32[]{:S(2)}) %collective-permute-start.29) | collective-permute-done | bytes 1048608 | tf_op jit(solution)/shard_map/ppermute | solution.py:976
  273.2 7.2 %collective-permute-start.33 = (bf16[512,1024]{1,0:T(8,128)(2,1)S(1)}, bf16[512,1024]{1,0:T(8,128)(2,1)S(1)}, u32[]{:S(2)}, u32[]{:S(2)}) collective-permute-start(bf16[512,1024]{1,0:T(8,128)(2,1)S(1)} %copy-done.22), channel_id=1, source_target_pairs={{0,8},{1,9},{2,10},{3,11},{4,12},{5,13},{6,14},{7,15},{24,16},{25,... | collective-permute-start | bytes 3145736 | tf_op jit(solution)/shard_map/ppermute | solution.py:976
  280.4 32.7 %shard_map.224 = (bf16[1024,256]{1,0:T(8,128)(2,1)S(1)}, bf16[1024,768]{1,0:T(8,128)(2,1)}, bf16[1024,512]{1,0:T(8,128)(2,1)S(1)}, bf16[1024,512]{1,0:T(8,128)(2...) custom-call(s32[5]{0:T(128)S(1)} %stack.34.where, ...), custom_call_target="tpu_custom_call" | custom-call | flops 17999998976 | bytes 20971520 | tf_op jit(solution)/shard_map/pallas_call | solution.py:259
  323.4 32.0 %shard_map.225 = (bf16[1024,256]{1,0:T(8,128)(2,1)S(1)}, bf16[1024,768]{1,0:T(8,128)(2,1)}, bf16[1024,512]{1,0:T(8,128)(2,1)S(1)}, bf16[1024,512]{1,0:T(8,128)(2...) custom-call(s32[5]{0:T(128)S(1)} %stack.34.where, bf16[2048,2048]{1,0:T(8,128)(2,1)} %copy-done.78, ...), custom_call_target="tpu_custom_call" | custom-call | flops 17999998976 | bytes 20971520 | tf_op jit(solution)/shard_map/pallas_call | solution.py:259
  367.6 27.9 %shard_map.226 = (bf16[2048,1024]{1,0:T(8,128)(2,1)}, f32[1,1024]{1,0:T(1,128)S(1)}, bf16[1024,2048]{1,0:T(8,128)(2,1)}, bf16[1024,512]{1,0:T(8,128)(2,1)S(1)}, ...) custom-call(s32[5]{0:T(128)S(1)} %stack.34.where, ...), custom_call_target="tpu_custom_call" | custom-call | flops 17179869184 | bytes 33554432 | tf_op jit(solution)/shard_map/pallas_call | solution.py:259
  399.5 6.4 %collective-permute-start.40 = (bf16[1024,512]{1,0:T(8,128)(2,1)S(1)}, bf16[1024,512]{1,0:T(8,128)(2,1)S(1)}, u32[]{:S(2)}, u32[]{:S(2)}) collective-permute-start(bf16[1024,512]{1,0:T(8,128)(2,1)S(1)} %get-tuple-element.332), channel_id=1, source_target_pairs={{0,8},{1,9},{2,10},{3,11},{4,12},{5,13},{6,14},{7,15},{24,16},{25,... | collective-permute-start | bytes 3145736 | tf_op jit(solution)/shard_map/ppermute | solution.py:976
  405.9 22.5 %shard_map.227 = (bf16[1024,2048]{1,0:T(8,128)(2,1)}, bf16[1024,2048]{1,0:T(8,128)(2,1)}) custom-call(bf16[2048,768]{1,0:T(8,128)(2,1)S(1)} %constant_dynamic-update-slice_fusion.8.a, bf16[2048,768]{1,0:T(8,128)(2,1)} %get-tuple-element.286.refs_2_.aw, bf16[2048,1024]{1,0:T(8,128)(2,1)} %get-tuple-element.319.b, bf16[2048,1024]{1,0:T(8,128)(2,1)} %get-tuple-element.320.bw), custom_call_target="tpu_custom_call" | custom-call | flops 15032385536 | bytes 23068672 | tf_op jit(solution)/shard_map/pallas_call | solution.py:653
  434.3 17.2 %shard_map.228 = (bf16[1024,2048]{1,0:T(8,128)(2,1)}, bf16[1024,2048]{1,0:T(8,128)(2,1)}) custom-call(bf16[2048,256]{1,0:T(8,128)(2,1)S(1)} %copy-done.24, bf16[256,2048]{1,0:T(8,128)(2,1)S(1)} %copy-done.50, bf16[2048,1024]{1,0:T(8,128)(2,1)} %get-tuple-element.338.b, bf16[1024,2048]{1,0:T(8,128)(2,1)} %get-tuple-element.339.bw), custom_call_target="tpu_custom_call" | custom-call | flops 10737418240 | bytes 18874368 | tf_op jit(solution)/shard_map/pallas_call | solution.py:653
  451.5 16.6 %collective-permute-done.44.left = bf16[512,512]{1,0:T(8,128)(2,1)S(1)} collective-permute-done((bf16[512,512]{1,0:T(8,128)(2,1)S(1)}, bf16[512,512]{1,0:T(8,128)(2,1)S(1)}, u32[]{:S(2)}, u32[]{:S(2)}) %collective-permute-start.44) | collective-permute-done | bytes 524320 | tf_op jit(solution)/shard_map/ppermute | solution.py:976
  478.7 5.9 collective-permute-done.49.extra_x
  495.5 16.1 %collective-permute-done.46 = bf16[1024,512]{1,0:T(8,128)(2,1)S(1)} collective-permute-done((bf16[1024,512]{1,0:T(8,128)(2,1)}, bf16[1024,512]{1,0:T(8,128)(2,1)S(1)}, u32[]{:S(2)}, u32[]{:S(2)}) %collective-permute-start.46) | collective-permute-done | bytes 1048608 | tf_op jit(solution)/shard_map/ppermute | solution.py:976
  511.5 5.4 collective-permute-done.51.by_x
  528.7 6.3 %collective-permute-done.56.extra_x = bf16[128,2048]{1,0:T(8,128)(2,1)} collective-permute-done((bf16[128,2048]{1,0:T(8,128)(2,1)}, bf16[128,2048]{1,0:T(8,128)(2,1)}, u32[]{:S(2)}, u32[]{:S(2)}) %collective-permute-start.56) | collective-permute-done | bytes 524320 | tf_op jit(solution)/shard_map/ppermute | solution.py:969
  567.7 4.9 shard_map.235
  621.6 5.7 collective-permute-done.72.refs_2_
  (453 shorter events, 259.2 us)
Async XLA Ops:
  18.7 40.8 %collective-permute-start.2 = (bf16[256,2048]{1,0:T(8,128)(2,1)}, bf16[256,2048]{1,0:T(8,128)(2,1)}, u32[]{:S(2)}, u32[]{:S(2)}) collective-permute-start(bf16[256,2048]{1,0:T(8,128)(2,1)} %param.23), channel_id=1, source_target_pairs={{0,8},{1,9},{2,10},{3,11},{4,12},{5,13},{6,14},{7,15},{8,0},{9,1},... | collective-permute-start | bytes 3145736 | tf_op jit(solution)/shard_map/ppermute | solution.py:976
  59.5 31.1 %collective-permute-start.10 = (bf16[256,2048]{1,0:T(8,128)(2,1)S(1)}, bf16[256,2048]{1,0:T(8,128)(2,1)}, u32[]{:S(2)}, u32[]{:S(2)}) collective-permute-start(bf16[256,2048]{1,0:T(8,128)(2,1)S(1)} %copy-done.3), channel_id=1, source_target_pairs={{0,2},{1,3},{2,0},{3,1},{4,6},{5,7},{6,4},{7,5},{8,10},{9,11},{10,... | collective-permute-start | bytes 3145736 | tf_op jit(solution)/shard_map/ppermute | solution.py:969
  60.0 30.6 %collective-permute-start.9 = (bf16[256,2048]{1,0:T(8,128)(2,1)S(1)}, bf16[256,2048]{1,0:T(8,128)(2,1)}, u32[]{:S(2)}, u32[]{:S(2)}) collective-permute-start(bf16[256,2048]{1,0:T(8,128)(2,1)S(1)} %copy-done.3), channel_id=1, source_target_pairs={{0,1},{1,0},{2,3},{3,2},{4,5},{5,4},{6,7},{7,6},{8,9},{9,8},{10,11... | collective-permute-start | bytes 3145736 | tf_op jit(solution)/shard_map/ppermute | solution.py:969
  92.3 34.3 %collective-permute-start.18 = (bf16[768,2048]{1,0:T(8,128)(2,1)S(1)}, bf16[768,2048]{1,0:T(8,128)(2,1)S(1)}, u32[]{:S(2)}, u32[]{:S(2)}) collective-permute-start(bf16[768,2048]{1,0:T(8,128)(2,1)S(1)} %pad_maximum_fusion), channel_id=1, source_target_pairs={{0,4},{1,5},{2,6},{3,7},{4,0},{5,1},{6,2},{7,3},{8,12},{9,13},{10,... | collective-permute-start | bytes 9437192 | tf_op jit(solution)/shard_map/ppermute | solution.py:969
  128.7 39.1 %collective-permute-start.23 = (bf16[768,2048]{1,0:T(8,128)(2,1)}, bf16[768,2048]{1,0:T(8,128)(2,1)}, u32[]{:S(2)}, u32[]{:S(2)}) collective-permute-start(bf16[768,2048]{1,0:T(8,128)(2,1)} %pad_maximum_fusion.1), channel_id=1, source_target_pairs={{0,4},{1,5},{2,6},{3,7},{4,0},{5,1},{6,2},{7,3},{8,12},{9,13},{10,... | collective-permute-start | bytes 9437192 | tf_op jit(solution)/shard_map/ppermute | solution.py:969
  198.2 37.2 %collective-permute-start.28 = (bf16[1024,512]{1,0:T(8,128)(2,1)S(1)}, bf16[1024,512]{1,0:T(8,128)(2,1)}, u32[]{:S(2)}, u32[]{:S(2)}) collective-permute-start(bf16[1024,512]{1,0:T(8,128)(2,1)S(1)} %slice.184), channel_id=1, source_target_pairs={{8,16},{9,17},{10,18},{11,19},{12,20},{13,21},{14,22},{15,23},{16,... | collective-permute-start | bytes 3145736 | tf_op jit(solution)/shard_map/ppermute | solution.py:976
  199.9 35.6 %collective-permute-start.27 = (bf16[1024,512]{1,0:T(8,128)(2,1)S(1)}, bf16[1024,512]{1,0:T(8,128)(2,1)S(1)}, u32[]{:S(2)}, u32[]{:S(2)}) collective-permute-start(bf16[1024,512]{1,0:T(8,128)(2,1)S(1)} %collective-permute-done.25.refs_3_), channel_id=1, source_target_pairs={{8,0},{9,1},{10,2},{11,3},{12,4},{13,5},{14,6},{15,7},{16,24},{17,... | collective-permute-start | bytes 3145736 | tf_op jit(solution)/shard_map/ppermute | solution.py:976
  271.1 47.1 %collective-permute-start.34 = (bf16[512,1024]{1,0:T(8,128)(2,1)S(1)}, bf16[512,1024]{1,0:T(8,128)(2,1)S(1)}, u32[]{:S(2)}, u32[]{:S(2)}) collective-permute-start(bf16[512,1024]{1,0:T(8,128)(2,1)S(1)} %add_convert_fusion.5), channel_id=1, source_target_pairs={{8,16},{9,17},{10,18},{11,19},{12,20},{13,21},{14,22},{15,23},{16,... | collective-permute-start | bytes 3145736 | tf_op jit(solution)/shard_map/ppermute | solution.py:976
  271.9 46.4 %collective-permute-start.32 = (bf16[512,1024]{1,0:T(8,128)(2,1)}, bf16[512,1024]{1,0:T(8,128)(2,1)S(1)}, u32[]{:S(2)}, u32[]{:S(2)}) collective-permute-start(bf16[512,1024]{1,0:T(8,128)(2,1)} %collective-permute-done.8.middle_left), channel_id=1, source_target_pairs={{8,0},{9,1},{10,2},{11,3},{12,4},{13,5},{14,6},{15,7},{16,24},{17,... | collective-permute-start | bytes 3145736 | tf_op jit(solution)/shard_map/ppermute | solution.py:976
  273.2 45.1 %collective-permute-start.33 = (bf16[512,1024]{1,0:T(8,128)(2,1)S(1)}, bf16[512,1024]{1,0:T(8,128)(2,1)S(1)}, u32[]{:S(2)}, u32[]{:S(2)}) collective-permute-start(bf16[512,1024]{1,0:T(8,128)(2,1)S(1)} %copy-done.22), channel_id=1, source_target_pairs={{0,8},{1,9},{2,10},{3,11},{4,12},{5,13},{6,14},{7,15},{24,16},{25,... | collective-permute-start | bytes 3145736 | tf_op jit(solution)/shard_map/ppermute | solution.py:976
  319.7 39.1 %collective-permute-start.37 = (bf16[256,1024]{1,0:T(8,128)(2,1)}, bf16[256,1024]{1,0:T(8,128)(2,1)}, u32[]{:S(2)}, u32[]{:S(2)}) collective-permute-start(bf16[256,1024]{1,0:T(8,128)(2,1)} %select_convert_fusion.5), channel_id=1, source_target_pairs={{0,8},{1,9},{2,10},{3,11},{4,12},{5,13},{6,14},{7,15},{8,0},{9,1},... | collective-permute-start | bytes 1572872 | tf_op jit(solution)/shard_map/ppermute | solution.py:976
  321.1 37.7 %collective-permute-start.36 = (bf16[512,1024]{1,0:T(8,128)(2,1)}, bf16[512,1024]{1,0:T(8,128)(2,1)S(1)}, u32[]{:S(2)}, u32[]{:S(2)}) collective-permute-start(bf16[512,1024]{1,0:T(8,128)(2,1)} %add_convert_fusion.4), channel_id=1, source_target_pairs={{8,16},{9,17},{10,18},{11,19},{12,20},{13,21},{14,22},{15,23},{16,... | collective-permute-start | bytes 3145736 | tf_op jit(solution)/shard_map/ppermute | solution.py:976
  321.9 37.0 %collective-permute-start.35 = (bf16[512,1024]{1,0:T(8,128)(2,1)}, bf16[512,1024]{1,0:T(8,128)(2,1)S(1)}, u32[]{:S(2)}, u32[]{:S(2)}) collective-permute-start(bf16[512,1024]{1,0:T(8,128)(2,1)} %collective-permute-done.30.middle_right), channel_id=1, source_target_pairs={{8,0},{9,1},{10,2},{11,3},{12,4},{13,5},{14,6},{15,7},{16,24},{17,... | collective-permute-start | bytes 3145736 | tf_op jit(solution)/shard_map/ppermute | solution.py:976
  360.5 35.1 %collective-permute-start.39 = (bf16[256,1024]{1,0:T(8,128)(2,1)}, bf16[256,1024]{1,0:T(8,128)(2,1)}, u32[]{:S(2)}, u32[]{:S(2)}) collective-permute-start(bf16[256,1024]{1,0:T(8,128)(2,1)} %select_convert_fusion.4), channel_id=1, source_target_pairs={{0,8},{1,9},{2,10},{3,11},{4,12},{5,13},{6,14},{7,15},{8,0},{9,1},... | collective-permute-start | bytes 1572872 | tf_op jit(solution)/shard_map/ppermute | solution.py:976
  364.7 30.9 %collective-permute-start.38 = (bf16[1024,512]{1,0:T(8,128)(2,1)S(1)}, bf16[1024,512]{1,0:T(8,128)(2,1)}, u32[]{:S(2)}, u32[]{:S(2)}) collective-permute-start(bf16[1024,512]{1,0:T(8,128)(2,1)S(1)} %get-tuple-element.315), channel_id=1, source_target_pairs={{0,8},{1,9},{2,10},{3,11},{4,12},{5,13},{6,14},{7,15},{24,16},{25,... | collective-permute-start | bytes 3145736 | tf_op jit(solution)/shard_map/ppermute | solution.py:976
  428.5 39.6 %collective-permute-start.45 = (bf16[1024,2048]{1,0:T(8,128)(2,1)}, bf16[1024,2048]{1,0:T(8,128)(2,1)}, u32[]{:S(2)}, u32[]{:S(2)}) collective-permute-start(bf16[1024,2048]{1,0:T(8,128)(2,1)} %get-tuple-element.336), channel_id=1, source_target_pairs={{0,4},{1,5},{2,6},{3,7},{4,0},{5,1},{6,2},{7,3},{8,12},{9,13},{10,... | collective-permute-start | bytes 12582920 | tf_op jit(solution)/shard_map/ppermute | solution.py:969
  429.8 38.3 %collective-permute-start.43 = (bf16[1024,512]{1,0:T(8,128)(2,1)}, bf16[1024,512]{1,0:T(8,128)(2,1)S(1)}, u32[]{:S(2)}, u32[]{:S(2)}) collective-permute-start(bf16[1024,512]{1,0:T(8,128)(2,1)} %add_convert_fusion.2), channel_id=1, source_target_pairs={{8,16},{9,17},{10,18},{11,19},{12,20},{13,21},{14,22},{15,23},{16,... | collective-permute-start | bytes 3145736 | tf_op jit(solution)/shard_map/ppermute | solution.py:976
  430.5 37.5 %collective-permute-start.42 = (bf16[1024,512]{1,0:T(8,128)(2,1)}, bf16[1024,512]{1,0:T(8,128)(2,1)S(1)}, u32[]{:S(2)}, u32[]{:S(2)}) collective-permute-start(bf16[1024,512]{1,0:T(8,128)(2,1)} %get-tuple-element.348), channel_id=1, source_target_pairs={{0,8},{1,9},{2,10},{3,11},{4,12},{5,13},{6,14},{7,15},{24,16},{25,... | collective-permute-start | bytes 3145736 | tf_op jit(solution)/shard_map/ppermute | solution.py:976
  434.2 33.9 %collective-permute-start.44 = (bf16[512,512]{1,0:T(8,128)(2,1)S(1)}, bf16[512,512]{1,0:T(8,128)(2,1)S(1)}, u32[]{:S(2)}, u32[]{:S(2)}) collective-permute-start(bf16[512,512]{1,0:T(8,128)(2,1)S(1)} %select_convert_fusion.3), channel_id=1, source_target_pairs={{0,8},{1,9},{2,10},{3,11},{4,12},{5,13},{6,14},{7,15},{8,0},{9,1},... | collective-permute-start | bytes 1572872 | tf_op jit(solution)/shard_map/ppermute | solution.py:976
  468.1 51.8 %collective-permute-start.53 = (bf16[1024,2048]{1,0:T(8,128)(2,1)}, bf16[1024,2048]{1,0:T(8,128)(2,1)}, u32[]{:S(2)}, u32[]{:S(2)}) collective-permute-start(bf16[1024,2048]{1,0:T(8,128)(2,1)} %get-tuple-element.358), channel_id=1, source_target_pairs={{0,4},{1,5},{2,6},{3,7},{4,0},{5,1},{6,2},{7,3},{8,12},{9,13},{10,... | collective-permute-start | bytes 12582920 | tf_op jit(solution)/shard_map/ppermute | solution.py:969
  526.9 50.6 %collective-permute-start.54 = (bf16[1024,512]{1,0:T(8,128)(2,1)}, bf16[1024,512]{1,0:T(8,128)(2,1)}, u32[]{:S(2)}, u32[]{:S(2)}) collective-permute-start(bf16[1024,512]{1,0:T(8,128)(2,1)} %add_convert_fusion), channel_id=1, source_target_pairs={{8,16},{9,17},{10,18},{11,19},{12,20},{13,21},{14,22},{15,23},{16,... | collective-permute-start | bytes 3145736 | tf_op jit(solution)/shard_map/ppermute | solution.py:976
  540.2 37.4 %collective-permute-start.58 = (bf16[256,2048]{1,0:T(8,128)(2,1)}, bf16[256,2048]{1,0:T(8,128)(2,1)}, u32[]{:S(2)}, u32[]{:S(2)}) collective-permute-start(bf16[256,2048]{1,0:T(8,128)(2,1)} %get-tuple-element.369), channel_id=1, source_target_pairs={{0,1},{1,0},{2,3},{3,2},{4,5},{5,4},{6,7},{7,6},{8,9},{9,8},{10,11... | collective-permute-start | bytes 3145736 | tf_op jit(solution)/shard_map/ppermute | solution.py:969
  540.9 36.6 %collective-permute-start.59 = (bf16[256,2048]{1,0:T(8,128)(2,1)}, bf16[256,2048]{1,0:T(8,128)(2,1)}, u32[]{:S(2)}, u32[]{:S(2)}) collective-permute-start(bf16[256,2048]{1,0:T(8,128)(2,1)} %get-tuple-element.370), channel_id=1, source_target_pairs={{0,2},{1,3},{2,0},{3,1},{4,6},{5,7},{6,4},{7,5},{8,10},{9,11},{10,... | collective-permute-start | bytes 3145736 | tf_op jit(solution)/shard_map/ppermute | solution.py:969
  546.8 30.8 %collective-permute-start.55 = (bf16[512,512]{1,0:T(8,128)(2,1)}, bf16[512,512]{1,0:T(8,128)(2,1)}, u32[]{:S(2)}, u32[]{:S(2)}) collective-permute-start(bf16[512,512]{1,0:T(8,128)(2,1)} %select_convert_fusion.1), channel_id=1, source_target_pairs={{0,8},{1,9},{2,10},{3,11},{4,12},{5,13},{6,14},{7,15},{8,0},{9,1},... | collective-permute-start | bytes 1572872 | tf_op jit(solution)/shard_map/ppermute | solution.py:976
  (146 other events, 1991.2 us)

commit v3 on v2

--- a/solution.py
+++ b/solution.py
@@ -227,9 +227,10 @@
 
 
 MIB = 1024 * 1024
-
-
-def params(vmem=48):
+VMEM = 60
+
+
+def params(vmem=VMEM):
     return pltpu.CompilerParams(
         dimension_semantics=("arbitrary",), vmem_limit_bytes=vmem * MIB
     )
@@ -255,7 +256,7 @@
 ANYWHERE = pl.BlockSpec(memory_space=pl.ANY)
 
 
-def kernel(body, scalars, operands, in_specs, out_specs, out_shape, grid=(1,), scratch=(), work=(0, 0)):
+def kernel(body, scalars, operands, in_specs, out_specs, out_shape, grid=(1,), scratch=(), work=(0, 0), vmem=16):
     return pl.pallas_call(
         body,
         grid_spec=pltpu.PrefetchScalarGridSpec(
@@ -266,7 +267,7 @@
             scratch_shapes=list(scratch),
         ),
         out_shape=out_shape,
-        compiler_params=params(),
+        compiler_params=params(vmem),
         cost_estimate=cost(*work),
     )(scalars, *operands)
 
@@ -303,73 +304,67 @@
         pltpu.make_async_copy(source, target, sems.at[at]).wait()
 
 
-def copy_either(where, common, if_middle, if_end, sems):
+def places(where):
+    half, odd = where[HALF], where[ODD]
+    return (
+        (odd, 2 * half + odd),
+        (1 - odd, 2 * half + 1 - odd),
+        (2 + half, 2 - half),
+        (3 - half, 3 - 3 * half),
+    )
+
+
+def copy_pieces(where, pieces, of, sems):
+    own, neighbour, other_middle, other_end = places(where)
+    common = of(pieces[0], *own) + of(pieces[1], *neighbour)
+
     @pl.when(where[MIDDLE] == 1)
     def _():
-        copy_all(common + if_middle, sems)
+        copy_all(common + of(pieces[2], *other_middle) + of(pieces[3], *other_end), sems)
 
     @pl.when(where[MIDDLE] == 0)
     def _():
-        copy_all(common + if_end, sems)
+        copy_all(common + of(pieces[4], *other_middle) + of(pieces[5], *other_end), sems)
 
 
 def multiple(value, size):
     return pl.multiple_of(value * size, size)
 
 
-def attention_body(parts, merge, where, *refs):
+def attention_body(parts, run, merge, where, *refs):
+    hidden, cot, *refs = refs
+    weights, refs = refs[: 6 if merge else 2], refs[6 if merge else 2 :]
+    (bias, cosine, sine_a, sine_b, first), refs = refs[:5], refs[5:]
+    prior, refs = ((), refs) if merge else (refs[:4], refs[6:])
+    (context, d_packed, *grads), refs = refs[:6], refs[6:]
     if merge:
-        hidden, cot, pair, middle_left, middle_right, end_left, end_right = refs[:7]
-        bias, cosine, sine_a, sine_b, first = refs[7:12]
-        prior = ()
-        context, d_packed, *grads = refs[12:18]
-        qkv_w, dense_w, sum_qkv, sum_dense, sems = refs[18:]
+        qkv_w, dense_w, sum_qkv, sum_dense, sems = refs
     else:
-        hidden, cot, qkv_w, dense_w, bias, cosine, sine_a, sine_b, first = refs[:9]
-        prior = refs[9:13]
-        context, d_packed, *grads = refs[13:19]
-        sum_qkv, sum_dense = refs[19:]
+        (qkv_w, dense_w), (sum_qkv, sum_dense) = weights, refs
     step = pl.program_id(0)
-    run, wide = hidden.shape[0], dense_w.shape[0]
+    wide = dense_w.shape[0]
     scaling = 1.0 / math.sqrt(HEAD_DIM)
     block, own = sum_qkv.shape[0] // 4, wide // 4
     across = dense_w.shape[1] // parts
-    left_columns = grads[0].shape[1]
 
     if merge:
 
         @pl.when(step == 0)
         def _():
-            half = where[HALF]
-
-            def dense_copies(source, side, first_column):
+            def of(piece, place, plane):
                 return [
+                    (piece.at[:, : 3 * wide], qkv_w.at[pl.ds(multiple(place, block), block)])
+                ] + [
                     (
-                        source.at[
-                            i * block + j * own : i * block + (j + 1) * own,
-                            first_column : first_column + across,
-                        ],
+                        piece.at[j * own : (j + 1) * own, 3 * wide :],
                         dense_w.at[
-                            pl.ds(multiple(2 * side + i, own), own), j * across : (j + 1) * across
+                            pl.ds(multiple(plane, own), own), j * across : (j + 1) * across
                         ],
                     )
-                    for i in range(2)
                     for j in range(parts)
                 ]
 
-            rows, rest = 2 * block, 3 * wide - left_columns
-
-            def others(left, right):
-                return [
-                    (left, qkv_w.at[rows:, :left_columns]),
-                    (right.at[:, :rest], qkv_w.at[rows:, left_columns:]),
-                ] + dense_copies(right, 1 - half, rest)
-
-            common = [(pair.at[:, : 3 * wide], qkv_w.at[:rows])]
-            common += dense_copies(pair, half, 3 * wide)
-            copy_either(
-                where, common, others(middle_left, middle_right), others(end_left, end_right), sems
-            )
+            copy_pieces(where, weights, of, sems)
 
     c = jnp.tile(cosine[...], (1, wide // 128))
     sa = jnp.tile(sine_a[...], (1, wide // 128))
@@ -387,26 +382,31 @@
     d_context = nt(cot[...], dense_w[...]).astype(BF16)
     at = lax.broadcasted_iota(jnp.int32, (run, run), 1)
     row = lax.broadcasted_iota(jnp.int32, (run, run), 0)
-    seen = (at >= first[:, :1]) & (at <= row)
-    out, d_q, d_k, d_v = [], [], [], []
-    for h in range(wide // HEAD_DIM):
-        part = slice(h * HEAD_DIM, (h + 1) * HEAD_DIM)
-        q, k, v, g = queries[:, part], keys[:, part], values[:, part], d_context[:, part]
-        scores = jnp.where(seen, nt(q, k), -1e30)
-        raised = jnp.exp(scores - jnp.max(scores, axis=1, keepdims=True))
-        probs = raised * (1.0 / jnp.sum(raised, axis=1, keepdims=True))
-        low = probs.astype(BF16)
-        o = nn(low, v)
-        out.append(o)
-        d_v.append(tn(low, g))
-        delta = jnp.sum(o * g.astype(F32), axis=1, keepdims=True)
-        d_scores = (probs * (nt(g, v) - delta)).astype(BF16)
-        d_q.append(nn(d_scores, k) * scaling)
-        d_k.append(tn(d_scores, q))
-    context[...] = jnp.concatenate(out, axis=1).astype(BF16)
-    d_packed[:, :wide] = turn(jnp.concatenate(d_q, axis=1), -1.0).astype(BF16)
-    d_packed[:, wide : 2 * wide] = turn(jnp.concatenate(d_k, axis=1), -1.0).astype(BF16)
-    d_packed[:, 2 * wide :] = jnp.concatenate(d_v, axis=1).astype(BF16)
+    all_out, all_q, all_k, all_v = [], [], [], []
+    for begin in range(0, hidden.shape[0], run):
+        rows = slice(begin, begin + run)
+        seen = (at >= first[rows, :1]) & (at <= row)
+        out, d_q, d_k, d_v = [], [], [], []
+        for h in range(wide // HEAD_DIM):
+            part = slice(h * HEAD_DIM, (h + 1) * HEAD_DIM)
+            q, k, v, g = (x[rows, part] for x in (queries, keys, values, d_context))
+            scores = jnp.where(seen, nt(q, k), -1e30)
+            raised = jnp.exp(scores - jnp.max(scores, axis=1, keepdims=True))
+            probs = raised * (1.0 / jnp.sum(raised, axis=1, keepdims=True))
+            low = probs.astype(BF16)
+            o = nn(low, v)
+            out.append(o)
+            d_v.append(tn(low, g))
+            delta = jnp.sum(o * g.astype(F32), axis=1, keepdims=True)
+            d_scores = (probs * (nt(g, v) - delta)).astype(BF16)
+            d_q.append(nn(d_scores, k) * scaling)
+            d_k.append(tn(d_scores, q))
+        for held, new in ((all_out, out), (all_q, d_q), (all_k, d_k), (all_v, d_v)):
+            held.append(jnp.concatenate(new, axis=1))
+    context[...] = jnp.concatenate(all_out, axis=0).astype(BF16)
+    d_packed[:, :wide] = turn(jnp.concatenate(all_q, axis=0), -1.0).astype(BF16)
+    d_packed[:, wide : 2 * wide] = turn(jnp.concatenate(all_k, axis=0), -1.0).astype(BF16)
+    d_packed[:, 2 * wide :] = jnp.concatenate(all_v, axis=0).astype(BF16)
 
     @pl.when(step == 0)
     def _():
@@ -418,107 +418,82 @@
 
     @pl.when(step == pl.num_programs(0) - 1)
     def _():
-        for pair_at in range(2):
-            for i in range(2):
-                half = where[HALF] if pair_at == 0 else 1 - where[HALF]
-                rows = slice(i * block, (i + 1) * block)
-                start = (2 * pair_at + i) * block
-                summed = sum_qkv[start : start + block]
-                beside = sum_dense[pl.ds(multiple(2 * half + i, own), own), :]
-                beside = jnp.concatenate(
-                    [beside[:, j * across : (j + 1) * across] for j in range(parts)], axis=0
-                )
-                first_half = summed[:, :left_columns]
-                second_half = jnp.concatenate([summed[:, left_columns:], beside], axis=1)
-                if prior:
-                    first_half += prior[2 * pair_at][rows].astype(F32)
-                    second_half += prior[2 * pair_at + 1][rows].astype(F32)
-                grads[2 * pair_at][rows] = first_half.astype(BF16)
-                grads[2 * pair_at + 1][rows] = second_half.astype(BF16)
-
-
-def attention(where, run, start, count, parts, hidden, cot, weights, streams, prior):
-    width = hidden.shape[1]
-    merge = len(weights) == 5
+        for at, (out, (place, plane)) in enumerate(zip(grads, places(where))):
+            summed = sum_qkv[pl.ds(multiple(place, block), block), :]
+            beside = sum_dense[pl.ds(multiple(plane, own), own), :]
+            beside = jnp.concatenate(
+                [beside[:, j * across : (j + 1) * across] for j in range(parts)], axis=0
+            )
+            total = jnp.concatenate([summed, beside], axis=1)
+            if prior:
+                total += prior[at][...].astype(F32)
+            out[...] = total.astype(BF16)
+
+
+def attention(where, run, parts, hidden, cot, weights, streams, prior, filled):
+    count, width = 2 * hidden.shape[0], hidden.shape[1]
+    merge = not prior
     bias = streams[0]
     wide = bias.shape[1] // 3
-    grad = shaped((width // 2, (3 * wide + width // parts) // 2))
-    sums = [pltpu.VMEM((width, 3 * wide), F32), pltpu.VMEM((wide, width), F32)]
+    rows = run
+    steps = count // rows // 2
+    start = 0 if merge else steps
+    grad = shaped((width // 4, 3 * wide + width // parts))
+
+    def rows_of_run(columns):
+        return pl.BlockSpec((rows, columns), lambda i, _: (i + start, 0))
+
     joined = [shaped((width, 3 * wide)), shaped((wide, width))] if merge else []
-    outs = kernel(
-        functools.partial(attention_body, parts, merge),
-        where,
-        [hidden, cot, *weights, *streams, *prior],
-        [rows_of(hidden, run, start), rows_of(cot, run, start)]
-        + ([ANYWHERE] * 5 if merge else [whole(array) for array in weights])
-        + [whole(bias)]
-        + [rows_of(array, run, start) for array in streams[1:]]
-        + [whole(array) for array in prior],
-        [
-            pl.BlockSpec((run, wide), lambda i, _: (i, 0)),
-            pl.BlockSpec((run, 3 * wide), lambda i, _: (i, 0)),
-        ]
-        + [fixed(grad.shape)] * 4
-        + [fixed(array.shape) for array in joined],
-        [shaped((count, wide)), shaped((count, 3 * wide))] + [grad] * 4 + joined,
-        grid=(count // run,),
-        scratch=sums + ([pltpu.SemaphoreType.DMA((3 + 4 * parts,))] if merge else []),
-        work=(18 * 10**9, 20 * MIB),
-    )
-    return outs[0], outs[1], outs[2:6], outs[6:]
+    operands = [hidden, cot, *weights, *streams, *prior, *filled]
+    first_filled = 1 + len(operands) - len(filled)
+    outs = pl.pallas_call(
+        functools.partial(attention_body, parts, run, merge),
+        grid_spec=pltpu.PrefetchScalarGridSpec(
+            num_scalar_prefetch=1,
+            grid=(steps,),
+            in_specs=[pl.BlockSpec((rows, width), lambda i, _: (i, 0))] * 2
+            + ([ANYWHERE] * 6 if merge else [whole(array) for array in weights])
+            + [whole(bias)]
+            + [rows_of_run(array.shape[1]) for array in streams[1:]]
+            + [whole(array) for array in prior]
+            + [ANYWHERE for _ in filled],
+            out_specs=[rows_of_run(wide), rows_of_run(3 * wide)]
+            + [fixed(grad.shape)] * 4
+            + [fixed(array.shape) for array in joined],
+            scratch_shapes=[pltpu.VMEM((width, 3 * wide), F32), pltpu.VMEM((wide, width), F32)]
+            + ([pltpu.SemaphoreType.DMA((4 * (1 + parts),))] if merge else []),
+        ),
+        out_shape=[shaped((count, wide)), shaped((count, 3 * wide))] + [grad] * 4 + joined,
+        input_output_aliases={first_filled + i: i for i in range(len(filled))},
+        compiler_params=params(),
+        cost_estimate=cost(18 * 10**9, 20 * MIB),
+    )(where, *operands)
+    return outs[:2], outs[2:6], outs[6:]
 
 
 GELU_A = math.sqrt(2.0 / math.pi)
 GELU_B = 0.044715
 
 
-def write_halves(where, total, grads, order):
-    rows, columns = grads[0].shape
-    for pair_at in range(2):
-        if order:
-            half = where[HALF] if pair_at == 0 else 1 - where[HALF]
-            part = pl.ds(multiple(half, rows), rows)
-        else:
-            part = slice(pair_at * rows, (pair_at + 1) * rows)
-        for side in range(2):
-            grads[2 * pair_at + side][...] = total[
-                part, side * columns : (side + 1) * columns
-            ].astype(BF16)
-
-
-def forward_body(
-    columns,
-    where,
-    hidden,
-    cot,
-    pair,
-    middle_left,
-    middle_right,
-    end_left,
-    end_right,
-    bias,
-    active,
-    slope,
-    up_w,
-    *rest,
-):
-    grads, total, sems = rest[:-2], rest[-2], rest[-1]
+def write_blocks(where, total, grads, by_plane):
+    size = grads[0].shape[0]
+    for out, (place, plane) in zip(grads, places(where)):
+        at = multiple(plane if by_plane else place, size)
+        out[...] = total[pl.ds(at, size), :].astype(BF16)
+
+
+def forward_body(columns, where, hidden, cot, *refs):
+    pieces, (bias, active, slope, up_w), (*grads, total, sems) = refs[:6], refs[6:10], refs[10:]
     step = pl.program_id(0)
 
     @pl.when(step == 0)
     def _():
-        rows, middle = pair.shape[0], middle_left.shape[1]
-
-        def others(left, right):
-            return [(left, up_w.at[rows:, :middle]), (right, up_w.at[rows:, middle:])]
-
-        copy_either(
-            where,
-            [(pair, up_w.at[:rows])],
-            others(middle_left, middle_right),
-            others(end_left, end_right),
-            sems,
-        )
+        size = pieces[0].shape[0]
+
+        def of(piece, place, plane):
+            return [(piece, up_w.at[pl.ds(multiple(place, size), size)])]
+
+        copy_pieces(where, pieces, of, sems)
         total[...] = jnp.zeros_like(total)
 
     for j in range(up_w.shape[1] // columns):
@@ -536,62 +511,42 @@
 
     @pl.when(step == pl.num_programs(0) - 1)
     def _():
-        write_halves(where, total, grads, True)
+        write_blocks(where, total, grads, True)
 
 
 def forward(where, hidden, cot, pieces, bias, rows=512, columns=512):
     count, wide = hidden.shape[0], bias.shape[1]
     width = cot.shape[1]
-    grad = shaped((wide // 2, width // 2))
+    grad = shaped((wide // 4, width))
     outs = kernel(
         functools.partial(forward_body, columns),
         where,
         [hidden, cot, *pieces, bias],
-        [rows_of(hidden, rows), rows_of(cot, rows)] + [ANYWHERE] * 5 + [whole(bias)],
+        [rows_of(hidden, rows), rows_of(cot, rows)] + [ANYWHERE] * 6 + [whole(bias)],
         [pl.BlockSpec((rows, wide), lambda i, _: (i, 0))] * 2
         + [fixed((width, wide))]
         + [fixed(grad.shape)] * 4,
         [shaped((count, wide))] * 2 + [shaped((width, wide))] + [grad] * 4,
         grid=(count // rows,),
-        scratch=[pltpu.VMEM((wide, width), F32), pltpu.SemaphoreType.DMA((3,))],
-        work=(4 * hidden.size * wide, 32 * MIB),
+        scratch=[pltpu.VMEM((wide, width), F32), pltpu.SemaphoreType.DMA((4,))],
+        work=(4 * count * width * wide, 32 * MIB),
+        vmem=VMEM,
     )
     return outs[0], outs[1], outs[2], outs[3:]
 
 
-def backward_body(
-    where,
-    cot,
-    hidden,
-    pair,
-    middle_left,
-    middle_right,
-    end_left,
-    end_right,
-    slope,
-    d_upward,
-    sums,
-    down_w,
-    *rest,
-):
-    grads, total, sems = rest[:-2], rest[-2], rest[-1]
+def backward_body(where, cot, hidden, *refs):
+    pieces, (slope, d_upward, sums, down_w), (*grads, total, sems) = refs[:6], refs[6:10], refs[10:]
     step = pl.program_id(0)
 
     @pl.when(step == 0)
     def _():
-        rows, middle = middle_left.shape
-
-        def others(left, right):
-            part = pl.ds(multiple(1 - where[HALF], rows), rows)
-            return [(left, down_w.at[part, :middle]), (right, down_w.at[part, middle:])]
-
-        copy_either(
-            where,
-            [(pair, down_w.at[pl.ds(multiple(where[HALF], rows), rows)])],
-            others(middle_left, middle_right),
-            others(end_left, end_right),
-            sems,
-        )
+        size = pieces[0].shape[0]
+
+        def of(piece, place, plane):
+            return [(piece, down_w.at[pl.ds(multiple(plane, size), size)])]
+
+        copy_pieces(where, pieces, of, sems)
         sums[...] = jnp.zeros_like(sums)
         total[...] = jnp.zeros_like(total)
 
@@ -602,18 +557,18 @@
 
     @pl.when(step == pl.num_programs(0) - 1)
     def _():
-        write_halves(where, total, grads, False)
+        write_blocks(where, total, grads, False)
 
 
 def backward(where, cot, hidden, pieces, slope, rows=256):
     count, wide = slope.shape
     width = hidden.shape[1]
-    grad = shaped((width // 2, wide // 2))
+    grad = shaped((width // 4, wide))
     outs = kernel(
         backward_body,
         where,
         [cot, hidden, *pieces, slope],
-        [rows_of(cot, rows), rows_of(hidden, rows)] + [ANYWHERE] * 5 + [rows_of(slope, rows)],
+        [rows_of(cot, rows), rows_of(hidden, rows)] + [ANYWHERE] * 6 + [rows_of(slope, rows)],
         [
             pl.BlockSpec((rows, wide), lambda i, _: (i, 0)),
             pl.BlockSpec((1, wide), lambda i, _: (0, 0)),
@@ -622,8 +577,9 @@
         + [fixed(grad.shape)] * 4,
         [shaped((count, wide)), shaped((1, wide), F32), shaped((wide, width))] + [grad] * 4,
         grid=(count // rows,),
-        scratch=[pltpu.VMEM((width, wide), F32), pltpu.SemaphoreType.DMA((3,))],
-        work=(4 * cot.size * wide, 32 * MIB),
+        scratch=[pltpu.VMEM((width, wide), F32), pltpu.SemaphoreType.DMA((4,))],
+        work=(4 * count * width * wide, 32 * MIB),
+        vmem=VMEM,
     )
     return outs[0], outs[1], outs[2], outs[3:]
 
@@ -759,20 +715,11 @@
     )
 
 
-def finish_body(chips, wide, where, own_left, own_right, came_left, came_right, left, right, *outs):
+def finish_body(chips, wide, where, own, middle, last, *outs):
     keep, send = outs[:2]
-    n, columns = left.shape[0], left.shape[1]
+    n = own.shape[0]
     step = n // (CORES * chips)
-    total = jnp.concatenate(
-        [
-            own[...].astype(F32) + came[...].astype(F32) + last[...].astype(F32)
-            for own, came, last in (
-                (own_left, came_left, left),
-                (own_right, came_right, right),
-            )
-        ],
-        axis=1,
-    )
+    total = own[...].astype(F32) + middle[...].astype(F32) + last[...].astype(F32)
     low = total[:, :wide].astype(BF16)
     for core in range(CORES):
 
@@ -791,18 +738,17 @@
             beside[:, j * across : (j + 1) * across] = total[j * step : (j + 1) * step, wide:]
 
 
-def finish(where, chips, wide, own_left, own_right, came_left, came_right, left, right):
-    n, columns = left.shape
-    mine = pl.BlockSpec((n, columns), lambda i, where: (where[ODD], 0))
+def finish(where, chips, wide, own, middle, last):
+    n, columns = own.shape
     step = n // (CORES * chips)
     shapes = [shaped((chips, step, wide))] * 2
-    if wide < 2 * columns:
-        shapes.append(shaped((step, (2 * columns - wide) * CORES * chips), F32))
+    if wide < columns:
+        shapes.append(shaped((step, (columns - wide) * CORES * chips), F32))
     return kernel(
         functools.partial(finish_body, chips, wide),
         where,
-        [own_left, own_right, came_left, came_right, left, right],
-        [mine] * 4 + [whole(left), whole(right)],
+        [own, middle, last],
+        [whole(own)] * 3,
         [fixed(shape.shape) for shape in shapes],
         shapes,
         work=(0, 4 * MIB),
@@ -841,21 +787,48 @@
     )
 
 
-def corners_body(where, near_a, near_b, came_a, came_b, first, second):
-    first[...] = (near_a[...].astype(F32) + came_a[...].astype(F32)).astype(BF16)
-    second[...] = (near_b[...].astype(F32) + came_b[...].astype(F32)).astype(BF16)
-
-
-def corners(where, near, came):
-    rows, width = near.shape[0] // 8, near.shape[1]
-    blocks = [fixed((rows, width), 6), fixed((rows, width), 7)]
+def corners_body(where, *refs):
+    sources, outs = refs[:-2], refs[-2:]
+    for at in range(len(sources) // 4):
+        for i, out in enumerate(outs):
+            near, came = sources[4 * at + 2 * i], sources[4 * at + 2 * i + 1]
+            rows = near.shape[0]
+            total = near[...].astype(F32) + came[...].astype(F32)
+            out[at * rows : (at + 1) * rows] = total.astype(BF16)
+
+
+def corners(where, *sums):
+    rows, width = sums[0][0].shape[0] // 8, sums[0][0].shape[1]
+    out = shaped((len(sums) * rows, width))
     return kernel(
         corners_body,
         where,
-        [near, near, came, came],
-        blocks * 2,
-        [fixed((rows, width))] * 2,
-        [shaped((rows, width))] * 2,
+        [term for terms in sums for _ in range(2) for term in terms],
+        [fixed((rows, width), 6 + i) for _ in sums for i in range(2) for _ in range(2)],
+        [fixed(out.shape)] * 2,
+        [out] * 2,
+        work=(0, 4 * MIB),
+    )
+
+
+def pair_halves_body(where, *refs):
+    sources, outs = refs[:-2], refs[-2:]
+    for at in range(len(sources) // 2):
+        for i, out in enumerate(outs):
+            rows = sources[0].shape[0]
+            out[at * rows : (at + 1) * rows] = sources[2 * at + i][...]
+
+
+def pair_halves(where, *pairs):
+    rows, width = pairs[0][0].shape[0] // 2, pairs[0][0].shape[1]
+    out = shaped((len(pairs) * rows, width))
+    return kernel(
+        pair_halves_body,
+        where,
+        [array for by_x, by_y in pairs for array in (by_y, by_x)],
+        [fixed((rows, width), i) for _ in pairs for i in range(2)],
+        [fixed(out.shape)] * 2,
+        [out] * 2,
         work=(0, 4 * MIB),
     )
 
@@ -870,14 +843,14 @@
     for_y[half:] = y[half:].astype(BF16)
 
 
-def sides(where, near, came, extra_y, extra_x):
+def sides(where, near, came, extra_y, extra_x, at):
     rows, width = near.shape[0] // 4, near.shape[1]
     blocks = [fixed((rows, width), 1), fixed((rows, width), 2)]
     return kernel(
         sides_body,
         where,
         [near, near, came, came, extra_x, extra_y],
-        blocks * 2 + [whole(extra_x), whole(extra_y)],
+        blocks * 2 + [fixed((rows // 2, width), at)] * 2,
         [fixed((rows, width))] * 2,
         [shaped((rows, width))] * 2,
         work=(0, 8 * MIB),
@@ -989,43 +962,32 @@
     def inwards(value):
         return between(value, [(0, 1), (3, 2)])
 
-    def paired(own, came):
-        return jnp.where(
-            z % 2 == 0,
-            jnp.concatenate([own, came], axis=0),
-            jnp.concatenate([came, own], axis=0),
-        )
-
     def added(*terms):
         return sum(term.astype(F32) for term in terms)
 
-    def middle_share(other, came):
-        return added(other, came).astype(BF16)
-
-    def neighbour_share(own, came):
-        size = own.shape[0] // 2
-        lower, upper = [added(own[part], came[part]) for part in (slice(0, size), slice(size, None))]
-        return jnp.where(z % 2 == 1, lower, upper).astype(BF16)
+    def add(*terms, dtype=BF16):
+        return added(*terms).astype(dtype)
 
     def deal_over_chips(keep, send):
         blocks = deal_second(where, keep, flip(send, chips))
         return [blocks[0]] + [flip(blocks[r], r) for r in range(1, chips)]
 
     def over_planes(table):
+        return table + sum(
+            between(table, [(p, (p + r) % planes) for p in range(planes)])
+            for r in range(1, planes)
+        )
+
+    def over_chips(table):
+        return table + sum(flip(table, r) for r in range(1, chips))
+
+    def over_chips_in_turn(table):
         for r in (1, 2):
-            table = table + between(table, [(p, p ^ r) for p in range(planes)])
-        return table
-
-    def over_mates(table):
-        for r in (1, 2, 4):
             table = table + flip(table, r)
         return table
 
-    def left(value):
-        return value[:, : value.shape[1] // 2]
-
-    def right(value):
-        return value[:, value.shape[1] // 2 :]
+    def over_cores(table):
+        return table + flip(table, chips)
 
     def turned(value):
         middle = value.shape[1] // 2
@@ -1039,25 +1001,28 @@
     def near_first(block):
         return flip(block, 1), flip(block, 2)
 
-    def near_second(by_x, by_y):
-        return flip(by_y[:half], 1), flip(by_x[half:], 2)
-
-    def most_of(block, by_x, by_y):
-        return jnp.concatenate([block, by_x, by_y], axis=0)
-
     parts = [ln_gain, ln_bias, qkv_bias, dense_bias, up_bias, down_bias, lengths[0].astype(BF16)]
     sizes = [part.shape[0] for part in parts]
     starts = [sum(sizes[:i]) for i in range(len(sizes))]
     own_row = jnp.concatenate(parts)
     own_row = jnp.pad(own_row, (0, -len(own_row) % 128))
+    first_pieces = deal_first(where, planes, chips, up_weight, qkv_weight)
     table = jnp.where(jnp.arange(owners)[:, None] == rank, own_row[None, :], 0)
-    table, down_own = tied(over_planes(table), down_weight)
-
     wide = 3 * heads_width
-    w1 = to_neighbour(down_own)
-    dealt = deal_over_chips(*deal_first(where, planes, chips, up_weight, qkv_weight))
+    keep, send = first_pieces
+    table = over_planes(table)
+    blocks, table, down_own = tied(deal_second(where, keep, flip(send, chips)), table, down_weight)
+    dealt = [blocks[0]] + [flip(blocks[r], r) for r in range(1, chips)]
+    w1, w2a = to_neighbour(down_own), over_middle(down_own)
+    table = over_cores(over_chips(table))
     u_own, a_own = deal_last(where, dealt, dense_weight, planes * ff_block)
-    table = over_mates(table).astype(F32)
+    u_own, a_own, table, w1, w2a, cot_own = tied(
+        u_own, a_own, table, w1, w2a, cotangent
+    )
+    table = table.astype(F32)
+
+    a1, a2a = to_neighbour(a_own), over_middle(a_own)
+    cot_near = near_first(cot_own)
 
     def column(i):
         return table[:, starts[i] : starts[i] + sizes[i]].reshape(-1)
@@ -1099,152 +1064,136 @@
     sine_b = jnp.where((lane >= ROT // 2) & (lane < ROT), sine, 0.0)
     first = jnp.broadcast_to(offsets.reshape(count, 1), (count, 2 * HEAD_DIM))
 
-    w1, u_own, a_own, cot_own = tied(w1, u_own, a_own, cotangent)
-
-    w_pair = paired(down_own, w1)
-    u1 = to_neighbour(u_own)
-    w2_left = over_middle(left(w_pair))
-    cot_near = near_first(cot_own)
-
-    u1, w2_left, cot_near, a_own, hidden_own = tied(u1, w2_left, cot_near, a_own, hidden_own)
-    u_pair = paired(u_own, u1)
-    u2_left = over_middle(left(u_pair))
-    a1 = to_neighbour(a_own)
+    a1, a2a, cot_near, hidden_own, u_own = tied(a1, a2a, cot_near, hidden_own, u_own)
+    a3a, a2b = outwards(a2a), over_middle(a1)
     hidden_near = near_first(hidden_own)
-    cot_most = most_of(cot_own, *cot_near)
-    cot_across = flip(cot_most, chips)
-
-    u2_left, a1, hidden_near, cot_across, u_pair, cot_near = tied(
-        u2_left, a1, hidden_near, cot_across, u_pair, cot_near
-    )
-    a_pair = paired(a_own, a1)
-    u3_left = outwards(u2_left)
-    u2_right = over_middle(right(u_pair))
-    corner_y = flip(jnp.concatenate([cot_near[1][:half], hidden_near[1][:half]], axis=0), 1)
-    corner_x = flip(jnp.concatenate([cot_near[0][half:], hidden_near[0][half:]], axis=0), 2)
-    hidden_most = most_of(hidden_own, *hidden_near)
-    hidden_across = flip(hidden_most, chips)
-
-    u3_left, u2_right, corner_x, corner_y, a_pair, hidden_across = tied(
-        u3_left, u2_right, corner_x, corner_y, a_pair, hidden_across
-    )
-    u3_right = outwards(u2_right)
-    a2_left = over_middle(left(a_pair))
-    corner = jnp.concatenate([corner_y, corner_x], axis=0)
-    corner_across = flip(corner, chips)
-
-    def all_rows(most, across, at):
-        pieces = [most]
-        for corners_of in (corner, corner_across):
-            pieces += [corners_of[at : at + half], corners_of[at + 2 * half : at + 3 * half]]
-        return jnp.concatenate(pieces[:3] + [across] + pieces[3:], axis=0)
-
-    cot, hidden = all_rows(cot_most, cot_across, 0), all_rows(hidden_most, hidden_across, half)
-    u3_right, a2_left, a_pair, hidden, cot = tied(u3_right, a2_left, a_pair, hidden, cot)
-    a3_left = outwards(a2_left)
-    a2_right = over_middle(right(a_pair))
-    active, slope, up_w, g_w = forward(
-        where, hidden, cot, [u_pair, u2_left, u2_right, u3_left, u3_right], upward_bias
-    )
-
-    a3_left, a2_right, g_w, w_pair, cosine, sine_a, sine_b, first = tied(
-        a3_left, a2_right, g_w, w_pair, cosine, sine_a, sine_b, first
-    )
-    a3_right = outwards(a2_right)
-    w2_right = over_middle(right(w_pair))
-    q1_w_left = inwards(g_w[2])
-
-    a3_right, w2_right, q1_w_left, w2_left, g_w, hidden = tied(
-        a3_right, w2_right, q1_w_left, w2_left, g_w, hidden
-    )
-    w3_left = outwards(w2_left)
-    q1_w_right = inwards(g_w[3])
-    q2_w_left = over_middle(middle_share(g_w[2], q1_w_left))
+
+    a3a, a2b, hidden_near, cot_near, u_own = tied(a3a, a2b, hidden_near, cot_near, u_own)
+    a3b, u2a = outwards(a2b), over_middle(u_own)
+    for_x, for_y = pair_halves(where, cot_near, hidden_near)
+    corner_y, corner_x = flip(for_x, 1), flip(for_y, 2)
+    cot_most = jnp.concatenate([cot_own, *cot_near], axis=0)
+    hidden_most = jnp.concatenate([hidden_own, *hidden_near], axis=0)
+
+    a3b, u2a, corner_x, corner_y, hidden_most, cot_most, u_own, w1, cosine, sine_a, sine_b, first = tied(
+        a3b, u2a, corner_x, corner_y, hidden_most, cot_most, u_own, w1, cosine, sine_a, sine_b, first
+    )
+    u1, w2b = to_neighbour(u_own), over_middle(w1)
+    cot = jnp.concatenate([cot_most, corner_y[:half], corner_x[:half]], axis=0)
+    hidden = jnp.concatenate([hidden_most, corner_y[half:], corner_x[half:]], axis=0)
+    hidden, cot = [hidden, flip(hidden, chips)], [cot, flip(cot, chips)]
     streams = [packed_bias, cosine, sine_a, sine_b, first]
-    context_a, d_packed_a, g_a, (qkv_w, dense_w) = attention(
+    rows_a, g_a, (qkv_w, dense_w) = attention(
         where,
         row_count,
-        0,
-        count // 2,
         mates,
-        hidden,
-        cot,
-        [a_pair, a2_left, a2_right, a3_left, a3_right],
+        hidden[0],
+        cot[0],
+        [a_own, a1, a2a, a2b, a3a, a3b],
         streams,
         [],
-    )
-
-    w3_left, q1_w_right, q2_w_left, w2_right, g_a, hidden, g_w = tied(
-        w3_left, q1_w_right, q2_w_left, w2_right, g_a, hidden, g_w
-    )
-    w3_right = outwards(w2_right)
-    q2_w_right = over_middle(middle_share(g_w[3], q1_w_right))
-    q3_w_left = to_neighbour(neighbour_share(g_w[0], q2_w_left))
-    context_b, d_packed_b, g_a, _ = attention(
-        where,
-        row_count,
-        count // 2,
-        count // 2,
-        mates,
-        hidden,
-        cot,
-        [qkv_w, dense_w],
-        streams,
-        g_a,
-    )
-
-    w3_right, q2_w_right, q3_w_left, g_a, cot, slope, g_w = tied(
-        w3_right, q2_w_right, q3_w_left, g_a, cot, slope, g_w
-    )
-    q1_a_left = inwards(g_a[2])
-    q3_w_right = to_neighbour(neighbour_share(g_w[1], q2_w_right))
+        [],
+    )
+
+    u1, w2b, u2a, rows_a, g_a, hidden, cot = tied(u1, w2b, u2a, rows_a, g_a, hidden, cot)
+    u3a, u2b = outwards(u2a), over_middle(u1)
+    (context, d_packed), g_a, _ = attention(
+        where, row_count, mates, hidden[1], cot[1], [qkv_w, dense_w], streams, g_a, rows_a
+    )
+
+    u3a, u2b, g_a, w2a, d_packed, hidden, cot = tied(u3a, u2b, g_a, w2a, d_packed, hidden, cot)
+    u3b, q1_a_end = outwards(u2b), inwards(g_a[3])
+    hidden, cot = jnp.concatenate(hidden, axis=0), jnp.concatenate(cot, axis=0)
+    mine = jnp.arange(mates) == m
+    packed_sum = jnp.sum(d_packed.astype(F32), axis=0).reshape(3, planes, 1, HEAD_DIM)
+    packed_sum = jnp.where(mine[None, None, :, None], packed_sum, 0.0).reshape(owners, -1)
+    cot_sum = jnp.sum(cotangent.astype(F32), axis=0).reshape(owners, -1)
+
+    u3b, q1_a_end, g_a, w2a, hidden, cot, packed_sum, cot_sum = tied(
+        u3b, q1_a_end, g_a, w2a, hidden, cot, packed_sum, cot_sum
+    )
+    w3a, q1_a_mid, q2_a_end = outwards(w2a), inwards(g_a[2]), over_middle(add(g_a[3], q1_a_end))
+    active, slope, up_w, g_w = forward(
+        where, hidden, cot, [u_own, u1, u2a, u2b, u3a, u3b], upward_bias
+    )
+
+    w3a, q1_a_mid, q2_a_end, g_a, g_w, w2b = tied(w3a, q1_a_mid, q2_a_end, g_a, g_w, w2b)
+    w3b, q1_w_end, q2_a_mid = outwards(w2b), inwards(g_w[3]), over_middle(add(g_a[2], q1_a_mid))
+
+    w3b, q1_w_end, q2_a_mid, q2_a_end, g_a, g_w, cot = tied(
+        w3b, q1_w_end, q2_a_mid, q2_a_end, g_a, g_w, cot
+    )
+    q3_a, q2_w_end = to_neighbour(add(g_a[1], q2_a_end)), over_middle(add(g_w[3], q1_w_end))
     d_upward, upward_sum, down_w, g_u = backward(
-        where, cot, hidden, [w_pair, w2_left, w2_right, w3_left, w3_right], slope
-    )
-
-    q1_a_left, q3_w_right, q3_w_left, g_u, d_upward, g_a = tied(
-        q1_a_left, q3_w_right, q3_w_left, g_u, d_upward, g_a
-    )
-    q1_a_right = inwards(g_a[3])
-    q2_a_left = over_middle(middle_share(g_a[2], q1_a_left))
-    context = jnp.concatenate([context_a, context_b], axis=0)
-    d_packed = jnp.concatenate([d_packed_a, d_packed_b], axis=0)
+        where, cot, hidden, [down_own, w1, w2a, w2b, w3a, w3b], slope
+    )
+
+    q3_a, q2_w_end, g_w, g_u, d_upward, q2_a_mid, upward_sum = tied(
+        q3_a, q2_w_end, g_w, g_u, d_upward, q2_a_mid, upward_sum
+    )
+    q1_u_end = inwards(g_u[3])
     d_hidden_far, d_hidden_near = two_dots(nt, d_packed, qkv_w, d_upward, up_w, width)
-
-    q1_a_right, q2_a_left, d_hidden_far, d_hidden_near, g_u, g_a, context = tied(
-        q1_a_right, q2_a_left, d_hidden_far, d_hidden_near, g_u, g_a, context
-    )
+    upward_sum = upward_sum.reshape(planes, 1, ff_block)
+    upward_sum = jnp.where(mine[None, :, None], upward_sum, 0.0).reshape(owners, -1)
+    keep, send, grad_dense_w = finish(where, chips, wide, g_a[0], q2_a_mid, q3_a)
+    came = flip(send, chips)
+
+    q1_u_end, d_hidden_far, d_hidden_near, g_u, g_w, context, upward_sum, keep, came = tied(
+        q1_u_end, d_hidden_far, d_hidden_near, g_u, g_w, context, upward_sum, keep, came
+    )
+    q1_u_mid, q2_u_end = inwards(g_u[2]), over_middle(add(g_u[3], q1_u_end))
     d_hidden_came = flip(d_hidden_far, chips)
-    q1_u_left = inwards(g_u[2])
-    q2_a_right = over_middle(middle_share(g_a[3], q1_a_right))
-    q3_a_left = to_neighbour(neighbour_share(g_a[0], q2_a_left))
     out_far, out_near = two_dots(nn, context, dense_w, active, down_w, width)
-    own_down = jnp.concatenate([added(*both) for both in zip(g_w[:2], (q2_w_left, q2_w_right))], axis=1)
-    grad_down_w = lax.dynamic_slice_in_dim(
-        own_down, (z % 2) * ff_block, ff_block, 0
-    ) + jnp.concatenate([q3_w_left, q3_w_right], axis=1).astype(F32)
-
-    q1_u_left, q2_a_right, q3_a_left, d_hidden_came, out_far, out_near, g_u, g_a = tied(
-        q1_u_left, q2_a_right, q3_a_left, d_hidden_came, out_far, out_near, g_u, g_a
-    )
+    corner_y, corner_x = corners(where, (d_hidden_near, d_hidden_came))
+    extra_y, extra_x = flip(corner_y, 1), flip(corner_x, 2)
+
+    q1_u_mid, q2_u_end, extra_x, extra_y, out_far, out_near, g_u, g_w, keep = tied(
+        q1_u_mid, q2_u_end, extra_x, extra_y, out_far, out_near, g_u, g_w, keep
+    )
+    q3_u, q2_u_mid = to_neighbour(add(g_u[1], q2_u_end)), over_middle(add(g_u[2], q1_u_mid))
     out_came = flip(out_far, chips)
-    corner_a, corner_b = corners(where, d_hidden_near, d_hidden_came)
-    extra_y, extra_x = flip(corner_a, 1), flip(corner_b, 2)
-    for_x, for_y = sides(where, d_hidden_near, d_hidden_came, extra_y, extra_x)
+    corner_y, corner_x = corners(where, (out_near, out_came))
+    out_extra_y, out_extra_x = flip(corner_y, 1), flip(corner_x, 2)
+    blocks = deal_second(where, keep, came)
+
+    q3_u, q2_u_mid, out_extra_x, out_extra_y, g_u, g_w, blocks = tied(
+        q3_u, q2_u_mid, out_extra_x, out_extra_y, g_u, g_w, blocks
+    )
+    q1_w_mid = inwards(g_w[2])
+    for_x, for_y = sides(where, d_hidden_near, d_hidden_came, extra_y, extra_x, 0)
     d_hidden_last = flip(for_x, 1), flip(for_y, 2)
-    q1_u_right = inwards(g_u[3])
-    q2_u_left = over_middle(middle_share(g_u[2], q1_u_left))
-    q3_a_right = to_neighbour(neighbour_share(g_a[1], q2_a_right))
-
-    q1_u_right, q2_u_left, q3_a_right, d_hidden_last, out_came, g_u, q3_a_left = tied(
-        q1_u_right, q2_u_left, q3_a_right, d_hidden_last, out_came, g_u, q3_a_left
-    )
-    corner_a, corner_b = corners(where, out_near, out_came)
-    extra_y, extra_x = flip(corner_a, 1), flip(corner_b, 2)
-    for_x, for_y = sides(where, out_near, out_came, extra_y, extra_x)
+    block_x, block_y, block_xy = [flip(blocks[r], r) for r in range(1, chips)]
+    for_x, for_y = sides(where, out_near, out_came, out_extra_y, out_extra_x, 0)
+    keep, send = finish(where, chips, planes * ff_block, g_u[0], q2_u_mid, q3_u)
+
+    (
+        q1_w_mid,
+        q2_w_end,
+        d_hidden_last,
+        for_x,
+        for_y,
+        g_w,
+        block_x,
+        block_y,
+        block_xy,
+        keep,
+        send,
+    ) = tied(
+        q1_w_mid,
+        q2_w_end,
+        d_hidden_last,
+        for_x,
+        for_y,
+        g_w,
+        block_x,
+        block_y,
+        block_xy,
+        keep,
+        send,
+    )
+    q3_w, q2_w_mid = to_neighbour(add(g_w[1], q2_w_end)), over_middle(add(g_w[2], q1_w_mid))
     out_last = flip(for_x, 1), flip(for_y, 2)
-    q2_u_right = over_middle(middle_share(g_u[3], q1_u_right))
-    q3_u_left = to_neighbour(neighbour_share(g_u[0], q2_u_left))
+    held = deal_second(where, keep, flip(send, chips))
     grad_tokens, gain_sum, shift_sum = norm_back(
         where,
         d_hidden_near,
@@ -1254,50 +1203,31 @@
         cotangent,
         gain.reshape(1, -1),
     )
-    keep, send, grad_dense_w = finish(
-        where, chips, wide, g_a[0], g_a[1], q2_a_left, q2_a_right, q3_a_left, q3_a_right
-    )
-    blocks = deal_second(where, keep, flip(send, chips))
-
-    q2_u_right, q3_u_left, out_last, blocks, grad_tokens, gain_sum, g_u = tied(
-        q2_u_right, q3_u_left, out_last, blocks, grad_tokens, gain_sum, g_u
-    )
-    q3_u_right = to_neighbour(neighbour_share(g_u[1], q2_u_right))
-    blocks = [blocks[0]] + [flip(blocks[r], r) for r in range(1, chips)]
-    output = added(out_near[:row_count], out_came[:row_count], *out_last)
-    output = (inputs_f + output + out_bias).astype(BF16)
-
-    q3_u_right, blocks = tied(q3_u_right, blocks)
-    keep, send = finish(
-        where,
-        chips,
-        planes * ff_block,
-        g_u[0],
-        g_u[1],
-        q2_u_left,
-        q2_u_right,
-        q3_u_left,
-        q3_u_right,
-    )
-    grad_up_w = back(where, deal_over_chips(keep, send), planes)
-    grad_qkv_w = back(where, blocks, 3 * planes)
-
-    mine = jnp.arange(mates) == m
-    packed_sum = jnp.sum(d_packed.astype(F32), axis=0).reshape(3, planes, 1, HEAD_DIM)
-    packed_sum = jnp.where(mine[None, None, :, None], packed_sum, 0.0)
-    upward_sum = upward_sum.reshape(planes, 1, ff_block)
-    upward_sum = jnp.where(mine[None, :, None], upward_sum, 0.0)
     sums = jnp.concatenate(
         [
             gain_sum.reshape(owners, -1),
             shift_sum.reshape(owners, -1),
-            jnp.sum(cotangent.astype(F32), axis=0).reshape(owners, -1),
-            packed_sum.reshape(owners, -1),
-            upward_sum.reshape(owners, -1),
+            cot_sum,
+            packed_sum,
+            upward_sum,
         ],
         axis=1,
     )
-    total = lax.dynamic_index_in_dim(over_mates(over_planes(sums)), rank, 0, keepdims=False)
+
+    q3_w, q2_w_mid, g_w, out_last, sums, held = tied(q3_w, q2_w_mid, g_w, out_last, sums, held)
+    received = [flip(held[r], r) for r in range(1, chips)]
+    for r in (1, 2):
+        sums = sums + between(sums, [(p, p ^ r) for p in range(planes)])
+    grad_qkv_w = back(where, [blocks[0], block_x, block_y, block_xy], 3 * planes)
+    output = added(out_near[:row_count], out_came[:row_count], *out_last)
+    output = (inputs_f + output + out_bias).astype(BF16)
+    grad_down_w = add(g_w[0], q2_w_mid, q3_w, dtype=F32)
+    received, sums, grad_qkv_w, output, grad_down_w = tied(
+        received, sums, grad_qkv_w, output, grad_down_w
+    )
+    sums = over_cores(over_chips(sums))
+    grad_up_w = back(where, [held[0]] + received, planes)
+    total = lax.dynamic_index_in_dim(sums, rank, 0, keepdims=False)
     grad_gain, grad_shift, grad_out_b, grad_packed_b, grad_up_b = jnp.split(
         total,
         [
@@ -1307,7 +1237,6 @@
             sizes[0] + sizes[1] + sizes[3] + sizes[2],
         ],
     )
-
     return (
         output,
         grad_tokens,

time: 641 us -> 574 us (0.90)
  waiting for transfers between devices: 197 us -> 141 us
  local copies, waits for them, and re-layouts: 61.7 us -> 35 us
  starting transfers between devices: 106 us -> 115 us
  other arithmetic: 63.6 us -> 71.5 us
    pallas_call x0 -> x2, Pallas kernels: none -> 68.7 us  [attention(): pl.pallas_call(functools.partial(attention_body, parts, run, merge), grid...]
    pallas_call x18 -> x17, Pallas kernels: 159 us -> 93 us  [kernel(): pl.pallas_call(body, grid_spec=pltpu.PrefetchScalarGridSpec(num_scalar_pr...]
    ppermute x37 -> x35, waiting for transfers between devices: 128 us -> 89 us  [between(): lax.ppermute(value, AXES, [(p * mates + i, q * mates + i) for p, q in pai...]
    unnamed x202 -> x110, local copies, waits for them, and re-layouts: 40.4 us -> 21.3 us
    concatenate x6 -> x5, other arithmetic: 5.24 us -> 24.2 us  [the longest x1 8.54 us: by_planes(): jnp.concatenate(cot, axis=0)]
    ppermute x37 -> x38, waiting for transfers between devices: 69.4 us -> 51.5 us  [flip(): lax.ppermute(value, AXES, [(p * mates + i, p * mates + (i ^ r)) for p in...]
    select_n x5 -> x2, other arithmetic: 9.53 us -> 0.75 us  [the longest x1 0.67 us: by_planes(): jnp.where(mine[None, :, None], upward_sum, 0.0).reshape(owners, -1)]
    ppermute x37 -> x35, starting transfers between devices: 77.1 us -> 83.9 us  [between(): lax.ppermute(value, AXES, [(p * mates + i, q * mates + i) for p, q in pai...]
  transfers between devices with their start and end apart: 74 -> 73, of which waited for: 29 -> 31; matrix products, arithmetic and copies ran while one was open for 11% -> 13% of each run, Pallas kernels for 31% -> 35%
where the time goes in v3:
time: 574 us; the launch traced here: 566 us
  Pallas kernels  202 us (35%)
  waiting for transfers between devices  141 us (25%)
  starting transfers between devices  115 us (20%)
  other arithmetic  71.5 us (12%)
  local copies, waits for them, and re-layouts  35 us (6%)
    pallas_call x17, Pallas kernels, kernel(): pl.pallas_call(body, grid_spec=pltpu.PrefetchScalarGridSpec(num_scalar_pr...  93 us
    ppermute x35, waiting for transfers between devices, between(): lax.ppermute(value, AXES, [(p * mates + i, q * mates + i) for p, q in pai...  89 us
    ppermute x35, starting transfers between devices, between(): lax.ppermute(value, AXES, [(p * mates + i, q * mates + i) for p, q in pai...  83.9 us
    pallas_call x2, Pallas kernels, attention(): pl.pallas_call(functools.partial(attention_body, parts, run, merge), grid...  68.7 us
    ppermute x38, waiting for transfers between devices, flip(): lax.ppermute(value, AXES, [(p * mates + i, p * mates + (i ^ r)) for p in...  51.5 us
    pallas_call x2, Pallas kernels, two_dots(): pl.pallas_call(functools.partial(two_dots_body, dot), grid=(steps,), in_s...  40.2 us
    ppermute x38, starting transfers between devices, flip(): lax.ppermute(value, AXES, [(p * mates + i, p * mates + (i ^ r)) for p in...  31.5 us
    convert_element_type x9, other arithmetic, add(): return added(*terms).astype(dtype)  22.1 us
  transfers between devices with their start and end apart: 73, of which 31 were waited for; matrix products, arithmetic and copies ran while one was open for 13% of the time, Pallas kernels for 35%

profile of v3, /device:TPU:0, one launch (start us, length us, event | category | flops | bytes accessed | tf_op | source)
XLA Modules:
  0.0 566.2 jit_solution(12990168488976253508)
XLA Ops:
  39.6 8.2 %collective-permute-done.4.refs_1_ = bf16[2,64,1792]{2,1,0:T(8,128)(2,1)S(1)} collective-permute-done((bf16[2,64,1792]{2,1,0:T(8,128)(2,1)}, bf16[2,64,1792]{2,1,0:T(8,128)(2,1)S(1)}, u32[]{:S(2)}, u32[]{:S(2)}) %collective-permute-start.4) | collective-permute-done | bytes 458784 | tf_op jit(solution)/shard_map/ppermute | solution.py:942
  47.8 10.4 %collective-permute-done.5.refs_2_ = bf16[2,64,1792]{2,1,0:T(8,128)(2,1)S(1)} collective-permute-done((bf16[2,64,1792]{2,1,0:T(8,128)(2,1)}, bf16[2,64,1792]{2,1,0:T(8,128)(2,1)S(1)}, u32[]{:S(2)}, u32[]{:S(2)}) %collective-permute-start.5) | collective-permute-done | bytes 458784 | tf_op jit(solution)/shard_map/ppermute | solution.py:942
  69.7 17.5 %collective-permute-done.13.refs_3_ = bf16[512,1024]{1,0:T(8,128)(2,1)} collective-permute-done((bf16[512,1024]{1,0:T(8,128)(2,1)}, bf16[512,1024]{1,0:T(8,128)(2,1)}, u32[]{:S(2)}, u32[]{:S(2)}) %collective-permute-start.13) | collective-permute-done | bytes 1048608 | tf_op jit(solution)/shard_map/ppermute | solution.py:949
  96.6 19.8 %collective-permute-done.17.refs_6_ = bf16[512,1024]{1,0:T(8,128)(2,1)} collective-permute-done((bf16[512,1024]{1,0:T(8,128)(2,1)}, bf16[512,1024]{1,0:T(8,128)(2,1)}, u32[]{:S(2)}, u32[]{:S(2)}) %collective-permute-start.17) | collective-permute-done | bytes 1048608 | tf_op jit(solution)/shard_map/ppermute | solution.py:949
  123.8 5.8 %fusion.8 = (f32[2048,128]{1,0:T(8,128)}, f32[2048,128]{1,0:T(8,128)}, f32[2048,128]{1,0:T(8,128)}) fusion(f32[128]{0:T(128)S(1)} %fusion.15, f32[2048]{0:T(1024)S(1)} %subtract_convert_fusion, pred[128]{0:T(512)(128)(4,1)S(1)} %get-tuple-element.520, pred[128]{0:T(512)(128)(4,1)S(1)} %get-tuple-element.521, pred[128]{0:T(512)(128)(4,1)S(1)} %broadcast_compare_fusion.1), kind=kLoop, calls=%fused_computation.31 | loop fusion | flops 1310720 | bytes 3154816 | tf_op jit(solution)/shard_map/jit(_where)/select_n | solution.py:1064
  132.1 11.1 %collective-permute-done.21.refs_7_ = bf16[512,1024]{1,0:T(8,128)(2,1)S(1)} collective-permute-done((bf16[512,1024]{1,0:T(8,128)(2,1)}, bf16[512,1024]{1,0:T(8,128)(2,1)S(1)}, u32[]{:S(2)}, u32[]{:S(2)}) %collective-permute-start.21) | collective-permute-done | bytes 1048608 | tf_op jit(solution)/shard_map/ppermute | solution.py:949
  153.1 5.9 %collective-permute-start.25 = (bf16[512,1024]{1,0:T(8,128)(2,1)S(1)}, bf16[512,1024]{1,0:T(8,128)(2,1)}, u32[]{:S(2)}, u32[]{:S(2)}) collective-permute-start(bf16[512,1024]{1,0:T(8,128)(2,1)S(1)} %copy-done.36), channel_id=1, source_target_pairs={{0,8},{1,9},{2,10},{3,11},{4,12},{5,13},{6,14},{7,15},{8,0},{9,1},... | collective-permute-start | bytes 3145736 | tf_op jit(solution)/shard_map/ppermute | solution.py:949
  160.8 34.9 %shard_map.224 = (bf16[2048,256]{1,0:T(8,128)(2,1)}, bf16[2048,768]{1,0:T(8,128)(2,1)}, bf16[512,1024]{1,0:T(8,128)(2,1)}, bf16[512,1024]{1,0:T(8,128)(2,1)}, bf...) custom-call(s32[5]{0:T(128)} %copy-done.31, ...), custom_call_target="tpu_custom_call" | custom-call | flops 17999998976 | bytes 20971520 | tf_op jit(solution)/shard_map/pallas_call | solution.py:449
  199.3 33.8 %shard_map.225 = (bf16[2048,256]{1,0:T(8,128)(2,1)}, bf16[2048,768]{1,0:T(8,128)(2,1)}, bf16[512,1024]{1,0:T(8,128)(2,1)}, bf16[512,1024]{1,0:T(8,128)(2,1)}, bf...) custom-call(s32[5]{0:T(128)} %copy-done.31, ...), custom_call_target="tpu_custom_call", output_to_operand_aliasing={{0}: (14, {}), {1}: (15, {})} | custom-call | flops 17999998976 | bytes 20971520 | tf_op jit(solution)/shard_map/pallas_call | solution.py:449
  234.4 7.9 %collective-permute-start.32 = (bf16[512,1024]{1,0:T(8,128)(2,1)}, bf16[512,1024]{1,0:T(8,128)(2,1)}, u32[]{:S(2)}, u32[]{:S(2)}) collective-permute-start(bf16[512,1024]{1,0:T(8,128)(2,1)} %get-tuple-element.340), channel_id=1, source_target_pairs={{0,8},{1,9},{2,10},{3,11},{4,12},{5,13},{6,14},{7,15},{24,16},{25,... | collective-permute-start | bytes 3145736 | tf_op jit(solution)/shard_map/ppermute | solution.py:949
  245.5 8.5 %pad_maximum_fusion.hidden = bf16[2048,2048]{1,0:T(8,128)(2,1)} fusion(bf16[1024,2048]{1,0:T(8,128)(2,1)} %collective-permute-done.27.refs_0_, bf16[1024,2048]{1,0:T(8,128)(2,1)} %pad_maximum_fusion.2.refs_0_), kind=kLoop, calls=%fused_computation | loop fusion | flops 16777216 | bytes 16777216 | tf_op jit(solution)/shard_map/concatenate | solution.py:1106
  254.0 8.5 %pad_maximum_fusion.1.cot = bf16[2048,2048]{1,0:T(8,128)(2,1)} fusion(bf16[1024,2048]{1,0:T(8,128)(2,1)} %collective-permute-done.28.refs_1_, bf16[1024,2048]{1,0:T(8,128)(2,1)} %pad_maximum_fusion.3.refs_1_), kind=kLoop, calls=%fused_computation.1 | loop fusion | flops 16777216 | bytes 16777216 | tf_op jit(solution)/shard_map/concatenate | solution.py:1106
  264.6 6.5 %collective-permute-start.34 = (bf16[512,1024]{1,0:T(8,128)(2,1)S(1)}, bf16[512,1024]{1,0:T(8,128)(2,1)}, u32[]{:S(2)}, u32[]{:S(2)}) collective-permute-start(bf16[512,1024]{1,0:T(8,128)(2,1)S(1)} %copy-done.41), channel_id=1, source_target_pairs={{0,8},{1,9},{2,10},{3,11},{4,12},{5,13},{6,14},{7,15},{24,16},{25,... | collective-permute-start | bytes 3145736 | tf_op jit(solution)/shard_map/ppermute | solution.py:949
  275.8 33.3 %shard_map.226 = (bf16[2048,1024]{1,0:T(8,128)(2,1)}, bf16[2048,1024]{1,0:T(8,128)(2,1)}, bf16[2048,1024]{1,0:T(8,128)(2,1)}, bf16[256,2048]{1,0:T(8,128)(2,1)},...) custom-call(s32[5]{0:T(128)} %copy-done.31, ...), custom_call_target="tpu_custom_call" | custom-call | flops 17179869184 | bytes 33554432 | tf_op jit(solution)/shard_map/pallas_call | solution.py:260
  310.5 6.5 %collective-permute-start.37 = (bf16[256,2048]{1,0:T(8,128)(2,1)}, bf16[256,2048]{1,0:T(8,128)(2,1)}, u32[]{:S(2)}, u32[]{:S(2)}) collective-permute-start(bf16[256,2048]{1,0:T(8,128)(2,1)} %get-tuple-element.365), channel_id=1, source_target_pairs={{0,8},{1,9},{2,10},{3,11},{4,12},{5,13},{6,14},{7,15},{24,16},{25,... | collective-permute-start | bytes 3145736 | tf_op jit(solution)/shard_map/ppermute | solution.py:949
  320.4 13.9 %collective-permute-done.36.refs_5_ = bf16[256,2048]{1,0:T(8,128)(2,1)} collective-permute-done((bf16[256,2048]{1,0:T(8,128)(2,1)}, bf16[256,2048]{1,0:T(8,128)(2,1)}, u32[]{:S(2)}, u32[]{:S(2)}) %collective-permute-start.36) | collective-permute-done | bytes 1048608 | tf_op jit(solution)/shard_map/ppermute | solution.py:949
  339.8 6.3 %collective-permute-start.39 = (bf16[512,1024]{1,0:T(8,128)(2,1)}, bf16[512,1024]{1,0:T(8,128)(2,1)}, u32[]{:S(2)}, u32[]{:S(2)}) collective-permute-start(bf16[512,1024]{1,0:T(8,128)(2,1)} %add_convert_fusion.6), channel_id=1, source_target_pairs={{0,8},{1,9},{2,10},{3,11},{4,12},{5,13},{6,14},{7,15},{8,0},{9,1},... | collective-permute-start | bytes 3145736 | tf_op jit(solution)/shard_map/ppermute | solution.py:949
  350.3 28.8 %shard_map.227 = (bf16[2048,1024]{1,0:T(8,128)(2,1)}, f32[1,1024]{1,0:T(1,128)}, bf16[1024,2048]{1,0:T(8,128)(2,1)}, bf16[512,1024]{1,0:T(8,128)(2,1)}, bf16[512...) custom-call(s32[5]{0:T(128)} %copy-done.31, bf16[2048,2048]{1,0:T(8,128)(2,1)} %pad_maximum_fusion.1.cot, ...), custom_call_target="tpu_custom_call" | custom-call | flops 17179869184 | bytes 33554432 | tf_op jit(solution)/shard_map/pallas_call | solution.py:260
  388.2 22.8 %shard_map.228 = (bf16[1024,2048]{1,0:T(8,128)(2,1)}, bf16[1024,2048]{1,0:T(8,128)(2,1)}) custom-call(bf16[2048,768]{1,0:T(8,128)(2,1)} %get-tuple-element.337.a, bf16[2048,768]{1,0:T(8,128)(2,1)} %get-tuple-element.311.refs_2_.aw, bf16[2048,1024]{1,0:T(8,128)(2,1)} %get-tuple-element.382.b, bf16[2048,1024]{1,0:T(8,128)(2,1)} %get-tuple-element.383.bw), custom_call_target="tpu_custom_call" | custom-call | flops 15032385536 | bytes 23068672 | tf_op jit(solution)/shard_map/pallas_call | solution.py:609
  427.6 17.4 %shard_map.231 = (bf16[1024,2048]{1,0:T(8,128)(2,1)}, bf16[1024,2048]{1,0:T(8,128)(2,1)}) custom-call(bf16[2048,256]{1,0:T(8,128)(2,1)} %get-tuple-element.406.a, bf16[256,2048]{1,0:T(8,128)(2,1)} %get-tuple-element.312.refs_3_.aw, bf16[2048,1024]{1,0:T(8,128)(2,1)} %get-tuple-element.407.b, bf16[1024,2048]{1,0:T(8,128)(2,1)} %get-tuple-element.408.bw), custom_call_target="tpu_custom_call" | custom-call | flops 10737418240 | bytes 18874368 | tf_op jit(solution)/shard_map/pallas_call | solution.py:609
  457.6 15.5 %collective-permute-done.48.last = bf16[512,1024]{1,0:T(8,128)(2,1)S(1)} collective-permute-done((bf16[512,1024]{1,0:T(8,128)(2,1)S(1)}, bf16[512,1024]{1,0:T(8,128)(2,1)S(1)}, u32[]{:S(2)}, u32[]{:S(2)}) %collective-permute-start.48) | collective-permute-done | bytes 1048608 | tf_op jit(solution)/shard_map/ppermute | solution.py:949
  473.5 7.3 %collective-permute-start.53 = (bf16[256,2048]{1,0:T(8,128)(2,1)S(1)}, bf16[256,2048]{1,0:T(8,128)(2,1)S(1)}, u32[]{:S(2)}, u32[]{:S(2)}) collective-permute-start(bf16[256,2048]{1,0:T(8,128)(2,1)S(1)} %copy-done.38), channel_id=1, source_target_pairs={{0,8},{1,9},{2,10},{3,11},{4,12},{5,13},{6,14},{7,15},{24,16},{25,... | collective-permute-start | bytes 3145736 | tf_op jit(solution)/shard_map/ppermute | solution.py:949
  482.1 8.9 %collective-permute-done.54.by_x = bf16[256,2048]{1,0:T(8,128)(2,1)S(1)} collective-permute-done((bf16[256,2048]{1,0:T(8,128)(2,1)S(1)}, bf16[256,2048]{1,0:T(8,128)(2,1)S(1)}, u32[]{:S(2)}, u32[]{:S(2)}) %collective-permute-start.54) | collective-permute-done | bytes 1048608 | tf_op jit(solution)/shard_map/ppermute | solution.py:942
  497.3 6.1 %collective-permute-done.55.by_y = bf16[256,2048]{1,0:T(8,128)(2,1)S(1)} collective-permute-done((bf16[256,2048]{1,0:T(8,128)(2,1)S(1)}, bf16[256,2048]{1,0:T(8,128)(2,1)S(1)}, u32[]{:S(2)}, u32[]{:S(2)}) %collective-permute-start.55) | collective-permute-done | bytes 1048608 | tf_op jit(solution)/shard_map/ppermute | solution.py:942
  (337 shorter events, 218.9 us)
Async XLA Ops:
  30.0 32.8 %collective-permute-start.11 = (bf16[256,2048]{1,0:T(8,128)(2,1)}, bf16[256,2048]{1,0:T(8,128)(2,1)}, u32[]{:S(2)}, u32[]{:S(2)}) collective-permute-start(bf16[256,2048]{1,0:T(8,128)(2,1)} %refs_0_), channel_id=1, source_target_pairs={{0,8},{1,9},{2,10},{3,11},{4,12},{5,13},{6,14},{7,15},{8,0},{9,1},... | collective-permute-start | bytes 3145736 | tf_op jit(solution)/shard_map/ppermute | solution.py:949
  30.3 32.5 %collective-permute-start.12 = (bf16[256,2048]{1,0:T(8,128)(2,1)}, bf16[256,2048]{1,0:T(8,128)(2,1)}, u32[]{:S(2)}, u32[]{:S(2)}) collective-permute-start(bf16[256,2048]{1,0:T(8,128)(2,1)} %refs_0_), channel_id=1, source_target_pairs={{8,16},{9,17},{10,18},{11,19},{12,20},{13,21},{14,22},{15,23},{16,... | collective-permute-start | bytes 3145736 | tf_op jit(solution)/shard_map/ppermute | solution.py:949
  148.0 47.8 %collective-permute-start.27 = (bf16[1024,2048]{1,0:T(8,128)(2,1)}, bf16[1024,2048]{1,0:T(8,128)(2,1)}, u32[]{:S(2)}, u32[]{:S(2)}) collective-permute-start(bf16[1024,2048]{1,0:T(8,128)(2,1)} %pad_maximum_fusion.2.refs_0_), channel_id=1, source_target_pairs={{0,4},{1,5},{2,6},{3,7},{4,0},{5,1},{6,2},{7,3},{8,12},{9,13},{10,... | collective-permute-start | bytes 12582920 | tf_op jit(solution)/shard_map/ppermute | solution.py:942
  150.4 45.4 %collective-permute-start.28 = (bf16[1024,2048]{1,0:T(8,128)(2,1)}, bf16[1024,2048]{1,0:T(8,128)(2,1)}, u32[]{:S(2)}, u32[]{:S(2)}) collective-permute-start(bf16[1024,2048]{1,0:T(8,128)(2,1)} %pad_maximum_fusion.3.refs_1_), channel_id=1, source_target_pairs={{0,4},{1,5},{2,6},{3,7},{4,0},{5,1},{6,2},{7,3},{8,12},{9,13},{10,... | collective-permute-start | bytes 12582920 | tf_op jit(solution)/shard_map/ppermute | solution.py:942
  153.1 42.7 %collective-permute-start.25 = (bf16[512,1024]{1,0:T(8,128)(2,1)S(1)}, bf16[512,1024]{1,0:T(8,128)(2,1)}, u32[]{:S(2)}, u32[]{:S(2)}) collective-permute-start(bf16[512,1024]{1,0:T(8,128)(2,1)S(1)} %copy-done.36), channel_id=1, source_target_pairs={{0,8},{1,9},{2,10},{3,11},{4,12},{5,13},{6,14},{7,15},{8,0},{9,1},... | collective-permute-start | bytes 3145736 | tf_op jit(solution)/shard_map/ppermute | solution.py:949
  158.9 36.9 %collective-permute-start.26 = (bf16[256,2048]{1,0:T(8,128)(2,1)}, bf16[256,2048]{1,0:T(8,128)(2,1)}, u32[]{:S(2)}, u32[]{:S(2)}) collective-permute-start(bf16[256,2048]{1,0:T(8,128)(2,1)} %collective-permute-done.11.refs_1_), channel_id=1, source_target_pairs={{8,16},{9,17},{10,18},{11,19},{12,20},{13,21},{14,22},{15,23},{16,... | collective-permute-start | bytes 3145736 | tf_op jit(solution)/shard_map/ppermute | solution.py:949
  195.8 37.2 %collective-permute-start.29 = (bf16[512,1024]{1,0:T(8,128)(2,1)}, bf16[512,1024]{1,0:T(8,128)(2,1)S(1)}, u32[]{:S(2)}, u32[]{:S(2)}) collective-permute-start(bf16[512,1024]{1,0:T(8,128)(2,1)} %copy-done.50), channel_id=1, source_target_pairs={{8,0},{9,1},{10,2},{11,3},{12,4},{13,5},{14,6},{15,7},{16,24},{17,... | collective-permute-start | bytes 3145736 | tf_op jit(solution)/shard_map/ppermute | solution.py:949
  197.1 35.9 %collective-permute-start.30 = (bf16[512,1024]{1,0:T(8,128)(2,1)}, bf16[512,1024]{1,0:T(8,128)(2,1)}, u32[]{:S(2)}, u32[]{:S(2)}) collective-permute-start(bf16[512,1024]{1,0:T(8,128)(2,1)} %collective-permute-done.25.refs_1_), channel_id=1, source_target_pairs={{8,16},{9,17},{10,18},{11,19},{12,20},{13,21},{14,22},{15,23},{16,... | collective-permute-start | bytes 3145736 | tf_op jit(solution)/shard_map/ppermute | solution.py:949
  233.1 29.5 %collective-permute-start.31 = (bf16[512,1024]{1,0:T(8,128)(2,1)}, bf16[512,1024]{1,0:T(8,128)(2,1)}, u32[]{:S(2)}, u32[]{:S(2)}) collective-permute-start(bf16[512,1024]{1,0:T(8,128)(2,1)} %collective-permute-done.30.refs_3_), channel_id=1, source_target_pairs={{8,0},{9,1},{10,2},{11,3},{12,4},{13,5},{14,6},{15,7},{16,24},{17,... | collective-permute-start | bytes 3145736 | tf_op jit(solution)/shard_map/ppermute | solution.py:949
  234.4 29.0 %collective-permute-start.32 = (bf16[512,1024]{1,0:T(8,128)(2,1)}, bf16[512,1024]{1,0:T(8,128)(2,1)}, u32[]{:S(2)}, u32[]{:S(2)}) collective-permute-start(bf16[512,1024]{1,0:T(8,128)(2,1)} %get-tuple-element.340), channel_id=1, source_target_pairs={{0,8},{1,9},{2,10},{3,11},{4,12},{5,13},{6,14},{7,15},{24,16},{25,... | collective-permute-start | bytes 3145736 | tf_op jit(solution)/shard_map/ppermute | solution.py:949
  263.3 45.8 %collective-permute-start.33 = (bf16[256,2048]{1,0:T(8,128)(2,1)}, bf16[256,2048]{1,0:T(8,128)(2,1)}, u32[]{:S(2)}, u32[]{:S(2)}) collective-permute-start(bf16[256,2048]{1,0:T(8,128)(2,1)} %collective-permute-done.12.refs_2_), channel_id=1, source_target_pairs={{8,0},{9,1},{10,2},{11,3},{12,4},{13,5},{14,6},{15,7},{16,24},{17,... | collective-permute-start | bytes 3145736 | tf_op jit(solution)/shard_map/ppermute | solution.py:949
  264.6 44.5 %collective-permute-start.34 = (bf16[512,1024]{1,0:T(8,128)(2,1)S(1)}, bf16[512,1024]{1,0:T(8,128)(2,1)}, u32[]{:S(2)}, u32[]{:S(2)}) collective-permute-start(bf16[512,1024]{1,0:T(8,128)(2,1)S(1)} %copy-done.41), channel_id=1, source_target_pairs={{0,8},{1,9},{2,10},{3,11},{4,12},{5,13},{6,14},{7,15},{24,16},{25,... | collective-permute-start | bytes 3145736 | tf_op jit(solution)/shard_map/ppermute | solution.py:949
  274.0 35.1 %collective-permute-start.35 = (bf16[512,1024]{1,0:T(8,128)(2,1)}, bf16[512,1024]{1,0:T(8,128)(2,1)}, u32[]{:S(2)}, u32[]{:S(2)}) collective-permute-start(bf16[512,1024]{1,0:T(8,128)(2,1)} %add_convert_fusion.8), channel_id=1, source_target_pairs={{8,16},{9,17},{10,18},{11,19},{12,20},{13,21},{14,22},{15,23},{16,... | collective-permute-start | bytes 3145736 | tf_op jit(solution)/shard_map/ppermute | solution.py:949
  310.5 26.0 %collective-permute-start.37 = (bf16[256,2048]{1,0:T(8,128)(2,1)}, bf16[256,2048]{1,0:T(8,128)(2,1)}, u32[]{:S(2)}, u32[]{:S(2)}) collective-permute-start(bf16[256,2048]{1,0:T(8,128)(2,1)} %get-tuple-element.365), channel_id=1, source_target_pairs={{0,8},{1,9},{2,10},{3,11},{4,12},{5,13},{6,14},{7,15},{24,16},{25,... | collective-permute-start | bytes 3145736 | tf_op jit(solution)/shard_map/ppermute | solution.py:949
  339.8 39.4 %collective-permute-start.39 = (bf16[512,1024]{1,0:T(8,128)(2,1)}, bf16[512,1024]{1,0:T(8,128)(2,1)}, u32[]{:S(2)}, u32[]{:S(2)}) collective-permute-start(bf16[512,1024]{1,0:T(8,128)(2,1)} %add_convert_fusion.6), channel_id=1, source_target_pairs={{0,8},{1,9},{2,10},{3,11},{4,12},{5,13},{6,14},{7,15},{8,0},{9,1},... | collective-permute-start | bytes 3145736 | tf_op jit(solution)/shard_map/ppermute | solution.py:949
  348.6 30.5 %collective-permute-start.40 = (bf16[256,2048]{1,0:T(8,128)(2,1)}, bf16[256,2048]{1,0:T(8,128)(2,1)}, u32[]{:S(2)}, u32[]{:S(2)}) collective-permute-start(bf16[256,2048]{1,0:T(8,128)(2,1)} %add_convert_fusion.5), channel_id=1, source_target_pairs={{8,16},{9,17},{10,18},{11,19},{12,20},{13,21},{14,22},{15,23},{16,... | collective-permute-start | bytes 3145736 | tf_op jit(solution)/shard_map/ppermute | solution.py:949
  379.2 33.7 %collective-permute-start.41 = (bf16[512,1024]{1,0:T(8,128)(2,1)}, bf16[512,1024]{1,0:T(8,128)(2,1)}, u32[]{:S(2)}, u32[]{:S(2)}) collective-permute-start(bf16[512,1024]{1,0:T(8,128)(2,1)} %get-tuple-element.400), channel_id=1, source_target_pairs={{0,8},{1,9},{2,10},{3,11},{4,12},{5,13},{6,14},{7,15},{24,16},{25,... | collective-permute-start | bytes 3145736 | tf_op jit(solution)/shard_map/ppermute | solution.py:949
  413.4 31.6 %collective-permute-start.43 = (bf16[512,1024]{1,0:T(8,128)(2,1)}, bf16[512,1024]{1,0:T(8,128)(2,1)}, u32[]{:S(2)}, u32[]{:S(2)}) collective-permute-start(bf16[512,1024]{1,0:T(8,128)(2,1)} %get-tuple-element.419), channel_id=1, source_target_pairs={{0,8},{1,9},{2,10},{3,11},{4,12},{5,13},{6,14},{7,15},{24,16},{25,... | collective-permute-start | bytes 3145736 | tf_op jit(solution)/shard_map/ppermute | solution.py:949
  418.6 26.4 %collective-permute-start.44 = (bf16[512,1024]{1,0:T(8,128)(2,1)}, bf16[512,1024]{1,0:T(8,128)(2,1)}, u32[]{:S(2)}, u32[]{:S(2)}) collective-permute-start(bf16[512,1024]{1,0:T(8,128)(2,1)} %add_convert_fusion.4), channel_id=1, source_target_pairs={{8,16},{9,17},{10,18},{11,19},{12,20},{13,21},{14,22},{15,23},{16,... | collective-permute-start | bytes 3145736 | tf_op jit(solution)/shard_map/ppermute | solution.py:949
  455.8 35.2 %collective-permute-start.54 = (bf16[256,2048]{1,0:T(8,128)(2,1)S(1)}, bf16[256,2048]{1,0:T(8,128)(2,1)S(1)}, u32[]{:S(2)}, u32[]{:S(2)}) collective-permute-start(bf16[256,2048]{1,0:T(8,128)(2,1)S(1)} %get-tuple-element.439), channel_id=1, source_target_pairs={{0,1},{1,0},{2,3},{3,2},{4,5},{5,4},{6,7},{7,6},{8,9},{9,8},{10,11... | collective-permute-start | bytes 3145736 | tf_op jit(solution)/shard_map/ppermute | solution.py:942
  473.1 30.3 %collective-permute-start.55 = (bf16[256,2048]{1,0:T(8,128)(2,1)S(1)}, bf16[256,2048]{1,0:T(8,128)(2,1)S(1)}, u32[]{:S(2)}, u32[]{:S(2)}) collective-permute-start(bf16[256,2048]{1,0:T(8,128)(2,1)S(1)} %get-tuple-element.440), channel_id=1, source_target_pairs={{0,2},{1,3},{2,0},{3,1},{4,6},{5,7},{6,4},{7,5},{8,10},{9,11},{10,... | collective-permute-start | bytes 3145736 | tf_op jit(solution)/shard_map/ppermute | solution.py:942
  473.5 33.0 %collective-permute-start.53 = (bf16[256,2048]{1,0:T(8,128)(2,1)S(1)}, bf16[256,2048]{1,0:T(8,128)(2,1)S(1)}, u32[]{:S(2)}, u32[]{:S(2)}) collective-permute-start(bf16[256,2048]{1,0:T(8,128)(2,1)S(1)} %copy-done.38), channel_id=1, source_target_pairs={{0,8},{1,9},{2,10},{3,11},{4,12},{5,13},{6,14},{7,15},{24,16},{25,... | collective-permute-start | bytes 3145736 | tf_op jit(solution)/shard_map/ppermute | solution.py:949
  509.2 28.1 %collective-permute-start.59 = (bf16[256,2048]{1,0:T(8,128)(2,1)}, bf16[256,2048]{1,0:T(8,128)(2,1)}, u32[]{:S(2)}, u32[]{:S(2)}) collective-permute-start(bf16[256,2048]{1,0:T(8,128)(2,1)} %add_convert_fusion.1), channel_id=1, source_target_pairs={{0,8},{1,9},{2,10},{3,11},{4,12},{5,13},{6,14},{7,15},{8,0},{9,1},... | collective-permute-start | bytes 3145736 | tf_op jit(solution)/shard_map/ppermute | solution.py:949
  511.1 26.3 %collective-permute-start.60 = (bf16[256,2048]{1,0:T(8,128)(2,1)}, bf16[256,2048]{1,0:T(8,128)(2,1)}, u32[]{:S(2)}, u32[]{:S(2)}) collective-permute-start(bf16[256,2048]{1,0:T(8,128)(2,1)} %add_convert_fusion), channel_id=1, source_target_pairs={{8,16},{9,17},{10,18},{11,19},{12,20},{13,21},{14,22},{15,23},{16,... | collective-permute-start | bytes 3145736 | tf_op jit(solution)/shard_map/ppermute | solution.py:949
  (102 other events, 1482.9 us)

commit v4 on v3

--- a/solution.py
+++ b/solution.py
@@ -338,9 +338,17 @@
     prior, refs = ((), refs) if merge else (refs[:4], refs[6:])
     (context, d_packed, *grads), refs = refs[:6], refs[6:]
     if merge:
-        qkv_w, dense_w, sum_qkv, sum_dense, sems = refs
+        joined, (sum_qkv, sum_dense, held, out_sems, qkv_w, dense_w, sems) = refs[:2], refs[2:]
+        kept = [
+            pltpu.make_async_copy(source, target, out_sems.at[4 + i])
+            for i, (source, target) in enumerate(zip((qkv_w, dense_w), joined))
+        ]
     else:
-        (qkv_w, dense_w), (sum_qkv, sum_dense) = weights, refs
+        (qkv_w, dense_w), (sum_qkv, sum_dense, held, out_sems, before) = weights, refs
+        kept = [
+            pltpu.make_async_copy(source, before.at[i], out_sems.at[4 + i])
+            for i, source in enumerate(prior)
+        ]
     step = pl.program_id(0)
     wide = dense_w.shape[0]
     scaling = 1.0 / math.sqrt(HEAD_DIM)
@@ -365,6 +373,11 @@
                 ]
 
             copy_pieces(where, weights, of, sems)
+
+    @pl.when(step == 0)
+    def _():
+        for copy in kept:
+            copy.start()
 
     c = jnp.tile(cosine[...], (1, wide // 128))
     sa = jnp.tile(sine_a[...], (1, wide // 128))
@@ -401,8 +414,8 @@
             d_scores = (probs * (nt(g, v) - delta)).astype(BF16)
             d_q.append(nn(d_scores, k) * scaling)
             d_k.append(tn(d_scores, q))
-        for held, new in ((all_out, out), (all_q, d_q), (all_k, d_k), (all_v, d_v)):
-            held.append(jnp.concatenate(new, axis=1))
+        for rows_of_all, new in ((all_out, out), (all_q, d_q), (all_k, d_k), (all_v, d_v)):
+            rows_of_all.append(jnp.concatenate(new, axis=1))
     context[...] = jnp.concatenate(all_out, axis=0).astype(BF16)
     d_packed[:, :wide] = turn(jnp.concatenate(all_q, axis=0), -1.0).astype(BF16)
     d_packed[:, wide : 2 * wide] = turn(jnp.concatenate(all_k, axis=0), -1.0).astype(BF16)
@@ -418,16 +431,19 @@
 
     @pl.when(step == pl.num_programs(0) - 1)
     def _():
-        for at, (out, (place, plane)) in enumerate(zip(grads, places(where))):
+        for copy in kept:
+            copy.wait()
+
+        def value(at, place, plane):
             summed = sum_qkv[pl.ds(multiple(place, block), block), :]
             beside = sum_dense[pl.ds(multiple(plane, own), own), :]
             beside = jnp.concatenate(
                 [beside[:, j * across : (j + 1) * across] for j in range(parts)], axis=0
             )
             total = jnp.concatenate([summed, beside], axis=1)
-            if prior:
-                total += prior[at][...].astype(F32)
-            out[...] = total.astype(BF16)
+            return total + before[at].astype(F32) if prior else total
+
+        write_blocks(where, value, grads, held, out_sems)
 
 
 def attention(where, run, parts, hidden, cot, weights, streams, prior, filled):
@@ -455,13 +471,21 @@
             + ([ANYWHERE] * 6 if merge else [whole(array) for array in weights])
             + [whole(bias)]
             + [rows_of_run(array.shape[1]) for array in streams[1:]]
-            + [whole(array) for array in prior]
-            + [ANYWHERE for _ in filled],
+            + [ANYWHERE for _ in (*prior, *filled)],
             out_specs=[rows_of_run(wide), rows_of_run(3 * wide)]
-            + [fixed(grad.shape)] * 4
-            + [fixed(array.shape) for array in joined],
-            scratch_shapes=[pltpu.VMEM((width, 3 * wide), F32), pltpu.VMEM((wide, width), F32)]
-            + ([pltpu.SemaphoreType.DMA((4 * (1 + parts),))] if merge else []),
+            + [ANYWHERE] * (4 + len(joined)),
+            scratch_shapes=[
+                pltpu.VMEM((width, 3 * wide), F32),
+                pltpu.VMEM((wide, width), F32),
+                pltpu.VMEM((4,) + grad.shape, BF16),
+                pltpu.SemaphoreType.DMA((8,)),
+            ]
+            + [pltpu.VMEM(array.shape, BF16) for array in joined]
+            + (
+                [pltpu.SemaphoreType.DMA((4 * (1 + parts),))]
+                if merge
+                else [pltpu.VMEM((4,) + grad.shape, BF16)]
+            ),
         ),
         out_shape=[shaped((count, wide)), shaped((count, 3 * wide))] + [grad] * 4 + joined,
         input_output_aliases={first_filled + i: i for i in range(len(filled))},
@@ -475,16 +499,21 @@
 GELU_B = 0.044715
 
 
-def write_blocks(where, total, grads, by_plane):
-    size = grads[0].shape[0]
-    for out, (place, plane) in zip(grads, places(where)):
-        at = multiple(plane if by_plane else place, size)
-        out[...] = total[pl.ds(at, size), :].astype(BF16)
+def write_blocks(where, values, grads, held, sems):
+    copies = []
+    for at, (out, place) in enumerate(zip(grads, places(where))):
+        held[at] = values(at, *place).astype(BF16)
+        copies.append(pltpu.make_async_copy(held.at[at], out, sems.at[at]))
+        copies[-1].start()
+    for copy in copies:
+        copy.wait()
 
 
 def forward_body(columns, where, hidden, cot, *refs):
-    pieces, (bias, active, slope, up_w), (*grads, total, sems) = refs[:6], refs[6:10], refs[10:]
-    step = pl.program_id(0)
+    pieces, (bias, active, slope, joined), refs = refs[:6], refs[6:10], refs[10:]
+    (*grads, total, up_w, held, sems, out_sems) = refs
+    step, last = pl.program_id(0), pl.num_programs(0) - 1
+    join = pltpu.make_async_copy(up_w, joined, out_sems.at[4])
 
     @pl.when(step == 0)
     def _():
@@ -494,6 +523,7 @@
             return [(piece, up_w.at[pl.ds(multiple(place, size), size)])]
 
         copy_pieces(where, pieces, of, sems)
+        join.start()
         total[...] = jnp.zeros_like(total)
 
     for j in range(up_w.shape[1] // columns):
@@ -509,9 +539,15 @@
         ).astype(BF16)
         total[part] += tn(low, cot[...])
 
-    @pl.when(step == pl.num_programs(0) - 1)
+    @pl.when(step == last)
     def _():
-        write_blocks(where, total, grads, True)
+        size = grads[0].shape[0]
+
+        def block(at, place, plane):
+            return total[pl.ds(multiple(plane, size), size), :]
+
+        write_blocks(where, block, grads, held, out_sems)
+        join.wait()
 
 
 def forward(where, hidden, cot, pieces, bias, rows=512, columns=512):
@@ -524,11 +560,16 @@
         [hidden, cot, *pieces, bias],
         [rows_of(hidden, rows), rows_of(cot, rows)] + [ANYWHERE] * 6 + [whole(bias)],
         [pl.BlockSpec((rows, wide), lambda i, _: (i, 0))] * 2
-        + [fixed((width, wide))]
-        + [fixed(grad.shape)] * 4,
+        + [ANYWHERE] * 5,
         [shaped((count, wide))] * 2 + [shaped((width, wide))] + [grad] * 4,
         grid=(count // rows,),
-        scratch=[pltpu.VMEM((wide, width), F32), pltpu.SemaphoreType.DMA((4,))],
+        scratch=[
+            pltpu.VMEM((wide, width), F32),
+            pltpu.VMEM((width, wide), BF16),
+            pltpu.VMEM((4,) + grad.shape, BF16),
+            pltpu.SemaphoreType.DMA((4,)),
+            pltpu.SemaphoreType.DMA((5,)),
+        ],
         work=(4 * count * width * wide, 32 * MIB),
         vmem=VMEM,
     )
@@ -536,8 +577,10 @@
 
 
 def backward_body(where, cot, hidden, *refs):
-    pieces, (slope, d_upward, sums, down_w), (*grads, total, sems) = refs[:6], refs[6:10], refs[10:]
-    step = pl.program_id(0)
+    pieces, (slope, d_upward, sums, joined), refs = refs[:6], refs[6:10], refs[10:]
+    (*grads, total, down_w, held, sems, out_sems) = refs
+    step, last = pl.program_id(0), pl.num_programs(0) - 1
+    join = pltpu.make_async_copy(down_w, joined, out_sems.at[4])
 
     @pl.when(step == 0)
     def _():
@@ -547,6 +590,7 @@
             return [(piece, down_w.at[pl.ds(multiple(plane, size), size)])]
 
         copy_pieces(where, pieces, of, sems)
+        join.start()
         sums[...] = jnp.zeros_like(sums)
         total[...] = jnp.zeros_like(total)
 
@@ -555,9 +599,15 @@
     sums[...] += jnp.sum(low.astype(F32), axis=0, keepdims=True)
     total[...] += tn(hidden[...], low)
 
-    @pl.when(step == pl.num_programs(0) - 1)
+    @pl.when(step == last)
     def _():
-        write_blocks(where, total, grads, False)
+        size = grads[0].shape[0]
+
+        def block(at, place, plane):
+            return total[pl.ds(multiple(place, size), size), :]
+
+        write_blocks(where, block, grads, held, out_sems)
+        join.wait()
 
 
 def backward(where, cot, hidden, pieces, slope, rows=256):
@@ -572,12 +622,17 @@
         [
             pl.BlockSpec((rows, wide), lambda i, _: (i, 0)),
             pl.BlockSpec((1, wide), lambda i, _: (0, 0)),
-            fixed((wide, width)),
         ]
-        + [fixed(grad.shape)] * 4,
+        + [ANYWHERE] * 5,
         [shaped((count, wide)), shaped((1, wide), F32), shaped((wide, width))] + [grad] * 4,
         grid=(count // rows,),
-        scratch=[pltpu.VMEM((width, wide), F32), pltpu.SemaphoreType.DMA((4,))],
+        scratch=[
+            pltpu.VMEM((width, wide), F32),
+            pltpu.VMEM((wide, width), BF16),
+            pltpu.VMEM((4,) + grad.shape, BF16),
+            pltpu.SemaphoreType.DMA((4,)),
+            pltpu.SemaphoreType.DMA((5,)),
+        ],
         work=(4 * count * width * wide, 32 * MIB),
         vmem=VMEM,
     )
@@ -1014,6 +1069,7 @@
     blocks, table, down_own = tied(deal_second(where, keep, flip(send, chips)), table, down_weight)
     dealt = [blocks[0]] + [flip(blocks[r], r) for r in range(1, chips)]
     w1, w2a = to_neighbour(down_own), over_middle(down_own)
+    table, dealt[1], dealt[2] = tied(table, dealt[1], dealt[2])
     table = over_cores(over_chips(table))
     u_own, a_own = deal_last(where, dealt, dense_weight, planes * ff_block)
     u_own, a_own, table, w1, w2a, cot_own = tied(
@@ -1072,15 +1128,22 @@
     a3b, u2a = outwards(a2b), over_middle(u_own)
     for_x, for_y = pair_halves(where, cot_near, hidden_near)
     corner_y, corner_x = flip(for_x, 1), flip(for_y, 2)
-    cot_most = jnp.concatenate([cot_own, *cot_near], axis=0)
-    hidden_most = jnp.concatenate([hidden_own, *hidden_near], axis=0)
+    room = jnp.zeros((row_count, width), BF16)
+    cot_most = jnp.concatenate([cot_own, *cot_near, room], axis=0)
+    hidden_most = jnp.concatenate([hidden_own, *hidden_near, room], axis=0)
 
     a3b, u2a, corner_x, corner_y, hidden_most, cot_most, u_own, w1, cosine, sine_a, sine_b, first = tied(
         a3b, u2a, corner_x, corner_y, hidden_most, cot_most, u_own, w1, cosine, sine_a, sine_b, first
     )
     u1, w2b = to_neighbour(u_own), over_middle(w1)
-    cot = jnp.concatenate([cot_most, corner_y[:half], corner_x[:half]], axis=0)
-    hidden = jnp.concatenate([hidden_most, corner_y[half:], corner_x[half:]], axis=0)
+    def with_corners(most, at):
+        for i, corner in enumerate((corner_y, corner_x)):
+            most = lax.dynamic_update_slice_in_dim(
+                most, corner[at : at + half], 3 * row_count + i * half, 0
+            )
+        return most
+
+    cot, hidden = with_corners(cot_most, 0), with_corners(hidden_most, half)
     hidden, cot = [hidden, flip(hidden, chips)], [cot, flip(cot, chips)]
     streams = [packed_bias, cosine, sine_a, sine_b, first]
     rows_a, g_a, (qkv_w, dense_w) = attention(
@@ -1112,24 +1175,25 @@
     u3b, q1_a_end, g_a, w2a, hidden, cot, packed_sum, cot_sum = tied(
         u3b, q1_a_end, g_a, w2a, hidden, cot, packed_sum, cot_sum
     )
-    w3a, q1_a_mid, q2_a_end = outwards(w2a), inwards(g_a[2]), over_middle(add(g_a[3], q1_a_end))
+    w3a, q1_a_mid = outwards(w2a), inwards(g_a[2])
     active, slope, up_w, g_w = forward(
         where, hidden, cot, [u_own, u1, u2a, u2b, u3a, u3b], upward_bias
     )
 
-    w3a, q1_a_mid, q2_a_end, g_a, g_w, w2b = tied(w3a, q1_a_mid, q2_a_end, g_a, g_w, w2b)
-    w3b, q1_w_end, q2_a_mid = outwards(w2b), inwards(g_w[3]), over_middle(add(g_a[2], q1_a_mid))
-
-    w3b, q1_w_end, q2_a_mid, q2_a_end, g_a, g_w, cot = tied(
-        w3b, q1_w_end, q2_a_mid, q2_a_end, g_a, g_w, cot
-    )
-    q3_a, q2_w_end = to_neighbour(add(g_a[1], q2_a_end)), over_middle(add(g_w[3], q1_w_end))
+    w3a, q1_a_mid, q1_a_end, g_a, g_w, w2b = tied(w3a, q1_a_mid, q1_a_end, g_a, g_w, w2b)
+    w3b, q1_w_end, q2_a_end = outwards(w2b), inwards(g_w[3]), over_middle(add(g_a[3], q1_a_end))
+    share_a_mid = add(g_a[2], q1_a_mid)
+
+    w3b, q1_w_end, q2_a_end, share_a_mid, g_a, g_w, cot = tied(
+        w3b, q1_w_end, q2_a_end, share_a_mid, g_a, g_w, cot
+    )
+    q3_a, q2_a_mid = to_neighbour(add(g_a[1], q2_a_end)), over_middle(share_a_mid)
     d_upward, upward_sum, down_w, g_u = backward(
         where, cot, hidden, [down_own, w1, w2a, w2b, w3a, w3b], slope
     )
 
-    q3_a, q2_w_end, g_w, g_u, d_upward, q2_a_mid, upward_sum = tied(
-        q3_a, q2_w_end, g_w, g_u, d_upward, q2_a_mid, upward_sum
+    q3_a, q2_a_mid, g_w, g_u, d_upward, upward_sum = tied(
+        q3_a, q2_a_mid, g_w, g_u, d_upward, upward_sum
     )
     q1_u_end = inwards(g_u[3])
     d_hidden_far, d_hidden_near = two_dots(nt, d_packed, qkv_w, d_upward, up_w, width)
@@ -1156,10 +1220,10 @@
     out_extra_y, out_extra_x = flip(corner_y, 1), flip(corner_x, 2)
     blocks = deal_second(where, keep, came)
 
-    q3_u, q2_u_mid, out_extra_x, out_extra_y, g_u, g_w, blocks = tied(
-        q3_u, q2_u_mid, out_extra_x, out_extra_y, g_u, g_w, blocks
-    )
-    q1_w_mid = inwards(g_w[2])
+    q3_u, q2_u_mid, out_extra_x, out_extra_y, g_u, g_w, q1_w_end, blocks = tied(
+        q3_u, q2_u_mid, out_extra_x, out_extra_y, g_u, g_w, q1_w_end, blocks
+    )
+    q1_w_mid, q2_w_end = inwards(g_w[2]), over_middle(add(g_w[3], q1_w_end))
     for_x, for_y = sides(where, d_hidden_near, d_hidden_came, extra_y, extra_x, 0)
     d_hidden_last = flip(for_x, 1), flip(for_y, 2)
     block_x, block_y, block_xy = [flip(blocks[r], r) for r in range(1, chips)]
@@ -1214,6 +1278,7 @@
         axis=1,
     )
 
+    sums = over_cores(sums)
     q3_w, q2_w_mid, g_w, out_last, sums, held = tied(q3_w, q2_w_mid, g_w, out_last, sums, held)
     received = [flip(held[r], r) for r in range(1, chips)]
     for r in (1, 2):
@@ -1225,7 +1290,7 @@
     received, sums, grad_qkv_w, output, grad_down_w = tied(
         received, sums, grad_qkv_w, output, grad_down_w
     )
-    sums = over_cores(over_chips(sums))
+    sums = over_chips(sums)
     grad_up_w = back(where, [held[0]] + received, planes)
     total = lax.dynamic_index_in_dim(sums, rank, 0, keepdims=False)
     grad_gain, grad_shift, grad_out_b, grad_packed_b, grad_up_b = jnp.split(

time: 574 us -> 555 us (0.967)
  waiting for transfers between devices: 141 us -> 128 us
    ppermute x38, waiting for transfers between devices: 51.5 us -> 41.7 us  [flip(): lax.ppermute(value, AXES, [(p * mates + i, p * mates + (i ^ r)) for p in...]
    unnamed x110 -> x100, local copies, waits for them, and re-layouts: 21.3 us -> 18.6 us
  transfers between devices with their start and end apart: 73 -> 73, of which waited for: 31 -> 28; matrix products, arithmetic and copies ran while one was open for 13% -> 13% of each run, Pallas kernels for 35% -> 35%
where the time goes in v4:
time: 555 us; the launch traced here: 548 us
  Pallas kernels  197 us (35%)
  waiting for transfers between devices  128 us (23%)
  starting transfers between devices  120 us (22%)
  other arithmetic  66.8 us (12%)
  local copies, waits for them, and re-layouts  33.8 us (6%)
    pallas_call x17, Pallas kernels, kernel(): pl.pallas_call(body, grid_spec=pltpu.PrefetchScalarGridSpec(num_scalar_pr...  90.4 us
    ppermute x35, waiting for transfers between devices, between(): lax.ppermute(value, AXES, [(p * mates + i, q * mates + i) for p, q in pai...  86.5 us
    ppermute x35, starting transfers between devices, between(): lax.ppermute(value, AXES, [(p * mates + i, q * mates + i) for p, q in pai...  84.9 us
    pallas_call x2, Pallas kernels, attention(): pl.pallas_call(functools.partial(attention_body, parts, run, merge), grid...  66.8 us
    ppermute x38, waiting for transfers between devices, flip(): lax.ppermute(value, AXES, [(p * mates + i, p * mates + (i ^ r)) for p in...  41.7 us
    pallas_call x2, Pallas kernels, two_dots(): pl.pallas_call(functools.partial(two_dots_body, dot), grid=(steps,), in_s...  40.1 us
    ppermute x38, starting transfers between devices, flip(): lax.ppermute(value, AXES, [(p * mates + i, p * mates + (i ^ r)) for p in...  35 us
    convert_element_type x9, other arithmetic, add(): return added(*terms).astype(dtype)  19.2 us
  transfers between devices with their start and end apart: 73, of which 28 were waited for; matrix products, arithmetic and copies ran while one was open for 13% of the time, Pallas kernels for 35%

profile of v4, /device:TPU:0, one launch (start us, length us, event | category | flops | bytes accessed | tf_op | source)
XLA Modules:
  0.0 548.1 jit_solution(2036195461296826676)
XLA Ops:
  30.4 5.2 collective-permute-done.4.refs_1_
  63.9 18.6 %collective-permute-done.13.refs_3_ = bf16[512,1024]{1,0:T(8,128)(2,1)} collective-permute-done((bf16[512,1024]{1,0:T(8,128)(2,1)}, bf16[512,1024]{1,0:T(8,128)(2,1)}, u32[]{:S(2)}, u32[]{:S(2)}) %collective-permute-start.13) | collective-permute-done | bytes 1048608 | tf_op jit(solution)/shard_map/ppermute | solution.py:1004
  91.2 23.8 %collective-permute-done.17.refs_6_ = bf16[512,1024]{1,0:T(8,128)(2,1)} collective-permute-done((bf16[512,1024]{1,0:T(8,128)(2,1)}, bf16[512,1024]{1,0:T(8,128)(2,1)}, u32[]{:S(2)}, u32[]{:S(2)}) %collective-permute-start.17) | collective-permute-done | bytes 1048608 | tf_op jit(solution)/shard_map/ppermute | solution.py:1004
  121.9 5.8 %fusion.8 = (f32[2048,128]{1,0:T(8,128)}, f32[2048,128]{1,0:T(8,128)}, f32[2048,128]{1,0:T(8,128)}) fusion(f32[128]{0:T(128)S(1)} %fusion.17, f32[2048]{0:T(1024)S(1)} %subtract_convert_fusion, pred[128]{0:T(512)(128)(4,1)S(1)} %get-tuple-element.538, pred[128]{0:T(512)(128)(4,1)S(1)} %get-tuple-element.539, pred[128]{0:T(512)(128)(4,1)S(1)} %broadcast_compare_fusion.1), kind=kLoop, calls=%fused_computation.29 | loop fusion | flops 1310720 | bytes 3154816 | tf_op jit(solution)/shard_map/jit(_where)/select_n | solution.py:1120
  127.7 5.5 %maximum_maximum_fusion.1 = (bf16[1024,2048]{1,0:T(8,128)(2,1)}, bf16[1024,2048]{1,0:T(8,128)(2,1)}) fusion(bf16[256,2048]{1,0:T(8,128)(2,1)} %collective-permute-done.16.refs_0_, bf16[256,2048]{1,0:T(8,128)(2,1)S(1)} %collective-permute-done.15.refs_1_, bf16[256,2048]{1,0:T(8,128)(2,1)S(1)} %copy-done.9, bf16[1024]{0:T(1024)(128)(2,1)S(1)} %pad.16.clone, ...), kind=kLoop, calls=%fused_computation.4 | loop fusion | flops 31457280 | bytes 14682112 | tf_op jit(solution)/shard_map/concatenate | solution.py:1132
  133.2 8.6 %collective-permute-done.21.refs_7_ = bf16[512,1024]{1,0:T(8,128)(2,1)S(1)} collective-permute-done((bf16[512,1024]{1,0:T(8,128)(2,1)}, bf16[512,1024]{1,0:T(8,128)(2,1)S(1)}, u32[]{:S(2)}, u32[]{:S(2)}) %collective-permute-start.21) | collective-permute-done | bytes 1048608 | tf_op jit(solution)/shard_map/ppermute | solution.py:1004
  149.3 6.9 %collective-permute-start.25 = (bf16[512,1024]{1,0:T(8,128)(2,1)S(1)}, bf16[512,1024]{1,0:T(8,128)(2,1)}, u32[]{:S(2)}, u32[]{:S(2)}) collective-permute-start(bf16[512,1024]{1,0:T(8,128)(2,1)S(1)} %copy-done.32), channel_id=1, source_target_pairs={{0,8},{1,9},{2,10},{3,11},{4,12},{5,13},{6,14},{7,15},{8,0},{9,1},... | collective-permute-start | bytes 3145736 | tf_op jit(solution)/shard_map/ppermute | solution.py:1004
  158.0 34.0 %shard_map.224 = (bf16[2048,256]{1,0:T(8,128)(2,1)}, bf16[2048,768]{1,0:T(8,128)(2,1)}, bf16[512,1024]{1,0:T(8,128)(2,1)}, bf16[512,1024]{1,0:T(8,128)(2,1)}, bf...) custom-call(s32[5]{0:T(128)} %copy-done.27, ...), custom_call_target="tpu_custom_call" | custom-call | flops 17999998976 | bytes 20971520 | tf_op jit(solution)/shard_map/pallas_call | solution.py:465
  195.6 32.8 %shard_map.225 = (bf16[2048,256]{1,0:T(8,128)(2,1)}, bf16[2048,768]{1,0:T(8,128)(2,1)}, bf16[512,1024]{1,0:T(8,128)(2,1)}, bf16[512,1024]{1,0:T(8,128)(2,1)}, bf...) custom-call(s32[5]{0:T(128)} %copy-done.27, ...), custom_call_target="tpu_custom_call", output_to_operand_aliasing={{0}: (14, {}), {1}: (15, {})} | custom-call | flops 17999998976 | bytes 20971520 | tf_op jit(solution)/shard_map/pallas_call | solution.py:465
  229.7 7.3 %collective-permute-start.32 = (bf16[512,1024]{1,0:T(8,128)(2,1)}, bf16[512,1024]{1,0:T(8,128)(2,1)}, u32[]{:S(2)}, u32[]{:S(2)}) collective-permute-start(bf16[512,1024]{1,0:T(8,128)(2,1)} %get-tuple-element.366), channel_id=1, source_target_pairs={{0,8},{1,9},{2,10},{3,11},{4,12},{5,13},{6,14},{7,15},{24,16},{25,... | collective-permute-start | bytes 3145736 | tf_op jit(solution)/shard_map/ppermute | solution.py:1004
  240.3 8.5 %pad_maximum_fusion.hidden = bf16[2048,2048]{1,0:T(8,128)(2,1)} fusion(bf16[1024,2048]{1,0:T(8,128)(2,1)} %collective-permute-done.27.refs_0_, bf16[1024,2048]{1,0:T(8,128)(2,1)} %get-tuple-element.344.refs_0_), kind=kLoop, calls=%fused_computation | loop fusion | flops 16777216 | bytes 16777216 | tf_op jit(solution)/shard_map/concatenate | solution.py:1169
  248.8 8.5 %pad_maximum_fusion.1.cot = bf16[2048,2048]{1,0:T(8,128)(2,1)} fusion(bf16[1024,2048]{1,0:T(8,128)(2,1)} %collective-permute-done.28.refs_1_, bf16[1024,2048]{1,0:T(8,128)(2,1)} %get-tuple-element.346.refs_1_), kind=kLoop, calls=%fused_computation.1 | loop fusion | flops 16777216 | bytes 16777216 | tf_op jit(solution)/shard_map/concatenate | solution.py:1169
  259.4 6.6 %collective-permute-start.34 = (bf16[512,1024]{1,0:T(8,128)(2,1)S(1)}, bf16[512,1024]{1,0:T(8,128)(2,1)}, u32[]{:S(2)}, u32[]{:S(2)}) collective-permute-start(bf16[512,1024]{1,0:T(8,128)(2,1)S(1)} %copy-done.40), channel_id=1, source_target_pairs={{0,8},{1,9},{2,10},{3,11},{4,12},{5,13},{6,14},{7,15},{24,16},{25,... | collective-permute-start | bytes 3145736 | tf_op jit(solution)/shard_map/ppermute | solution.py:1004
  266.0 32.4 %shard_map.226 = (bf16[2048,1024]{1,0:T(8,128)(2,1)}, bf16[2048,1024]{1,0:T(8,128)(2,1)}, bf16[2048,1024]{1,0:T(8,128)(2,1)}, bf16[256,2048]{1,0:T(8,128)(2,1)},...) custom-call(s32[5]{0:T(128)} %copy-done.27, ...), custom_call_target="tpu_custom_call" | custom-call | flops 17179869184 | bytes 33554432 | tf_op jit(solution)/shard_map/pallas_call | solution.py:260
  299.8 5.6 %collective-permute-start.36 = (bf16[256,2048]{1,0:T(8,128)(2,1)}, bf16[256,2048]{1,0:T(8,128)(2,1)S(1)}, u32[]{:S(2)}, u32[]{:S(2)}) collective-permute-start(bf16[256,2048]{1,0:T(8,128)(2,1)} %get-tuple-element.451), channel_id=1, source_target_pairs={{0,8},{1,9},{2,10},{3,11},{4,12},{5,13},{6,14},{7,15},{24,16},{25,... | collective-permute-start | bytes 3145736 | tf_op jit(solution)/shard_map/ppermute | solution.py:1004
  313.0 10.6 %collective-permute-done.35.refs_5_ = bf16[256,2048]{1,0:T(8,128)(2,1)} collective-permute-done((bf16[256,2048]{1,0:T(8,128)(2,1)}, bf16[256,2048]{1,0:T(8,128)(2,1)}, u32[]{:S(2)}, u32[]{:S(2)}) %collective-permute-start.35) | collective-permute-done | bytes 1048608 | tf_op jit(solution)/shard_map/ppermute | solution.py:1004
  329.1 6.3 %collective-permute-start.38 = (bf16[512,1024]{1,0:T(8,128)(2,1)}, bf16[512,1024]{1,0:T(8,128)(2,1)}, u32[]{:S(2)}, u32[]{:S(2)}) collective-permute-start(bf16[512,1024]{1,0:T(8,128)(2,1)} %add_convert_fusion.6), channel_id=1, source_target_pairs={{0,8},{1,9},{2,10},{3,11},{4,12},{5,13},{6,14},{7,15},{8,0},{9,1},... | collective-permute-start | bytes 3145736 | tf_op jit(solution)/shard_map/ppermute | solution.py:1004
  337.1 27.8 %shard_map.227 = (bf16[2048,1024]{1,0:T(8,128)(2,1)}, f32[1,1024]{1,0:T(1,128)}, bf16[1024,2048]{1,0:T(8,128)(2,1)}, bf16[512,1024]{1,0:T(8,128)(2,1)}, bf16[512...) custom-call(s32[5]{0:T(128)} %copy-done.27, bf16[2048,2048]{1,0:T(8,128)(2,1)} %pad_maximum_fusion.1.cot, ...), custom_call_target="tpu_custom_call" | custom-call | flops 17179869184 | bytes 33554432 | tf_op jit(solution)/shard_map/pallas_call | solution.py:260
  373.6 22.7 %shard_map.228 = (bf16[1024,2048]{1,0:T(8,128)(2,1)}, bf16[1024,2048]{1,0:T(8,128)(2,1)}) custom-call(bf16[2048,768]{1,0:T(8,128)(2,1)} %get-tuple-element.348.a, bf16[2048,768]{1,0:T(8,128)(2,1)} %get-tuple-element.322.refs_2_.aw, bf16[2048,1024]{1,0:T(8,128)(2,1)} %get-tuple-element.393.b, bf16[2048,1024]{1,0:T(8,128)(2,1)} %get-tuple-element.394.bw), custom_call_target="tpu_custom_call" | custom-call | flops 15032385536 | bytes 23068672 | tf_op jit(solution)/shard_map/pallas_call | solution.py:664
  412.1 17.4 %shard_map.231 = (bf16[1024,2048]{1,0:T(8,128)(2,1)}, bf16[1024,2048]{1,0:T(8,128)(2,1)}) custom-call(bf16[2048,256]{1,0:T(8,128)(2,1)} %get-tuple-element.418.a, bf16[256,2048]{1,0:T(8,128)(2,1)} %get-tuple-element.323.refs_3_.aw, bf16[2048,1024]{1,0:T(8,128)(2,1)} %get-tuple-element.419.b, bf16[1024,2048]{1,0:T(8,128)(2,1)} %get-tuple-element.420.bw), custom_call_target="tpu_custom_call" | custom-call | flops 10737418240 | bytes 18874368 | tf_op jit(solution)/shard_map/pallas_call | solution.py:664
  443.2 14.4 %collective-permute-done.47.last = bf16[512,1024]{1,0:T(8,128)(2,1)S(1)} collective-permute-done((bf16[512,1024]{1,0:T(8,128)(2,1)S(1)}, bf16[512,1024]{1,0:T(8,128)(2,1)S(1)}, u32[]{:S(2)}, u32[]{:S(2)}) %collective-permute-start.47) | collective-permute-done | bytes 1048608 | tf_op jit(solution)/shard_map/ppermute | solution.py:1004
  459.0 6.4 %collective-permute-start.52 = (bf16[256,2048]{1,0:T(8,128)(2,1)S(1)}, bf16[256,2048]{1,0:T(8,128)(2,1)S(1)}, u32[]{:S(2)}, u32[]{:S(2)}) collective-permute-start(bf16[256,2048]{1,0:T(8,128)(2,1)S(1)} %copy-done.35), channel_id=1, source_target_pairs={{0,8},{1,9},{2,10},{3,11},{4,12},{5,13},{6,14},{7,15},{24,16},{25,... | collective-permute-start | bytes 3145736 | tf_op jit(solution)/shard_map/ppermute | solution.py:1004
  467.3 9.2 %collective-permute-done.54.by_x = bf16[256,2048]{1,0:T(8,128)(2,1)S(1)} collective-permute-done((bf16[256,2048]{1,0:T(8,128)(2,1)S(1)}, bf16[256,2048]{1,0:T(8,128)(2,1)S(1)}, u32[]{:S(2)}, u32[]{:S(2)}) %collective-permute-start.54) | collective-permute-done | bytes 1048608 | tf_op jit(solution)/shard_map/ppermute | solution.py:997
  477.2 6.4 %collective-permute-done.55.by_y = bf16[256,2048]{1,0:T(8,128)(2,1)S(1)} collective-permute-done((bf16[256,2048]{1,0:T(8,128)(2,1)S(1)}, bf16[256,2048]{1,0:T(8,128)(2,1)S(1)}, u32[]{:S(2)}, u32[]{:S(2)}) %collective-permute-start.55) | collective-permute-done | bytes 1048608 | tf_op jit(solution)/shard_map/ppermute | solution.py:997
  (327 shorter events, 214.9 us)
Async XLA Ops:
  28.3 27.4 %collective-permute-start.11 = (bf16[256,2048]{1,0:T(8,128)(2,1)}, bf16[256,2048]{1,0:T(8,128)(2,1)}, u32[]{:S(2)}, u32[]{:S(2)}) collective-permute-start(bf16[256,2048]{1,0:T(8,128)(2,1)} %refs_0_), channel_id=1, source_target_pairs={{0,8},{1,9},{2,10},{3,11},{4,12},{5,13},{6,14},{7,15},{8,0},{9,1},... | collective-permute-start | bytes 3145736 | tf_op jit(solution)/shard_map/ppermute | solution.py:1004
  28.6 27.1 %collective-permute-start.12 = (bf16[256,2048]{1,0:T(8,128)(2,1)}, bf16[256,2048]{1,0:T(8,128)(2,1)}, u32[]{:S(2)}, u32[]{:S(2)}) collective-permute-start(bf16[256,2048]{1,0:T(8,128)(2,1)} %refs_0_), channel_id=1, source_target_pairs={{8,16},{9,17},{10,18},{11,19},{12,20},{13,21},{14,22},{15,23},{16,... | collective-permute-start | bytes 3145736 | tf_op jit(solution)/shard_map/ppermute | solution.py:1004
  55.7 26.8 %collective-permute-start.13 = (bf16[512,1024]{1,0:T(8,128)(2,1)}, bf16[512,1024]{1,0:T(8,128)(2,1)}, u32[]{:S(2)}, u32[]{:S(2)}) collective-permute-start(bf16[512,1024]{1,0:T(8,128)(2,1)} %get-tuple-element.280.refs_2_), channel_id=1, source_target_pairs={{0,8},{1,9},{2,10},{3,11},{4,12},{5,13},{6,14},{7,15},{8,0},{9,1},... | collective-permute-start | bytes 3145736 | tf_op jit(solution)/shard_map/ppermute | solution.py:1004
  86.5 28.6 %collective-permute-start.19 = (bf16[256,2048]{1,0:T(8,128)(2,1)}, bf16[256,2048]{1,0:T(8,128)(2,1)}, u32[]{:S(2)}, u32[]{:S(2)}) collective-permute-start(bf16[256,2048]{1,0:T(8,128)(2,1)} %pad_maximum_fusion.2), channel_id=1, source_target_pairs={{0,1},{1,0},{2,3},{3,2},{4,5},{5,4},{6,7},{7,6},{8,9},{9,8},{10,11... | collective-permute-start | bytes 3145736 | tf_op jit(solution)/shard_map/ppermute | solution.py:997
  87.1 28.0 %collective-permute-start.20 = (bf16[256,2048]{1,0:T(8,128)(2,1)}, bf16[256,2048]{1,0:T(8,128)(2,1)}, u32[]{:S(2)}, u32[]{:S(2)}) collective-permute-start(bf16[256,2048]{1,0:T(8,128)(2,1)} %pad_maximum_fusion.2), channel_id=1, source_target_pairs={{0,2},{1,3},{2,0},{3,1},{4,6},{5,7},{6,4},{7,5},{8,10},{9,11},{10,... | collective-permute-start | bytes 3145736 | tf_op jit(solution)/shard_map/ppermute | solution.py:997
  87.7 27.4 %collective-permute-start.17 = (bf16[512,1024]{1,0:T(8,128)(2,1)}, bf16[512,1024]{1,0:T(8,128)(2,1)}, u32[]{:S(2)}, u32[]{:S(2)}) collective-permute-start(bf16[512,1024]{1,0:T(8,128)(2,1)} %collective-permute-done.14.refs_4_), channel_id=1, source_target_pairs={{8,0},{9,1},{10,2},{11,3},{12,4},{13,5},{14,6},{15,7},{16,24},{17,... | collective-permute-start | bytes 3145736 | tf_op jit(solution)/shard_map/ppermute | solution.py:1004
  146.5 45.6 %collective-permute-start.27 = (bf16[1024,2048]{1,0:T(8,128)(2,1)}, bf16[1024,2048]{1,0:T(8,128)(2,1)}, u32[]{:S(2)}, u32[]{:S(2)}) collective-permute-start(bf16[1024,2048]{1,0:T(8,128)(2,1)} %get-tuple-element.344.refs_0_), channel_id=1, source_target_pairs={{0,4},{1,5},{2,6},{3,7},{4,0},{5,1},{6,2},{7,3},{8,12},{9,13},{10,... | collective-permute-start | bytes 12582920 | tf_op jit(solution)/shard_map/ppermute | solution.py:997
  146.5 45.6 %collective-permute-start.28 = (bf16[1024,2048]{1,0:T(8,128)(2,1)}, bf16[1024,2048]{1,0:T(8,128)(2,1)}, u32[]{:S(2)}, u32[]{:S(2)}) collective-permute-start(bf16[1024,2048]{1,0:T(8,128)(2,1)} %get-tuple-element.346.refs_1_), channel_id=1, source_target_pairs={{0,4},{1,5},{2,6},{3,7},{4,0},{5,1},{6,2},{7,3},{8,12},{9,13},{10,... | collective-permute-start | bytes 12582920 | tf_op jit(solution)/shard_map/ppermute | solution.py:997
  149.3 42.8 %collective-permute-start.25 = (bf16[512,1024]{1,0:T(8,128)(2,1)S(1)}, bf16[512,1024]{1,0:T(8,128)(2,1)}, u32[]{:S(2)}, u32[]{:S(2)}) collective-permute-start(bf16[512,1024]{1,0:T(8,128)(2,1)S(1)} %copy-done.32), channel_id=1, source_target_pairs={{0,8},{1,9},{2,10},{3,11},{4,12},{5,13},{6,14},{7,15},{8,0},{9,1},... | collective-permute-start | bytes 3145736 | tf_op jit(solution)/shard_map/ppermute | solution.py:1004
  156.1 36.0 %collective-permute-start.26 = (bf16[256,2048]{1,0:T(8,128)(2,1)}, bf16[256,2048]{1,0:T(8,128)(2,1)}, u32[]{:S(2)}, u32[]{:S(2)}) collective-permute-start(bf16[256,2048]{1,0:T(8,128)(2,1)} %collective-permute-done.11.refs_1_), channel_id=1, source_target_pairs={{8,16},{9,17},{10,18},{11,19},{12,20},{13,21},{14,22},{15,23},{16,... | collective-permute-start | bytes 3145736 | tf_op jit(solution)/shard_map/ppermute | solution.py:1004
  192.1 36.2 %collective-permute-start.29 = (bf16[512,1024]{1,0:T(8,128)(2,1)}, bf16[512,1024]{1,0:T(8,128)(2,1)S(1)}, u32[]{:S(2)}, u32[]{:S(2)}) collective-permute-start(bf16[512,1024]{1,0:T(8,128)(2,1)} %copy-done.45), channel_id=1, source_target_pairs={{8,0},{9,1},{10,2},{11,3},{12,4},{13,5},{14,6},{15,7},{16,24},{17,... | collective-permute-start | bytes 3145736 | tf_op jit(solution)/shard_map/ppermute | solution.py:1004
  193.4 35.0 %collective-permute-start.30 = (bf16[512,1024]{1,0:T(8,128)(2,1)}, bf16[512,1024]{1,0:T(8,128)(2,1)}, u32[]{:S(2)}, u32[]{:S(2)}) collective-permute-start(bf16[512,1024]{1,0:T(8,128)(2,1)} %collective-permute-done.25.refs_1_), channel_id=1, source_target_pairs={{8,16},{9,17},{10,18},{11,19},{12,20},{13,21},{14,22},{15,23},{16,... | collective-permute-start | bytes 3145736 | tf_op jit(solution)/shard_map/ppermute | solution.py:1004
  228.4 28.9 %collective-permute-start.31 = (bf16[512,1024]{1,0:T(8,128)(2,1)}, bf16[512,1024]{1,0:T(8,128)(2,1)}, u32[]{:S(2)}, u32[]{:S(2)}) collective-permute-start(bf16[512,1024]{1,0:T(8,128)(2,1)} %collective-permute-done.30.refs_3_), channel_id=1, source_target_pairs={{8,0},{9,1},{10,2},{11,3},{12,4},{13,5},{14,6},{15,7},{16,24},{17,... | collective-permute-start | bytes 3145736 | tf_op jit(solution)/shard_map/ppermute | solution.py:1004
  229.7 28.4 %collective-permute-start.32 = (bf16[512,1024]{1,0:T(8,128)(2,1)}, bf16[512,1024]{1,0:T(8,128)(2,1)}, u32[]{:S(2)}, u32[]{:S(2)}) collective-permute-start(bf16[512,1024]{1,0:T(8,128)(2,1)} %get-tuple-element.366), channel_id=1, source_target_pairs={{0,8},{1,9},{2,10},{3,11},{4,12},{5,13},{6,14},{7,15},{24,16},{25,... | collective-permute-start | bytes 3145736 | tf_op jit(solution)/shard_map/ppermute | solution.py:1004
  258.1 40.3 %collective-permute-start.33 = (bf16[256,2048]{1,0:T(8,128)(2,1)}, bf16[256,2048]{1,0:T(8,128)(2,1)}, u32[]{:S(2)}, u32[]{:S(2)}) collective-permute-start(bf16[256,2048]{1,0:T(8,128)(2,1)} %collective-permute-done.12.refs_2_), channel_id=1, source_target_pairs={{8,0},{9,1},{10,2},{11,3},{12,4},{13,5},{14,6},{15,7},{16,24},{17,... | collective-permute-start | bytes 3145736 | tf_op jit(solution)/shard_map/ppermute | solution.py:1004
  259.4 39.0 %collective-permute-start.34 = (bf16[512,1024]{1,0:T(8,128)(2,1)S(1)}, bf16[512,1024]{1,0:T(8,128)(2,1)}, u32[]{:S(2)}, u32[]{:S(2)}) collective-permute-start(bf16[512,1024]{1,0:T(8,128)(2,1)S(1)} %copy-done.40), channel_id=1, source_target_pairs={{0,8},{1,9},{2,10},{3,11},{4,12},{5,13},{6,14},{7,15},{24,16},{25,... | collective-permute-start | bytes 3145736 | tf_op jit(solution)/shard_map/ppermute | solution.py:1004
  329.1 35.8 %collective-permute-start.38 = (bf16[512,1024]{1,0:T(8,128)(2,1)}, bf16[512,1024]{1,0:T(8,128)(2,1)}, u32[]{:S(2)}, u32[]{:S(2)}) collective-permute-start(bf16[512,1024]{1,0:T(8,128)(2,1)} %add_convert_fusion.6), channel_id=1, source_target_pairs={{0,8},{1,9},{2,10},{3,11},{4,12},{5,13},{6,14},{7,15},{8,0},{9,1},... | collective-permute-start | bytes 3145736 | tf_op jit(solution)/shard_map/ppermute | solution.py:1004
  335.4 29.5 %collective-permute-start.39 = (bf16[512,1024]{1,0:T(8,128)(2,1)}, bf16[512,1024]{1,0:T(8,128)(2,1)}, u32[]{:S(2)}, u32[]{:S(2)}) collective-permute-start(bf16[512,1024]{1,0:T(8,128)(2,1)} %add_convert_fusion.7), channel_id=1, source_target_pairs={{8,16},{9,17},{10,18},{11,19},{12,20},{13,21},{14,22},{15,23},{16,... | collective-permute-start | bytes 3145736 | tf_op jit(solution)/shard_map/ppermute | solution.py:1004
  364.9 33.3 %collective-permute-start.40 = (bf16[512,1024]{1,0:T(8,128)(2,1)}, bf16[512,1024]{1,0:T(8,128)(2,1)}, u32[]{:S(2)}, u32[]{:S(2)}) collective-permute-start(bf16[512,1024]{1,0:T(8,128)(2,1)} %get-tuple-element.412), channel_id=1, source_target_pairs={{0,8},{1,9},{2,10},{3,11},{4,12},{5,13},{6,14},{7,15},{24,16},{25,... | collective-permute-start | bytes 3145736 | tf_op jit(solution)/shard_map/ppermute | solution.py:1004
  398.8 30.7 %collective-permute-start.42 = (bf16[512,1024]{1,0:T(8,128)(2,1)}, bf16[512,1024]{1,0:T(8,128)(2,1)}, u32[]{:S(2)}, u32[]{:S(2)}) collective-permute-start(bf16[512,1024]{1,0:T(8,128)(2,1)} %get-tuple-element.432), channel_id=1, source_target_pairs={{0,8},{1,9},{2,10},{3,11},{4,12},{5,13},{6,14},{7,15},{24,16},{25,... | collective-permute-start | bytes 3145736 | tf_op jit(solution)/shard_map/ppermute | solution.py:1004
  441.2 35.3 %collective-permute-start.54 = (bf16[256,2048]{1,0:T(8,128)(2,1)S(1)}, bf16[256,2048]{1,0:T(8,128)(2,1)S(1)}, u32[]{:S(2)}, u32[]{:S(2)}) collective-permute-start(bf16[256,2048]{1,0:T(8,128)(2,1)S(1)} %get-tuple-element.455), channel_id=1, source_target_pairs={{0,1},{1,0},{2,3},{3,2},{4,5},{5,4},{6,7},{7,6},{8,9},{9,8},{10,11... | collective-permute-start | bytes 3145736 | tf_op jit(solution)/shard_map/ppermute | solution.py:997
  459.0 32.7 %collective-permute-start.52 = (bf16[256,2048]{1,0:T(8,128)(2,1)S(1)}, bf16[256,2048]{1,0:T(8,128)(2,1)S(1)}, u32[]{:S(2)}, u32[]{:S(2)}) collective-permute-start(bf16[256,2048]{1,0:T(8,128)(2,1)S(1)} %copy-done.35), channel_id=1, source_target_pairs={{0,8},{1,9},{2,10},{3,11},{4,12},{5,13},{6,14},{7,15},{24,16},{25,... | collective-permute-start | bytes 3145736 | tf_op jit(solution)/shard_map/ppermute | solution.py:1004
  493.0 28.9 %collective-permute-start.59 = (bf16[256,2048]{1,0:T(8,128)(2,1)}, bf16[256,2048]{1,0:T(8,128)(2,1)}, u32[]{:S(2)}, u32[]{:S(2)}) collective-permute-start(bf16[256,2048]{1,0:T(8,128)(2,1)} %add_convert_fusion.1), channel_id=1, source_target_pairs={{0,8},{1,9},{2,10},{3,11},{4,12},{5,13},{6,14},{7,15},{8,0},{9,1},... | collective-permute-start | bytes 3145736 | tf_op jit(solution)/shard_map/ppermute | solution.py:1004
  494.9 27.1 %collective-permute-start.60 = (bf16[256,2048]{1,0:T(8,128)(2,1)}, bf16[256,2048]{1,0:T(8,128)(2,1)}, u32[]{:S(2)}, u32[]{:S(2)}) collective-permute-start(bf16[256,2048]{1,0:T(8,128)(2,1)} %add_convert_fusion), channel_id=1, source_target_pairs={{8,16},{9,17},{10,18},{11,19},{12,20},{13,21},{14,22},{15,23},{16,... | collective-permute-start | bytes 3145736 | tf_op jit(solution)/shard_map/ppermute | solution.py:1004
  (97 other events, 1524.1 us)

commit v5 on v4

--- a/solution.py
+++ b/solution.py
@@ -393,27 +393,38 @@
     keys = turn(packed[:, wide : 2 * wide], 1.0).astype(BF16)
     values = packed[:, 2 * wide :].astype(BF16)
     d_context = nt(cot[...], dense_w[...]).astype(BF16)
-    at = lax.broadcasted_iota(jnp.int32, (run, run), 1)
-    row = lax.broadcasted_iota(jnp.int32, (run, run), 0)
+    half = run // 2
+
+    def attend(q, k, v, g, begin, after):
+        shape = (q.shape[0], k.shape[0])
+        at = lax.broadcasted_iota(jnp.int32, shape, 1)
+        row = lax.broadcasted_iota(jnp.int32, shape, 0) + after
+        starts = first[begin + after : begin + after + q.shape[0], :1]
+        seen = (at >= starts) & (at <= row)
+        scores = jnp.where(seen, nt(q, k), -1e30)
+        raised = jnp.exp(scores - jnp.max(scores, axis=1, keepdims=True))
+        probs = raised * (1.0 / jnp.sum(raised, axis=1, keepdims=True))
+        low = probs.astype(BF16)
+        o = nn(low, v)
+        delta = jnp.sum(o * g.astype(F32), axis=1, keepdims=True)
+        d_scores = (probs * (nt(g, v) - delta)).astype(BF16)
+        return o, nn(d_scores, k) * scaling, tn(d_scores, q), tn(low, g)
+
     all_out, all_q, all_k, all_v = [], [], [], []
     for begin in range(0, hidden.shape[0], run):
         rows = slice(begin, begin + run)
-        seen = (at >= first[rows, :1]) & (at <= row)
         out, d_q, d_k, d_v = [], [], [], []
         for h in range(wide // HEAD_DIM):
             part = slice(h * HEAD_DIM, (h + 1) * HEAD_DIM)
             q, k, v, g = (x[rows, part] for x in (queries, keys, values, d_context))
-            scores = jnp.where(seen, nt(q, k), -1e30)
-            raised = jnp.exp(scores - jnp.max(scores, axis=1, keepdims=True))
-            probs = raised * (1.0 / jnp.sum(raised, axis=1, keepdims=True))
-            low = probs.astype(BF16)
-            o = nn(low, v)
-            out.append(o)
-            d_v.append(tn(low, g))
-            delta = jnp.sum(o * g.astype(F32), axis=1, keepdims=True)
-            d_scores = (probs * (nt(g, v) - delta)).astype(BF16)
-            d_q.append(nn(d_scores, k) * scaling)
-            d_k.append(tn(d_scores, q))
+            upper = attend(q[:half], k[:half], v[:half], g[:half], begin, 0)
+            lower = attend(q[half:], k, v, g[half:], begin, half)
+            out.append(jnp.concatenate([upper[0], lower[0]], axis=0))
+            d_q.append(jnp.concatenate([upper[1], lower[1]], axis=0))
+            for held_back, i in ((d_k, 2), (d_v, 3)):
+                held_back.append(
+                    jnp.concatenate([upper[i] + lower[i][:half], lower[i][half:]], axis=0)
+                )
         for rows_of_all, new in ((all_out, out), (all_q, d_q), (all_k, d_k), (all_v, d_v)):
             rows_of_all.append(jnp.concatenate(new, axis=1))
     context[...] = jnp.concatenate(all_out, axis=0).astype(BF16)

time: 555 us -> 567 us (1.022)
  Pallas kernels: 197 us -> 209 us
    pallas_call x2, Pallas kernels: 66.8 us -> 78.3 us  [attention(): pl.pallas_call(functools.partial(attention_body, parts, run, merge), grid...]
  transfers between devices with their start and end apart: 73 -> 73, of which waited for: 28 -> 28; matrix products, arithmetic and copies ran while one was open for 13% -> 13% of each run, Pallas kernels for 35% -> 36%
where the time goes in v5:
time: 567 us; the launch traced here: 560 us
  Pallas kernels  209 us (37%)
  waiting for transfers between devices  128 us (23%)
  starting transfers between devices  120 us (21%)
  other arithmetic  66.8 us (12%)
  local copies, waits for them, and re-layouts  33.8 us (6%)
    pallas_call x17, Pallas kernels, kernel(): pl.pallas_call(body, grid_spec=pltpu.PrefetchScalarGridSpec(num_scalar_pr...  90.4 us
    ppermute x35, waiting for transfers between devices, between(): lax.ppermute(value, AXES, [(p * mates + i, q * mates + i) for p, q in pai...  86.6 us
    ppermute x35, starting transfers between devices, between(): lax.ppermute(value, AXES, [(p * mates + i, q * mates + i) for p, q in pai...  84.9 us
    pallas_call x2, Pallas kernels, attention(): pl.pallas_call(functools.partial(attention_body, parts, run, merge), grid...  78.3 us
    ppermute x38, waiting for transfers between devices, flip(): lax.ppermute(value, AXES, [(p * mates + i, p * mates + (i ^ r)) for p in...  41.8 us
    pallas_call x2, Pallas kernels, two_dots(): pl.pallas_call(functools.partial(two_dots_body, dot), grid=(steps,), in_s...  40.1 us
    ppermute x38, starting transfers between devices, flip(): lax.ppermute(value, AXES, [(p * mates + i, p * mates + (i ^ r)) for p in...  35 us
    convert_element_type x9, other arithmetic, add(): return added(*terms).astype(dtype)  19.2 us
  transfers between devices with their start and end apart: 73, of which 28 were waited for; matrix products, arithmetic and copies ran while one was open for 13% of the time, Pallas kernels for 36%

profile of v5, /device:TPU:0, one launch (start us, length us, event | category | flops | bytes accessed | tf_op | source)
XLA Modules:
  0.0 559.6 jit_solution(1644604590376893095)
XLA Ops:
  30.4 5.2 collective-permute-done.4.refs_1_
  63.9 18.6 %collective-permute-done.13.refs_3_ = bf16[512,1024]{1,0:T(8,128)(2,1)} collective-permute-done((bf16[512,1024]{1,0:T(8,128)(2,1)}, bf16[512,1024]{1,0:T(8,128)(2,1)}, u32[]{:S(2)}, u32[]{:S(2)}) %collective-permute-start.13) | collective-permute-done | bytes 1048608 | tf_op jit(solution)/shard_map/ppermute | solution.py:1015
  91.2 23.8 %collective-permute-done.17.refs_6_ = bf16[512,1024]{1,0:T(8,128)(2,1)} collective-permute-done((bf16[512,1024]{1,0:T(8,128)(2,1)}, bf16[512,1024]{1,0:T(8,128)(2,1)}, u32[]{:S(2)}, u32[]{:S(2)}) %collective-permute-start.17) | collective-permute-done | bytes 1048608 | tf_op jit(solution)/shard_map/ppermute | solution.py:1015
  121.9 5.8 %fusion.8 = (f32[2048,128]{1,0:T(8,128)}, f32[2048,128]{1,0:T(8,128)}, f32[2048,128]{1,0:T(8,128)}) fusion(f32[128]{0:T(128)S(1)} %fusion.17, f32[2048]{0:T(1024)S(1)} %subtract_convert_fusion, pred[128]{0:T(512)(128)(4,1)S(1)} %get-tuple-element.538, pred[128]{0:T(512)(128)(4,1)S(1)} %get-tuple-element.539, pred[128]{0:T(512)(128)(4,1)S(1)} %broadcast_compare_fusion.1), kind=kLoop, calls=%fused_computation.29 | loop fusion | flops 1310720 | bytes 3154816 | tf_op jit(solution)/shard_map/jit(_where)/select_n | solution.py:1131
  127.7 5.5 maximum_maximum_fusion.1
  133.2 8.6 %collective-permute-done.21.refs_7_ = bf16[512,1024]{1,0:T(8,128)(2,1)S(1)} collective-permute-done((bf16[512,1024]{1,0:T(8,128)(2,1)}, bf16[512,1024]{1,0:T(8,128)(2,1)S(1)}, u32[]{:S(2)}, u32[]{:S(2)}) %collective-permute-start.21) | collective-permute-done | bytes 1048608 | tf_op jit(solution)/shard_map/ppermute | solution.py:1015
  149.3 6.9 %collective-permute-start.25 = (bf16[512,1024]{1,0:T(8,128)(2,1)S(1)}, bf16[512,1024]{1,0:T(8,128)(2,1)}, u32[]{:S(2)}, u32[]{:S(2)}) collective-permute-start(bf16[512,1024]{1,0:T(8,128)(2,1)S(1)} %copy-done.32), channel_id=1, source_target_pairs={{0,8},{1,9},{2,10},{3,11},{4,12},{5,13},{6,14},{7,15},{8,0},{9,1},... | collective-permute-start | bytes 3145736 | tf_op jit(solution)/shard_map/ppermute | solution.py:1015
  158.0 39.8 %shard_map.224 = (bf16[2048,256]{1,0:T(8,128)(2,1)}, bf16[2048,768]{1,0:T(8,128)(2,1)}, bf16[512,1024]{1,0:T(8,128)(2,1)}, bf16[512,1024]{1,0:T(8,128)(2,1)}, bf...) custom-call(s32[5]{0:T(128)} %copy-done.27, ...), custom_call_target="tpu_custom_call" | custom-call | flops 17999998976 | bytes 20971520 | tf_op jit(solution)/shard_map/pallas_call | solution.py:476
  201.3 38.6 %shard_map.225 = (bf16[2048,256]{1,0:T(8,128)(2,1)}, bf16[2048,768]{1,0:T(8,128)(2,1)}, bf16[512,1024]{1,0:T(8,128)(2,1)}, bf16[512,1024]{1,0:T(8,128)(2,1)}, bf...) custom-call(s32[5]{0:T(128)} %copy-done.27, ...), custom_call_target="tpu_custom_call", output_to_operand_aliasing={{0}: (14, {}), {1}: (15, {})} | custom-call | flops 17999998976 | bytes 20971520 | tf_op jit(solution)/shard_map/pallas_call | solution.py:476
  241.2 7.3 %collective-permute-start.32 = (bf16[512,1024]{1,0:T(8,128)(2,1)}, bf16[512,1024]{1,0:T(8,128)(2,1)}, u32[]{:S(2)}, u32[]{:S(2)}) collective-permute-start(bf16[512,1024]{1,0:T(8,128)(2,1)} %get-tuple-element.366), channel_id=1, source_target_pairs={{0,8},{1,9},{2,10},{3,11},{4,12},{5,13},{6,14},{7,15},{24,16},{25,... | collective-permute-start | bytes 3145736 | tf_op jit(solution)/shard_map/ppermute | solution.py:1015
  251.8 8.5 %pad_maximum_fusion.hidden = bf16[2048,2048]{1,0:T(8,128)(2,1)} fusion(bf16[1024,2048]{1,0:T(8,128)(2,1)} %collective-permute-done.27.refs_0_, bf16[1024,2048]{1,0:T(8,128)(2,1)} %get-tuple-element.344.refs_0_), kind=kLoop, calls=%fused_computation | loop fusion | flops 16777216 | bytes 16777216 | tf_op jit(solution)/shard_map/concatenate | solution.py:1180
  260.3 8.5 %pad_maximum_fusion.1.cot = bf16[2048,2048]{1,0:T(8,128)(2,1)} fusion(bf16[1024,2048]{1,0:T(8,128)(2,1)} %collective-permute-done.28.refs_1_, bf16[1024,2048]{1,0:T(8,128)(2,1)} %get-tuple-element.346.refs_1_), kind=kLoop, calls=%fused_computation.1 | loop fusion | flops 16777216 | bytes 16777216 | tf_op jit(solution)/shard_map/concatenate | solution.py:1180
  270.9 6.6 %collective-permute-start.34 = (bf16[512,1024]{1,0:T(8,128)(2,1)S(1)}, bf16[512,1024]{1,0:T(8,128)(2,1)}, u32[]{:S(2)}, u32[]{:S(2)}) collective-permute-start(bf16[512,1024]{1,0:T(8,128)(2,1)S(1)} %copy-done.40), channel_id=1, source_target_pairs={{0,8},{1,9},{2,10},{3,11},{4,12},{5,13},{6,14},{7,15},{24,16},{25,... | collective-permute-start | bytes 3145736 | tf_op jit(solution)/shard_map/ppermute | solution.py:1015
  277.6 32.4 %shard_map.226 = (bf16[2048,1024]{1,0:T(8,128)(2,1)}, bf16[2048,1024]{1,0:T(8,128)(2,1)}, bf16[2048,1024]{1,0:T(8,128)(2,1)}, bf16[256,2048]{1,0:T(8,128)(2,1)},...) custom-call(s32[5]{0:T(128)} %copy-done.27, ...), custom_call_target="tpu_custom_call" | custom-call | flops 17179869184 | bytes 33554432 | tf_op jit(solution)/shard_map/pallas_call | solution.py:260
  311.3 5.6 %collective-permute-start.36 = (bf16[256,2048]{1,0:T(8,128)(2,1)}, bf16[256,2048]{1,0:T(8,128)(2,1)S(1)}, u32[]{:S(2)}, u32[]{:S(2)}) collective-permute-start(bf16[256,2048]{1,0:T(8,128)(2,1)} %get-tuple-element.451), channel_id=1, source_target_pairs={{0,8},{1,9},{2,10},{3,11},{4,12},{5,13},{6,14},{7,15},{24,16},{25,... | collective-permute-start | bytes 3145736 | tf_op jit(solution)/shard_map/ppermute | solution.py:1015
  324.5 10.6 %collective-permute-done.35.refs_5_ = bf16[256,2048]{1,0:T(8,128)(2,1)} collective-permute-done((bf16[256,2048]{1,0:T(8,128)(2,1)}, bf16[256,2048]{1,0:T(8,128)(2,1)}, u32[]{:S(2)}, u32[]{:S(2)}) %collective-permute-start.35) | collective-permute-done | bytes 1048608 | tf_op jit(solution)/shard_map/ppermute | solution.py:1015
  340.6 6.3 %collective-permute-start.38 = (bf16[512,1024]{1,0:T(8,128)(2,1)}, bf16[512,1024]{1,0:T(8,128)(2,1)}, u32[]{:S(2)}, u32[]{:S(2)}) collective-permute-start(bf16[512,1024]{1,0:T(8,128)(2,1)} %add_convert_fusion.6), channel_id=1, source_target_pairs={{0,8},{1,9},{2,10},{3,11},{4,12},{5,13},{6,14},{7,15},{8,0},{9,1},... | collective-permute-start | bytes 3145736 | tf_op jit(solution)/shard_map/ppermute | solution.py:1015
  348.6 27.8 %shard_map.227 = (bf16[2048,1024]{1,0:T(8,128)(2,1)}, f32[1,1024]{1,0:T(1,128)}, bf16[1024,2048]{1,0:T(8,128)(2,1)}, bf16[512,1024]{1,0:T(8,128)(2,1)}, bf16[512...) custom-call(s32[5]{0:T(128)} %copy-done.27, bf16[2048,2048]{1,0:T(8,128)(2,1)} %pad_maximum_fusion.1.cot, ...), custom_call_target="tpu_custom_call" | custom-call | flops 17179869184 | bytes 33554432 | tf_op jit(solution)/shard_map/pallas_call | solution.py:260
  385.1 22.7 %shard_map.228 = (bf16[1024,2048]{1,0:T(8,128)(2,1)}, bf16[1024,2048]{1,0:T(8,128)(2,1)}) custom-call(bf16[2048,768]{1,0:T(8,128)(2,1)} %get-tuple-element.348.a, bf16[2048,768]{1,0:T(8,128)(2,1)} %get-tuple-element.322.refs_2_.aw, bf16[2048,1024]{1,0:T(8,128)(2,1)} %get-tuple-element.393.b, bf16[2048,1024]{1,0:T(8,128)(2,1)} %get-tuple-element.394.bw), custom_call_target="tpu_custom_call" | custom-call | flops 15032385536 | bytes 23068672 | tf_op jit(solution)/shard_map/pallas_call | solution.py:675
  423.6 17.4 %shard_map.231 = (bf16[1024,2048]{1,0:T(8,128)(2,1)}, bf16[1024,2048]{1,0:T(8,128)(2,1)}) custom-call(bf16[2048,256]{1,0:T(8,128)(2,1)} %get-tuple-element.418.a, bf16[256,2048]{1,0:T(8,128)(2,1)} %get-tuple-element.323.refs_3_.aw, bf16[2048,1024]{1,0:T(8,128)(2,1)} %get-tuple-element.419.b, bf16[1024,2048]{1,0:T(8,128)(2,1)} %get-tuple-element.420.bw), custom_call_target="tpu_custom_call" | custom-call | flops 10737418240 | bytes 18874368 | tf_op jit(solution)/shard_map/pallas_call | solution.py:675
  454.7 14.4 %collective-permute-done.47.last = bf16[512,1024]{1,0:T(8,128)(2,1)S(1)} collective-permute-done((bf16[512,1024]{1,0:T(8,128)(2,1)S(1)}, bf16[512,1024]{1,0:T(8,128)(2,1)S(1)}, u32[]{:S(2)}, u32[]{:S(2)}) %collective-permute-start.47) | collective-permute-done | bytes 1048608 | tf_op jit(solution)/shard_map/ppermute | solution.py:1015
  470.5 6.4 %collective-permute-start.52 = (bf16[256,2048]{1,0:T(8,128)(2,1)S(1)}, bf16[256,2048]{1,0:T(8,128)(2,1)S(1)}, u32[]{:S(2)}, u32[]{:S(2)}) collective-permute-start(bf16[256,2048]{1,0:T(8,128)(2,1)S(1)} %copy-done.35), channel_id=1, source_target_pairs={{0,8},{1,9},{2,10},{3,11},{4,12},{5,13},{6,14},{7,15},{24,16},{25,... | collective-permute-start | bytes 3145736 | tf_op jit(solution)/shard_map/ppermute | solution.py:1015
  478.9 9.2 %collective-permute-done.54.by_x = bf16[256,2048]{1,0:T(8,128)(2,1)S(1)} collective-permute-done((bf16[256,2048]{1,0:T(8,128)(2,1)S(1)}, bf16[256,2048]{1,0:T(8,128)(2,1)S(1)}, u32[]{:S(2)}, u32[]{:S(2)}) %collective-permute-start.54) | collective-permute-done | bytes 1048608 | tf_op jit(solution)/shard_map/ppermute | solution.py:1008
  488.7 6.4 %collective-permute-done.55.by_y = bf16[256,2048]{1,0:T(8,128)(2,1)S(1)} collective-permute-done((bf16[256,2048]{1,0:T(8,128)(2,1)S(1)}, bf16[256,2048]{1,0:T(8,128)(2,1)S(1)}, u32[]{:S(2)}, u32[]{:S(2)}) %collective-permute-start.55) | collective-permute-done | bytes 1048608 | tf_op jit(solution)/shard_map/ppermute | solution.py:1008
  (327 shorter events, 214.9 us)
Async XLA Ops:
  28.3 27.4 %collective-permute-start.11 = (bf16[256,2048]{1,0:T(8,128)(2,1)}, bf16[256,2048]{1,0:T(8,128)(2,1)}, u32[]{:S(2)}, u32[]{:S(2)}) collective-permute-start(bf16[256,2048]{1,0:T(8,128)(2,1)} %refs_0_), channel_id=1, source_target_pairs={{0,8},{1,9},{2,10},{3,11},{4,12},{5,13},{6,14},{7,15},{8,0},{9,1},... | collective-permute-start | bytes 3145736 | tf_op jit(solution)/shard_map/ppermute | solution.py:1015
  28.6 27.1 %collective-permute-start.12 = (bf16[256,2048]{1,0:T(8,128)(2,1)}, bf16[256,2048]{1,0:T(8,128)(2,1)}, u32[]{:S(2)}, u32[]{:S(2)}) collective-permute-start(bf16[256,2048]{1,0:T(8,128)(2,1)} %refs_0_), channel_id=1, source_target_pairs={{8,16},{9,17},{10,18},{11,19},{12,20},{13,21},{14,22},{15,23},{16,... | collective-permute-start | bytes 3145736 | tf_op jit(solution)/shard_map/ppermute | solution.py:1015
  55.7 26.8 %collective-permute-start.13 = (bf16[512,1024]{1,0:T(8,128)(2,1)}, bf16[512,1024]{1,0:T(8,128)(2,1)}, u32[]{:S(2)}, u32[]{:S(2)}) collective-permute-start(bf16[512,1024]{1,0:T(8,128)(2,1)} %get-tuple-element.280.refs_2_), channel_id=1, source_target_pairs={{0,8},{1,9},{2,10},{3,11},{4,12},{5,13},{6,14},{7,15},{8,0},{9,1},... | collective-permute-start | bytes 3145736 | tf_op jit(solution)/shard_map/ppermute | solution.py:1015
  86.5 28.6 %collective-permute-start.19 = (bf16[256,2048]{1,0:T(8,128)(2,1)}, bf16[256,2048]{1,0:T(8,128)(2,1)}, u32[]{:S(2)}, u32[]{:S(2)}) collective-permute-start(bf16[256,2048]{1,0:T(8,128)(2,1)} %pad_maximum_fusion.2), channel_id=1, source_target_pairs={{0,1},{1,0},{2,3},{3,2},{4,5},{5,4},{6,7},{7,6},{8,9},{9,8},{10,11... | collective-permute-start | bytes 3145736 | tf_op jit(solution)/shard_map/ppermute | solution.py:1008
  87.1 28.0 %collective-permute-start.20 = (bf16[256,2048]{1,0:T(8,128)(2,1)}, bf16[256,2048]{1,0:T(8,128)(2,1)}, u32[]{:S(2)}, u32[]{:S(2)}) collective-permute-start(bf16[256,2048]{1,0:T(8,128)(2,1)} %pad_maximum_fusion.2), channel_id=1, source_target_pairs={{0,2},{1,3},{2,0},{3,1},{4,6},{5,7},{6,4},{7,5},{8,10},{9,11},{10,... | collective-permute-start | bytes 3145736 | tf_op jit(solution)/shard_map/ppermute | solution.py:1008
  87.7 27.4 %collective-permute-start.17 = (bf16[512,1024]{1,0:T(8,128)(2,1)}, bf16[512,1024]{1,0:T(8,128)(2,1)}, u32[]{:S(2)}, u32[]{:S(2)}) collective-permute-start(bf16[512,1024]{1,0:T(8,128)(2,1)} %collective-permute-done.14.refs_4_), channel_id=1, source_target_pairs={{8,0},{9,1},{10,2},{11,3},{12,4},{13,5},{14,6},{15,7},{16,24},{17,... | collective-permute-start | bytes 3145736 | tf_op jit(solution)/shard_map/ppermute | solution.py:1015
  146.5 51.3 %collective-permute-start.27 = (bf16[1024,2048]{1,0:T(8,128)(2,1)}, bf16[1024,2048]{1,0:T(8,128)(2,1)}, u32[]{:S(2)}, u32[]{:S(2)}) collective-permute-start(bf16[1024,2048]{1,0:T(8,128)(2,1)} %get-tuple-element.344.refs_0_), channel_id=1, source_target_pairs={{0,4},{1,5},{2,6},{3,7},{4,0},{5,1},{6,2},{7,3},{8,12},{9,13},{10,... | collective-permute-start | bytes 12582920 | tf_op jit(solution)/shard_map/ppermute | solution.py:1008
  146.5 51.3 %collective-permute-start.28 = (bf16[1024,2048]{1,0:T(8,128)(2,1)}, bf16[1024,2048]{1,0:T(8,128)(2,1)}, u32[]{:S(2)}, u32[]{:S(2)}) collective-permute-start(bf16[1024,2048]{1,0:T(8,128)(2,1)} %get-tuple-element.346.refs_1_), channel_id=1, source_target_pairs={{0,4},{1,5},{2,6},{3,7},{4,0},{5,1},{6,2},{7,3},{8,12},{9,13},{10,... | collective-permute-start | bytes 12582920 | tf_op jit(solution)/shard_map/ppermute | solution.py:1008
  149.3 48.6 %collective-permute-start.25 = (bf16[512,1024]{1,0:T(8,128)(2,1)S(1)}, bf16[512,1024]{1,0:T(8,128)(2,1)}, u32[]{:S(2)}, u32[]{:S(2)}) collective-permute-start(bf16[512,1024]{1,0:T(8,128)(2,1)S(1)} %copy-done.32), channel_id=1, source_target_pairs={{0,8},{1,9},{2,10},{3,11},{4,12},{5,13},{6,14},{7,15},{8,0},{9,1},... | collective-permute-start | bytes 3145736 | tf_op jit(solution)/shard_map/ppermute | solution.py:1015
  156.1 41.7 %collective-permute-start.26 = (bf16[256,2048]{1,0:T(8,128)(2,1)}, bf16[256,2048]{1,0:T(8,128)(2,1)}, u32[]{:S(2)}, u32[]{:S(2)}) collective-permute-start(bf16[256,2048]{1,0:T(8,128)(2,1)} %collective-permute-done.11.refs_1_), channel_id=1, source_target_pairs={{8,16},{9,17},{10,18},{11,19},{12,20},{13,21},{14,22},{15,23},{16,... | collective-permute-start | bytes 3145736 | tf_op jit(solution)/shard_map/ppermute | solution.py:1015
  197.9 42.0 %collective-permute-start.29 = (bf16[512,1024]{1,0:T(8,128)(2,1)}, bf16[512,1024]{1,0:T(8,128)(2,1)S(1)}, u32[]{:S(2)}, u32[]{:S(2)}) collective-permute-start(bf16[512,1024]{1,0:T(8,128)(2,1)} %copy-done.45), channel_id=1, source_target_pairs={{8,0},{9,1},{10,2},{11,3},{12,4},{13,5},{14,6},{15,7},{16,24},{17,... | collective-permute-start | bytes 3145736 | tf_op jit(solution)/shard_map/ppermute | solution.py:1015
  199.2 40.7 %collective-permute-start.30 = (bf16[512,1024]{1,0:T(8,128)(2,1)}, bf16[512,1024]{1,0:T(8,128)(2,1)}, u32[]{:S(2)}, u32[]{:S(2)}) collective-permute-start(bf16[512,1024]{1,0:T(8,128)(2,1)} %collective-permute-done.25.refs_1_), channel_id=1, source_target_pairs={{8,16},{9,17},{10,18},{11,19},{12,20},{13,21},{14,22},{15,23},{16,... | collective-permute-start | bytes 3145736 | tf_op jit(solution)/shard_map/ppermute | solution.py:1015
  239.9 28.9 %collective-permute-start.31 = (bf16[512,1024]{1,0:T(8,128)(2,1)}, bf16[512,1024]{1,0:T(8,128)(2,1)}, u32[]{:S(2)}, u32[]{:S(2)}) collective-permute-start(bf16[512,1024]{1,0:T(8,128)(2,1)} %collective-permute-done.30.refs_3_), channel_id=1, source_target_pairs={{8,0},{9,1},{10,2},{11,3},{12,4},{13,5},{14,6},{15,7},{16,24},{17,... | collective-permute-start | bytes 3145736 | tf_op jit(solution)/shard_map/ppermute | solution.py:1015
  241.2 28.4 %collective-permute-start.32 = (bf16[512,1024]{1,0:T(8,128)(2,1)}, bf16[512,1024]{1,0:T(8,128)(2,1)}, u32[]{:S(2)}, u32[]{:S(2)}) collective-permute-start(bf16[512,1024]{1,0:T(8,128)(2,1)} %get-tuple-element.366), channel_id=1, source_target_pairs={{0,8},{1,9},{2,10},{3,11},{4,12},{5,13},{6,14},{7,15},{24,16},{25,... | collective-permute-start | bytes 3145736 | tf_op jit(solution)/shard_map/ppermute | solution.py:1015
  269.6 40.3 %collective-permute-start.33 = (bf16[256,2048]{1,0:T(8,128)(2,1)}, bf16[256,2048]{1,0:T(8,128)(2,1)}, u32[]{:S(2)}, u32[]{:S(2)}) collective-permute-start(bf16[256,2048]{1,0:T(8,128)(2,1)} %collective-permute-done.12.refs_2_), channel_id=1, source_target_pairs={{8,0},{9,1},{10,2},{11,3},{12,4},{13,5},{14,6},{15,7},{16,24},{17,... | collective-permute-start | bytes 3145736 | tf_op jit(solution)/shard_map/ppermute | solution.py:1015
  270.9 39.0 %collective-permute-start.34 = (bf16[512,1024]{1,0:T(8,128)(2,1)S(1)}, bf16[512,1024]{1,0:T(8,128)(2,1)}, u32[]{:S(2)}, u32[]{:S(2)}) collective-permute-start(bf16[512,1024]{1,0:T(8,128)(2,1)S(1)} %copy-done.40), channel_id=1, source_target_pairs={{0,8},{1,9},{2,10},{3,11},{4,12},{5,13},{6,14},{7,15},{24,16},{25,... | collective-permute-start | bytes 3145736 | tf_op jit(solution)/shard_map/ppermute | solution.py:1015
  340.6 35.8 %collective-permute-start.38 = (bf16[512,1024]{1,0:T(8,128)(2,1)}, bf16[512,1024]{1,0:T(8,128)(2,1)}, u32[]{:S(2)}, u32[]{:S(2)}) collective-permute-start(bf16[512,1024]{1,0:T(8,128)(2,1)} %add_convert_fusion.6), channel_id=1, source_target_pairs={{0,8},{1,9},{2,10},{3,11},{4,12},{5,13},{6,14},{7,15},{8,0},{9,1},... | collective-permute-start | bytes 3145736 | tf_op jit(solution)/shard_map/ppermute | solution.py:1015
  346.9 29.5 %collective-permute-start.39 = (bf16[512,1024]{1,0:T(8,128)(2,1)}, bf16[512,1024]{1,0:T(8,128)(2,1)}, u32[]{:S(2)}, u32[]{:S(2)}) collective-permute-start(bf16[512,1024]{1,0:T(8,128)(2,1)} %add_convert_fusion.7), channel_id=1, source_target_pairs={{8,16},{9,17},{10,18},{11,19},{12,20},{13,21},{14,22},{15,23},{16,... | collective-permute-start | bytes 3145736 | tf_op jit(solution)/shard_map/ppermute | solution.py:1015
  376.5 33.3 %collective-permute-start.40 = (bf16[512,1024]{1,0:T(8,128)(2,1)}, bf16[512,1024]{1,0:T(8,128)(2,1)}, u32[]{:S(2)}, u32[]{:S(2)}) collective-permute-start(bf16[512,1024]{1,0:T(8,128)(2,1)} %get-tuple-element.412), channel_id=1, source_target_pairs={{0,8},{1,9},{2,10},{3,11},{4,12},{5,13},{6,14},{7,15},{24,16},{25,... | collective-permute-start | bytes 3145736 | tf_op jit(solution)/shard_map/ppermute | solution.py:1015
  410.3 30.7 %collective-permute-start.42 = (bf16[512,1024]{1,0:T(8,128)(2,1)}, bf16[512,1024]{1,0:T(8,128)(2,1)}, u32[]{:S(2)}, u32[]{:S(2)}) collective-permute-start(bf16[512,1024]{1,0:T(8,128)(2,1)} %get-tuple-element.432), channel_id=1, source_target_pairs={{0,8},{1,9},{2,10},{3,11},{4,12},{5,13},{6,14},{7,15},{24,16},{25,... | collective-permute-start | bytes 3145736 | tf_op jit(solution)/shard_map/ppermute | solution.py:1015
  452.7 35.4 %collective-permute-start.54 = (bf16[256,2048]{1,0:T(8,128)(2,1)S(1)}, bf16[256,2048]{1,0:T(8,128)(2,1)S(1)}, u32[]{:S(2)}, u32[]{:S(2)}) collective-permute-start(bf16[256,2048]{1,0:T(8,128)(2,1)S(1)} %get-tuple-element.455), channel_id=1, source_target_pairs={{0,1},{1,0},{2,3},{3,2},{4,5},{5,4},{6,7},{7,6},{8,9},{9,8},{10,11... | collective-permute-start | bytes 3145736 | tf_op jit(solution)/shard_map/ppermute | solution.py:1008
  470.5 32.7 %collective-permute-start.52 = (bf16[256,2048]{1,0:T(8,128)(2,1)S(1)}, bf16[256,2048]{1,0:T(8,128)(2,1)S(1)}, u32[]{:S(2)}, u32[]{:S(2)}) collective-permute-start(bf16[256,2048]{1,0:T(8,128)(2,1)S(1)} %copy-done.35), channel_id=1, source_target_pairs={{0,8},{1,9},{2,10},{3,11},{4,12},{5,13},{6,14},{7,15},{24,16},{25,... | collective-permute-start | bytes 3145736 | tf_op jit(solution)/shard_map/ppermute | solution.py:1015
  504.5 28.9 %collective-permute-start.59 = (bf16[256,2048]{1,0:T(8,128)(2,1)}, bf16[256,2048]{1,0:T(8,128)(2,1)}, u32[]{:S(2)}, u32[]{:S(2)}) collective-permute-start(bf16[256,2048]{1,0:T(8,128)(2,1)} %add_convert_fusion.1), channel_id=1, source_target_pairs={{0,8},{1,9},{2,10},{3,11},{4,12},{5,13},{6,14},{7,15},{8,0},{9,1},... | collective-permute-start | bytes 3145736 | tf_op jit(solution)/shard_map/ppermute | solution.py:1015
  506.4 27.0 %collective-permute-start.60 = (bf16[256,2048]{1,0:T(8,128)(2,1)}, bf16[256,2048]{1,0:T(8,128)(2,1)}, u32[]{:S(2)}, u32[]{:S(2)}) collective-permute-start(bf16[256,2048]{1,0:T(8,128)(2,1)} %add_convert_fusion), channel_id=1, source_target_pairs={{8,16},{9,17},{10,18},{11,19},{12,20},{13,21},{14,22},{15,23},{16,... | collective-permute-start | bytes 3145736 | tf_op jit(solution)/shard_map/ppermute | solution.py:1015
  (97 other events, 1523.9 us)
